TPU v7x, 32 devices: a whole 2x2x4 slice. The times are simulated.
32 devices in a mesh: span: 4 (over y, x), wall: 8 (over z, core).
Axes of the slice: x: 2, y: 2, z: 4, core: 2. Of those that a mesh axis runs over, the one named last changes fastest.
Arguments:
- forcing: bfloat16 [2, 5, 4, 128, 32, 128], P(None, None, None, 'span', 'wall'), may hold values from -6 to 6
- span_factor: float32 [2, 5, 128], replicated, may hold values from -1 to 1
- pivot_inverse: bfloat16 [2, 5, 5, 128, 32, 128], P(None, None, None, 'span', 'wall'), may hold values from -0.1875 to 0.1875
- step_lower: bfloat16 [2, 5, 5, 128, 32, 128], P(None, None, None, 'span', 'wall'), may hold values from -1 to 1
- step_upper: bfloat16 [2, 5, 5, 128, 32, 128], P(None, None, None, 'span', 'wall'), may hold values from -1 to 1
Outputs:
- response: float32 [2, 5, 4, 128, 32, 128], P(None, None, None, 'span', 'wall')
All inputs are finite; a program needn't handle non-finite values.
Results may differ from a plain program's by a relative error of at most 0.0003.
Values may be sent and summed in bfloat16 or wider, within the bound.
No kernel may reach another device: no remote copies, remote signals or barrier semaphores. Data moves between devices by JAX's collectives and lax.ppermute only.
A program may use at most 128 MiB of HBM per device.

v0:
```python
import math

import jax
import jax.numpy as jnp
from jax import lax
from jax.sharding import PartitionSpec as P

exact_mode = lax.Precision.HIGHEST


def entering(x, axis, combine, identity, reverse):
    size, here = (lax.axis_size(axis), lax.axis_index(axis))
    everything = jax.tree.map(lambda part: lax.all_gather(part, axis), x)
    start = jax.tree.map(
        lambda part, zero: jnp.broadcast_to(jnp.asarray(zero, part.dtype), part.shape), x, identity
    )

    def lap(k, before):
        at = size - 1 - k if reverse else k
        reached = at > here if reverse else at < here
        new = combine(before, jax.tree.map(lambda part: part[at], everything))
        return jax.tree.map(lambda a, b: jnp.where(reached, a, b), new, before)

    return lax.fori_loop(0, size, lap, start)


def small_product(matrix, vector):
    left_re = matrix[0][:, :, None]
    left_im = matrix[1][:, :, None]
    right_re = vector[0][None]
    right_im = vector[1][None]
    real = jnp.sum(left_re * right_re - left_im * right_im, axis=1)
    imag = jnp.sum(left_re * right_im + left_im * right_re, axis=1)
    return jnp.stack([real, imag])


def block_vector(matrix, vector):
    return small_product(matrix, vector)


def block_matrix(left, right):
    return small_product(left, right)


def compose_maps(earlier, later):
    return (block_matrix(later[0], earlier[0]), block_vector(later[0], earlier[1]) + later[1])


def span_kernel(span_factor, points):
    count = span_factor.shape[2]
    modes = jnp.arange(count, dtype=jnp.int32)
    scale = 2.0 * math.pi / count
    angle_points = (points[:, None] * modes[None, :] % count).astype(jnp.float32) * scale
    angle_modes = (modes[:, None] * modes[None, :] % count).astype(jnp.float32) * scale
    cos_points = jnp.cos(angle_points)[None]
    sin_points = jnp.sin(angle_points)[None]
    factor_re = span_factor[0][:, None, :]
    factor_im = span_factor[1][:, None, :]
    left_re = factor_re * cos_points - factor_im * sin_points
    left_im = factor_re * sin_points + factor_im * cos_points
    cos_modes = jnp.cos(angle_modes)
    sin_modes = jnp.sin(angle_modes)
    kernel_re = (
        jnp.einsum("crk,kw->crw", left_re, cos_modes, precision=exact_mode)
        + jnp.einsum("crk,kw->crw", left_im, sin_modes, precision=exact_mode)
    ) / count
    kernel_im = (
        jnp.einsum("crk,kw->crw", left_im, cos_modes, precision=exact_mode)
        - jnp.einsum("crk,kw->crw", left_re, sin_modes, precision=exact_mode)
    ) / count
    return (kernel_re, kernel_im)


def apply_kernel(kernel_re, kernel_im, lines):
    real = jnp.einsum("czw,cqwyx->cqzyx", kernel_re, lines[0], precision=exact_mode) - jnp.einsum(
        "czw,cqwyx->cqzyx", kernel_im, lines[1], precision=exact_mode
    )
    imag = jnp.einsum("czw,cqwyx->cqzyx", kernel_re, lines[1], precision=exact_mode) + jnp.einsum(
        "czw,cqwyx->cqzyx", kernel_im, lines[0], precision=exact_mode
    )
    return jnp.stack([real, imag])


def forward_entry(transfer, offset, identity):
    summary = entering(
        (transfer, offset), "wall", compose_maps, (identity, jnp.zeros_like(offset)), False
    )
    return summary[1]


def backward_entry(transfer, offset, identity):
    summary = entering(
        (transfer, offset), "wall", compose_maps, (identity, jnp.zeros_like(offset)), True
    )
    return summary[1]


def row_of(array, height):
    return lax.dynamic_index_in_dim(array, height, 4, False)


def local(forcing, span_factor, pivot_inverse, step_lower, step_upper):
    span_count = forcing.shape[3]
    own_points = lax.axis_index("span") * span_count + jnp.arange(span_count, dtype=jnp.int32)
    kernel_re, kernel_im = span_kernel(span_factor, own_points)
    driving = apply_kernel(
        kernel_re,
        kernel_im,
        lax.all_gather(forcing, "span", axis=3, tiled=True).astype(jnp.float32),
    )
    fields = forcing.shape[1]
    plane = (forcing.shape[3], forcing.shape[5])
    unit = jnp.broadcast_to(
        jnp.eye(fields, dtype=jnp.float32)[:, :, None, None], (fields, fields) + plane
    )
    identity = jnp.stack([unit, jnp.zeros_like(unit)])
    heights = jnp.arange(forcing.shape[4], dtype=jnp.int32)
    vector_zero = jnp.zeros(forcing.shape[:3] + plane, jnp.float32)

    def local_forward(state, height):
        offset, transfer = state
        lower = row_of(step_lower, height).astype(jnp.float32)
        source = block_vector(
            row_of(pivot_inverse, height).astype(jnp.float32), row_of(driving, height)
        )
        return ((source - block_vector(lower, offset), -block_matrix(lower, transfer)), source)

    (offset_low, transfer_low), sources = lax.scan(local_forward, (vector_zero, identity), heights)
    incoming = forward_entry(transfer_low, offset_low, identity)

    def sweep_step(previous, inputs):
        height, source = inputs
        lower = row_of(step_lower, height).astype(jnp.float32)
        current = source - block_vector(lower, previous)
        return (current, current)

    sweeps = lax.scan(sweep_step, incoming, (heights, sources))[1]

    def local_backward(state, inputs):
        offset, transfer = state
        height, sweep = inputs
        upper = row_of(step_upper, height).astype(jnp.float32)
        return ((sweep - block_vector(upper, offset), -block_matrix(upper, transfer)), None)

    (offset_up, transfer_up), unused = lax.scan(
        local_backward, (vector_zero, identity), (heights, sweeps), reverse=True
    )
    arriving = backward_entry(transfer_up, offset_up, identity)

    def answer_step(following, inputs):
        height, sweep = inputs
        upper = row_of(step_upper, height).astype(jnp.float32)
        current = sweep - block_vector(upper, following)
        return (current, current)

    answers = lax.scan(answer_step, arriving, (heights, sweeps), reverse=True)[1]
    return jnp.moveaxis(answers, 0, 4)


def solution(mesh):
    placed = (
        P(None, None, None, "span", "wall", None),
        P(),
        P(None, None, None, "span", "wall", None),
        P(None, None, None, "span", "wall", None),
        P(None, None, None, "span", "wall", None),
    )
    return jax.shard_map(
        local,
        mesh=mesh,
        in_specs=placed,
        out_specs=P(None, None, None, "span", "wall", None),
        check_vma=False,
    )
```

profile of v0, /device:TPU:1, one launch (start us, length us, event | category | flops | bytes accessed | tf_op | source)
XLA Modules:
  0.0 572.3 jit_solution(4140786912850036920)
XLA Ops:
  6.5 2.7 copy.21
  9.5 1.5 copy-done.9
  11.0 1.5 copy.24
  12.9 1.5 copy.22
  16.5 56.3 %all-gather.10.cloned.1.call-done = bf16[2,5,4,128,4,128]{5,3,4,2,1,0:T(8,128)(2,1)} async-done(((bf16[2,5,4,32,4,128]{5,3,4,2,1,0:T(8,128)(2,1)}), bf16[2,5,4,128,4,128]{5,3,4,2,1,0:T(8,128)(2,1)}) %all-gather.10.cloned.1.call-update) | async-done | bytes 5242896 | tf_op jit(solution)/shard_map/all_gather | solution.py:109
  72.8 3.1 fusion.3
  75.9 2.9 fusion.4
  81.2 1.8 pad_maximum_fusion.1
  82.9 1.8 broadcast.91.clone.1
  84.8 31.1 %while.92 = (s32[]{:T(128)}, f32[2,5,4,32,128]{4,3,2,1,0:T(8,128)S(1)}, f32[2,5,5,32,128]{4,3,2,1,0:T(8,128)S(1)}, f32[4,2,5,4,32,128]{5,4,3,2,1,0:T(8,128)}, s3...) while((s32[]{:T(128)}, ...), condition=%wide.region_7.8_spmd.clone, body=%wide.region_0.7_spmd.clone.sunk | while | flops 11755526 | bytes 24249004 | solution.py:128
  117.7 2.9 copy.26
  120.6 52.7 %all-gather.14.cloned.1.call-done = f32[16,5,4,32,128]{4,3,2,1,0:T(8,128)} async-done(((f32[2,5,4,32,128]{4,3,2,1,0:T(8,128)}), f32[16,5,4,32,128]{4,3,2,1,0:T(8,128)}) %all-gather.14.cloned.1.call-update) | async-done | bytes 5242896 | tf_op jit(solution)/shard_map/all_gather | solution.py:13
  173.3 67.4 %all-gather.12.cloned.1.call-done = f32[16,5,5,32,128]{4,3,2,1,0:T(8,128)} async-done(((f32[2,5,5,32,128]{4,3,2,1,0:T(8,128)}), f32[16,5,5,32,128]{4,3,2,1,0:T(8,128)}) %all-gather.12.cloned.1.call-update) | async-done | bytes 6553616 | tf_op jit(solution)/shard_map/all_gather | solution.py:13
  240.7 25.2 %while.93 = (s32[]{:T(128)}, f32[2,5,4,32,128]{4,3,2,1,0:T(8,128)S(1)}, s32[]{:T(128)}, f32[8,2,5,5,32,128]{5,4,3,2,1,0:T(8,128)}, f32[8,2,5,4,32,128]{5,4,3,2,1,0:T(8,128)}, /*index=5*/s32[]{:T(128)}, s32[]{:T(128)}, s32[]{}) while((s32[]{:T(128)}, f32[2,5,4,32,128]{4,3,2,1,0:T(8,128)S(1)}, s32[]{:T(128)}, ...), condition=%wide.region_11.12_spmd.clone, body=%wide.region_8.11_spmd.clone.sunk | while | flops 3932165 | bytes 9011330 | solution.py:24
  265.9 1.9 broadcast.91
  267.8 26.9 %while.90 = (s32[]{:T(128)}, f32[2,5,4,32,128]{4,3,2,1,0:T(8,128)S(1)}, f32[4,2,5,4,32,128]{5,4,3,2,1,0:T(8,128)}, f32[4,2,5,4,32,128]{5,4,3,2,1,0:T(8,128)}, s3...) while((s32[]{:T(128)}, ...), condition=%wide.region_15.16_spmd, body=%wide.region_12.15_spmd.sunk | while | flops 3973125 | bytes 20726448 | solution.py:137
  294.8 25.1 %while.94 = (s32[]{:T(128)}, f32[2,5,4,32,128]{4,3,2,1,0:T(8,128)S(1)}, f32[2,5,5,32,128]{4,3,2,1,0:T(8,128)S(1)}, f32[4,2,5,4,32,128]{5,4,3,2,1,0:T(8,128)}, s3...) while((s32[]{:T(128)}, ...), condition=%wide.region_21.22_spmd.clone, body=%wide.region_16.21_spmd.clone.sunk | while | flops 8110087 | bytes 15319217 | solution.py:145
  321.3 54.2 %all-gather.18.cloned.1.call-done = f32[16,5,4,32,128]{4,3,2,1,0:T(8,128)} async-done(((f32[2,5,4,32,128]{4,3,2,1,0:T(8,128)}), f32[16,5,4,32,128]{4,3,2,1,0:T(8,128)}) %all-gather.18.cloned.1.call-update) | async-done | bytes 5242896 | tf_op jit(solution)/shard_map/all_gather | solution.py:13
  375.6 67.2 %all-gather.16.cloned.1.call-done = f32[16,5,5,32,128]{4,3,2,1,0:T(8,128)} async-done(((f32[2,5,5,32,128]{4,3,2,1,0:T(8,128)}), f32[16,5,5,32,128]{4,3,2,1,0:T(8,128)}) %all-gather.16.cloned.1.call-update) | async-done | bytes 6553616 | tf_op jit(solution)/shard_map/all_gather | solution.py:13
  442.8 25.2 %while.95 = (s32[]{:T(128)}, f32[2,5,4,32,128]{4,3,2,1,0:T(8,128)S(1)}, s32[]{:T(128)}, f32[8,2,5,5,32,128]{5,4,3,2,1,0:T(8,128)}, f32[8,2,5,4,32,128]{5,4,3,2,1...) while((s32[]{:T(128)}, f32[2,5,4,32,128]{4,3,2,1,0:T(8,128)S(1)}, ...), condition=%wide.region_25.26_spmd.clone, body=%wide.region_22.25_spmd.clone.sunk | while | flops 3932169 | bytes 9011392 | solution.py:24
  444.6 1.3 fusion.84
  447.7 1.3 fusion.84
  450.9 1.3 fusion.84
  454.1 1.3 fusion.84
  457.2 1.3 fusion.84
  460.4 1.3 fusion.84
  468.0 2.1 broadcast.91.clone
  470.2 95.5 %while.91 = (s32[]{:T(128)}, f32[2,5,4,32,128]{4,3,2,1,0:T(8,128)S(1)}, f32[4,2,5,4,32,128]{5,0,4,3,2,1:T(4,128)}, f32[4,2,5,4,32,128]{5,4,3,2,1,0:T(8,128)}, s3...) while((s32[]{:T(128)}, ...), condition=%wide.region_29.30_spmd, body=%wide.region_26.29_spmd.sunk | while | flops 3973126 | bytes 11550895 | solution.py:156
  475.8 17.0 %dynamic_update_slice.23 = f32[4,2,5,4,32,128]{5,0,4,3,2,1:T(4,128)} dynamic-update-slice(f32[4,2,5,4,32,128]{5,0,4,3,2,1:T(4,128)} %get-tuple-element.1307, f32[1,2,5,4,32,128]{5,0,4,3,2,1:T(1,128)S(1)} %bitcast.272, s32[]{:T(128)S(6)} %sub.195, s32[]{:T(128)} %constant.243.clone.1..sunk.1, s32[]{:T(128)} %constant.243.clone.1..sunk.1, s32[]{:T(128)} %constant.243.clone.1..sunk.1, ...) | dynamic-update-slice | bytes 1310724 | tf_op jit(solution)/shard_map/while/body/jit(dynamic_update_index_in_dim)/dynamic_update_slice | solution.py:128
  499.7 17.0 %dynamic_update_slice.23 = f32[4,2,5,4,32,128]{5,0,4,3,2,1:T(4,128)} dynamic-update-slice(f32[4,2,5,4,32,128]{5,0,4,3,2,1:T(4,128)} %get-tuple-element.1307, f32[1,2,5,4,32,128]{5,0,4,3,2,1:T(1,128)S(1)} %bitcast.272, s32[]{:T(128)S(6)} %sub.195, s32[]{:T(128)} %constant.243.clone.1..sunk.1, s32[]{:T(128)} %constant.243.clone.1..sunk.1, s32[]{:T(128)} %constant.243.clone.1..sunk.1, ...) | dynamic-update-slice | bytes 1310724 | tf_op jit(solution)/shard_map/while/body/jit(dynamic_update_index_in_dim)/dynamic_update_slice | solution.py:128
  523.6 17.0 %dynamic_update_slice.23 = f32[4,2,5,4,32,128]{5,0,4,3,2,1:T(4,128)} dynamic-update-slice(f32[4,2,5,4,32,128]{5,0,4,3,2,1:T(4,128)} %get-tuple-element.1307, f32[1,2,5,4,32,128]{5,0,4,3,2,1:T(1,128)S(1)} %bitcast.272, s32[]{:T(128)S(6)} %sub.195, s32[]{:T(128)} %constant.243.clone.1..sunk.1, s32[]{:T(128)} %constant.243.clone.1..sunk.1, s32[]{:T(128)} %constant.243.clone.1..sunk.1, ...) | dynamic-update-slice | bytes 1310724 | tf_op jit(solution)/shard_map/while/body/jit(dynamic_update_index_in_dim)/dynamic_update_slice | solution.py:128
  547.5 17.0 %dynamic_update_slice.23 = f32[4,2,5,4,32,128]{5,0,4,3,2,1:T(4,128)} dynamic-update-slice(f32[4,2,5,4,32,128]{5,0,4,3,2,1:T(4,128)} %get-tuple-element.1307, f32[1,2,5,4,32,128]{5,0,4,3,2,1:T(1,128)S(1)} %bitcast.272, s32[]{:T(128)S(6)} %sub.195, s32[]{:T(128)} %constant.243.clone.1..sunk.1, s32[]{:T(128)} %constant.243.clone.1..sunk.1, s32[]{:T(128)} %constant.243.clone.1..sunk.1, ...) | dynamic-update-slice | bytes 1310724 | tf_op jit(solution)/shard_map/while/body/jit(dynamic_update_index_in_dim)/dynamic_update_slice | solution.py:128
  (290 shorter events, 127.9 us)
Async XLA Ops:
  6.5 66.3 %all-gather.10.cloned.1.call-start = ((), (), s32[]{:S(2)}) async-start(), calls=%async_computation | async-start | bytes 6553600 | tf_op jit(solution)/shard_map/all_gather | solution.py:109
  9.2 164.1 %all-gather.14.cloned.1.call-start = ((), (), s32[]{:S(2)}) async-start(), calls=%async_computation.2 | async-start | bytes 5898240 | tf_op jit(solution)/shard_map/all_gather | solution.py:13
  9.3 1.7 copy-start.9
  9.5 66.4 %copy-start = (f32[2,5,5,32,128]{4,3,2,1,0:T(8,128)}, f32[2,5,5,32,128]{4,3,2,1,0:T(8,128)S(1)}, u32[]{:S(2)}) copy-start(f32[2,5,5,32,128]{4,3,2,1,0:T(8,128)S(1)} %stack.192) | copy-start | bytes 2457604
  11.0 1.9 copy-start.10
  12.9 1.5 copy-start.11
  72.8 6.0 %copy-start.8 = (bf16[2,5,4,128,4,128]{5,3,4,2,1,0:T(8,128)(2,1)S(1)}, bf16[2,5,4,128,4,128]{5,3,4,2,1,0:T(8,128)(2,1)}, u32[]{:S(2)}) copy-start(bf16[2,5,4,128,4,128]{5,3,4,2,1,0:T(8,128)(2,1)} %all-gather.10.cloned.1.call-done) | copy-start | bytes 15728644
  82.9 1.8 copy-start.4
  115.8 0.9 copy-start.7
  115.9 1.2 copy-start.3
  116.7 124.0 %all-gather.12.cloned.1.call-start = ((), (), s32[]{:S(2)}) async-start(), calls=%async_computation.1 | async-start | bytes 7372800 | tf_op jit(solution)/shard_map/all_gather | solution.py:13
  117.5 258.1 %all-gather.18.cloned.1.call-start = ((), (), s32[]{:S(2)}) async-start(), calls=%async_computation.4 | async-start | bytes 5898240 | tf_op jit(solution)/shard_map/all_gather | solution.py:13
  267.8 26.9 %copy-start.1 = (f32[2,5,5,32,128]{4,3,2,1,0:T(8,128)S(1)}, f32[2,5,5,32,128]{4,3,2,1,0:T(8,128)}, u32[]{:S(2)}) copy-start(f32[2,5,5,32,128]{4,3,2,1,0:T(8,128)} %copy-done) | copy-start | bytes 2457604
  271.7 1.7 copy-start.5
  278.4 1.7 copy-start.5
  285.2 1.7 copy-start.5
  291.9 1.7 copy-start.5
  319.9 0.8 copy-start.6
  319.9 1.1 copy-start.2
  320.7 122.0 %all-gather.16.cloned.1.call-start = ((), (), s32[]{:S(2)}) async-start(), calls=%async_computation.3 | async-start | bytes 7372800 | tf_op jit(solution)/shard_map/all_gather | solution.py:13
Sparse Core Ops, SparseCore 0:
  9.3 63.4 all-gather.9
  116.9 56.4 all-gather.13
  175.0 65.6 all-gather.11
  320.9 54.6 all-gather.17
  377.0 65.6 all-gather.15
where the time goes:
time: 577 us; the launch traced here: 572 us
  waiting for transfers between devices  299 us (52%)
  local copies, waits for them, and re-layouts  128 us (22%)
  other arithmetic  88 us (15%)
  loops' own time  33.2 us (6%)
  between operations  13.4 us (2%)
  matrix products  10.2 us (2%)
    all_gather x4, waiting for transfers between devices, entering(): everything = jax.tree.map(lambda part: lax.all_gather(part, axis), x)  242 us
    dynamic_update_slice x4, local copies, waits for them, and re-layouts, local(): lax.scan(local_forward, (vector_zero, identity), heights)  68.1 us
    all_gather x1, waiting for transfers between devices, local(): lax.all_gather(forcing, 'span', axis=3, tiled=True).astype(jnp.float32)  56.3 us
    mul x80, local copies, waits for them, and re-layouts, small_product(): real = jnp.sum(left_re * right_re - left_im * right_im, axis=1)  22.2 us
    select_n x16, other arithmetic, lap(): return jax.tree.map(lambda a, b: jnp.where(reached, a, b), new, before)  21.4 us
    reduce_sum x44, other arithmetic, small_product(): real = jnp.sum(left_re * right_re - left_im * right_im, axis=1)  21.3 us
    unnamed x26, local copies, waits for them, and re-layouts  12.6 us
  transfers between devices with their start and end apart: 5, of which 5 were waited for; matrix products, arithmetic and copies ran while one was open for 1% of the time, Pallas kernels for 0%

commit v1 on v0

v1 whole, which is shorter than its diff:
```python
import functools
import math

import jax
import jax.numpy as jnp
from jax import lax
from jax.experimental import pallas as pl
from jax.experimental.pallas import tpu as pltpu
from jax.sharding import PartitionSpec as P

exact_mode = lax.Precision.HIGHEST
VMEM_LIMIT = 44 * 1024 * 1024
CHUNKS = ((0, 1), (2, 3))


def call(kernel, out_shape, scratch=(), flops=0, moved=0, **options):
    return pl.pallas_call(
        kernel,
        out_shape=out_shape,
        scratch_shapes=scratch,
        compiler_params=pltpu.CompilerParams(vmem_limit_bytes=VMEM_LIMIT),
        cost_estimate=pl.CostEstimate(flops=flops, bytes_accessed=moved, transcendentals=0),
        **options,
    )


def smem():
    return pl.BlockSpec(memory_space=pltpu.SMEM)


def vmem():
    return pl.BlockSpec(memory_space=pltpu.VMEM)


def f32(*shape):
    return jax.ShapeDtypeStruct(shape, jnp.float32)


def block_vector(matrix, vector):
    size = len(vector[0])
    real, imag = [], []
    for i in range(size):
        re = im = None
        for j in range(size):
            a, b = matrix(0, i, j), matrix(1, i, j)
            c, d = vector[0][j], vector[1][j]
            term_re, term_im = a * c - b * d, a * d + b * c
            re = term_re if re is None else re + term_re
            im = term_im if im is None else im + term_im
        real.append(re)
        imag.append(im)
    return [real, imag]


def plus(left, right):
    return [[a + b for a, b in zip(x, y)] for x, y in zip(left, right)]


def minus(left, right):
    return [[a - b for a, b in zip(x, y)] for x, y in zip(left, right)]


def negative(vector):
    return [[-a for a in x] for x in vector]


def load_vector(ref, size, *where):
    return [[ref[(r, i) + where] for i in range(size)] for r in range(2)]


def store_vector(ref, vector, *where):
    for r in range(2):
        for i, plane in enumerate(vector[r]):
            ref[(r, i) + where] = plane


def entry(ref, *lead, rows=slice(None)):
    return lambda r, i, j: ref[lead + (r, i, j, rows)].astype(jnp.float32)


def reorder_matrix(points, rows):
    size = points * rows
    to = lax.broadcasted_iota(jnp.int32, (size, size), 0)
    of = lax.broadcasted_iota(jnp.int32, (size, size), 1)
    wanted = (to % points) * rows + to // points
    return jnp.where(of == wanted, 1.0, 0.0).astype(jnp.bfloat16)


def repack_kernel(columns, rows, forcing_ref, *out_refs):
    parts, fields = forcing_ref.shape[:2]
    points = forcing_ref.shape[3] // rows
    order = reorder_matrix(points, rows)
    for place, column in enumerate(columns):
        for r in range(parts):
            for i in range(fields):
                moved = jnp.dot(
                    order, forcing_ref[r, i, place], preferred_element_type=jnp.float32
                ).astype(jnp.bfloat16)
                for y in range(rows):
                    out_refs[place][r, i, y] = moved[y * points : (y + 1) * points]


def prepare_kernel(
    rows,
    here_ref,
    pivot_ref,
    lower_ref,
    upper_ref,
    pivot_out,
    lower_out,
    upper_out,
    keep_ref,
    send_ref,
    held_ref,
):
    size = pivot_ref.shape[1]
    points = pivot_ref.shape[3] // rows
    half = points // 2
    order = reorder_matrix(points, rows)

    def move(index, carry):
        r, i = index // size, index % size
        for source, target in (
            (pivot_ref, pivot_out),
            (lower_ref, lower_out),
            (upper_ref, upper_out),
        ):
            for j in range(size):
                moved = jnp.dot(
                    order, source[r, i, j], preferred_element_type=jnp.float32
                ).astype(target.dtype)
                for y in range(rows):
                    target[y, r, i, j] = moved[y * points : (y + 1) * points]
        return carry

    lax.fori_loop(0, 2 * size, move, 0)

    core = here_ref[0]

    def summarize(index, carry):
        part, j = index // size, index % size
        span = pl.ds(part * half, half)

        def column(ref, y):
            return [
                [-ref[y, r, i, j, span].astype(jnp.float32) for i in range(size)]
                for r in range(2)
            ]

        def store(which, vector):
            @pl.when(part == core)
            def _():
                for r in range(2):
                    for i in range(size):
                        keep_ref[which, r, i, j] = vector[r][i]

            @pl.when(part != core)
            def _():
                for r in range(2):
                    for i in range(size):
                        send_ref[which, r, i, j] = vector[r][i]

        state = column(lower_out, 0)
        store_vector(held_ref.at[0], state)
        for y in range(1, rows):
            state = negative(block_vector(entry(lower_out, y, rows=span), state))
            store_vector(held_ref.at[y], state)
        store(0, state)
        for y in range(rows - 2, -1, -1):
            state = minus(
                load_vector(held_ref.at[y], size),
                block_vector(entry(upper_out, y, rows=span), state),
            )
        store(2, state)
        state = column(upper_out, rows - 1)
        for y in range(rows - 2, -1, -1):
            state = negative(block_vector(entry(upper_out, y, rows=span), state))
        store(1, state)
        return carry

    lax.fori_loop(0, 2 * size, summarize, 0)


def pair_matrices_kernel(here_ref, keep_ref, other_ref, pair_ref, chip_ref, joint_ref):
    core = here_ref[0]
    size = keep_ref.shape[2]
    for which in range(3):
        for r in range(2):
            for i in range(size):
                for j in range(size):
                    pair_ref[core, which, r, i, j] = keep_ref[which, r, i, j]
                    pair_ref[1 - core, which, r, i, j] = other_ref[which, r, i, j]

    def column(j, carry):
        def read(*lead):
            return [[pair_ref[lead + (r, i, j)] for i in range(size)] for r in range(2)]

        def write(ref, vector, *lead):
            for r in range(2):
                for i in range(size):
                    ref[lead + (r, i, j)] = vector[r][i]

        through = read(0, 0)
        write(chip_ref, block_vector(entry(pair_ref, 1, 0), through), 0)
        write(chip_ref, block_vector(entry(pair_ref, 0, 1), read(1, 1)), 1)
        joint = block_vector(entry(pair_ref, 1, 2), through)
        write(joint_ref, joint)
        write(chip_ref, plus(read(0, 2), block_vector(entry(pair_ref, 0, 1), joint)), 2)
        return carry

    lax.fori_loop(0, size, column, 0)


def upper_half_kernel(here_ref, chip_ref, beside_ref, out_ref):
    size = chip_ref.shape[2]

    @pl.when(here_ref[1] == 2)
    def _():
        def column(j, carry):
            state = [[chip_ref[0, r, i, j] for i in range(size)] for r in range(2)]
            state = block_vector(entry(beside_ref), state)
            state = block_vector(entry(chip_ref, 1), state)
            for r in range(2):
                for i in range(size):
                    out_ref[r, i, j] = chip_ref[2, r, i, j] + state[r][i]
            return carry

        lax.fori_loop(0, size, column, 0)

    @pl.when(here_ref[1] != 2)
    def _():
        out_ref[...] = jnp.zeros_like(out_ref)


def local_kernel(
    columns, sources, rows, here_ref, kernel_ref, pivot_ref, lower_ref, upper_ref, *refs
):
    arrived = refs[: columns * sources * 2]
    source_ref, keep_ref, send_ref, driving_ref, sweep_ref = refs[columns * sources * 2 :]
    size = pivot_ref.shape[2]
    points = pivot_ref.shape[4]
    half = points // 2
    for i in range(size):
        for c in range(columns):
            for y in range(0, rows, 2):
                right = jnp.concatenate(
                    [
                        jnp.concatenate(
                            [
                                arrived[(c * sources + m) * 2 + r][i, y + side]
                                for m in range(sources)
                                for r in range(2)
                            ],
                            axis=0,
                        )
                        for side in range(2)
                    ],
                    axis=1,
                )
                both = jnp.dot(kernel_ref[i], right, preferred_element_type=jnp.float32)
                total = both[: 2 * points] + both[2 * points :]
                for side in range(2):
                    lanes = slice(side * 128, (side + 1) * 128)
                    for r in range(2):
                        driving_ref[y + side, c, r, i] = total[
                            r * points : (r + 1) * points, lanes
                        ]
    core = here_ref[0]

    def solve(index, carry):
        part, c = index // columns, index % columns
        span = pl.ds(part * half, half)
        state = None
        for y in range(rows):
            source = block_vector(
                entry(pivot_ref, y, rows=span),
                load_vector(driving_ref.at[y, c], size, span),
            )
            store_vector(source_ref.at[y, c], source, span)
            if state is None:
                state = source
            else:
                state = minus(source, block_vector(entry(lower_ref, y, rows=span), state))
            store_vector(sweep_ref.at[y], state)
        back = state
        for y in range(rows - 2, -1, -1):
            back = minus(
                load_vector(sweep_ref.at[y], size),
                block_vector(entry(upper_ref, y, rows=span), back),
            )
        forth = load_vector(sweep_ref.at[rows - 1], size)

        @pl.when(part == core)
        def _():
            store_vector(keep_ref.at[0, c], forth)
            store_vector(keep_ref.at[1, c], back)

        @pl.when(part != core)
        def _():
            store_vector(send_ref.at[0, c], forth)
            store_vector(send_ref.at[1, c], back)

        return carry

    lax.fori_loop(0, 2 * columns, solve, 0)


def pair_kernel(
    columns, here_ref, pair_ref, keep_ref, other_ref, chip_ref, inner_ref, send_ref, both_ref
):
    core = here_ref[0]
    low = here_ref[1] < here_ref[2]
    size = pair_ref.shape[3]
    both_ref[core] = keep_ref[...]
    both_ref[1 - core] = other_ref[...]

    def column(c, carry):
        first = load_vector(both_ref.at[0, 0, c], size)
        forth = plus(
            load_vector(both_ref.at[1, 0, c], size), block_vector(entry(pair_ref, 1, 0), first)
        )
        entering = plus(
            load_vector(both_ref.at[1, 1, c], size), block_vector(entry(pair_ref, 1, 2), first)
        )
        back = plus(
            load_vector(both_ref.at[0, 1, c], size),
            block_vector(entry(pair_ref, 0, 1), entering),
        )
        store_vector(inner_ref.at[0, c], first)
        store_vector(inner_ref.at[1, c], entering)
        store_vector(chip_ref.at[0, c], forth)
        store_vector(chip_ref.at[1, c], back)

        @pl.when(low)
        def _():
            store_vector(send_ref.at[c], forth)

        @pl.when(jnp.logical_not(low))
        def _():
            store_vector(send_ref.at[c], back)

        return carry

    lax.fori_loop(0, columns, column, 0)


def halves_kernel(
    columns, here_ref, matrices_ref, beside_ref, chip_ref, came_ref, out_ref
):
    size = beside_ref.shape[1]
    chip = here_ref[1]

    @pl.when(chip == 1)
    def _():
        def column(c, carry):
            moved = block_vector(entry(matrices_ref, 0), load_vector(came_ref.at[c], size))
            store_vector(out_ref.at[c], plus(load_vector(chip_ref.at[0, c], size), moved))
            return carry

        lax.fori_loop(0, columns, column, 0)

    @pl.when(chip == 2)
    def _():
        def column(c, carry):
            forth = load_vector(chip_ref.at[0, c], size)
            moved = plus(load_vector(came_ref.at[c], size), block_vector(entry(beside_ref), forth))
            moved = block_vector(entry(matrices_ref, 1), moved)
            store_vector(out_ref.at[c], plus(load_vector(chip_ref.at[1, c], size), moved))
            return carry

        lax.fori_loop(0, columns, column, 0)

    @pl.when((chip == 0) | (chip == 3))
    def _():
        out_ref[...] = jnp.zeros_like(out_ref)


def middle_kernel(
    columns,
    here_ref,
    matrices_ref,
    beside_ref,
    upper_ref,
    chip_ref,
    first_ref,
    mine_ref,
    came_ref,
    edge_ref,
    out_ref,
):
    size = beside_ref.shape[1]
    chip = here_ref[1]

    @pl.when(chip == 1)
    def _():
        def column(c, carry):
            answer = plus(
                load_vector(came_ref.at[c], size),
                block_vector(entry(upper_ref), load_vector(mine_ref.at[c], size)),
            )
            store_vector(edge_ref.at[1, c], answer)
            onward = plus(
                load_vector(chip_ref.at[1, c], size), block_vector(entry(matrices_ref, 1), answer)
            )
            entering = load_vector(first_ref.at[c], size)
            store_vector(edge_ref.at[0, c], entering)
            store_vector(
                out_ref.at[c], plus(onward, block_vector(entry(matrices_ref, 2), entering))
            )
            return carry

        lax.fori_loop(0, columns, column, 0)

    @pl.when(chip == 2)
    def _():
        def column(c, carry):
            entering = load_vector(came_ref.at[c], size)
            store_vector(edge_ref.at[0, c], entering)
            onward = plus(
                load_vector(chip_ref.at[0, c], size),
                block_vector(entry(matrices_ref, 0), entering),
            )
            store_vector(out_ref.at[c], onward)
            store_vector(
                edge_ref.at[1, c],
                plus(
                    load_vector(first_ref.at[c], size), block_vector(entry(beside_ref), onward)
                ),
            )
            return carry

        lax.fori_loop(0, columns, column, 0)

    @pl.when((chip == 0) | (chip == 3))
    def _():
        edge_ref[...] = jnp.zeros_like(edge_ref)
        out_ref[...] = jnp.zeros_like(out_ref)


def split_kernel(
    columns, outer, here_ref, pair_ref, joint_ref, inner_ref, edge_ref, *refs
):
    came_ref = refs[0] if outer else None
    keep_ref, send_ref, entry_ref = refs[-3:]
    core, chip = here_ref[0], here_ref[1]
    size = pair_ref.shape[3]
    entry_ref[...] = edge_ref[...]
    if outer:

        @pl.when(chip == 0)
        def _():
            entry_ref[1] = came_ref[...]

        @pl.when(chip == 3)
        def _():
            entry_ref[0] = came_ref[...]

    def column(c, carry):
        sweep = load_vector(entry_ref.at[0, c], size)
        upper_sweep = plus(
            load_vector(inner_ref.at[0, c], size), block_vector(entry(pair_ref, 0, 0), sweep)
        )
        middle = plus(
            load_vector(inner_ref.at[1, c], size), block_vector(entry(joint_ref), sweep)
        )
        answer = load_vector(entry_ref.at[1, c], size)
        lower_answer = plus(middle, block_vector(entry(pair_ref, 1, 1), answer))

        def put(lower_target, upper_target):
            store_vector(lower_target.at[0, c], sweep)
            store_vector(lower_target.at[1, c], lower_answer)
            store_vector(upper_target.at[0, c], upper_sweep)
            store_vector(upper_target.at[1, c], answer)

        @pl.when(core == 0)
        def _():
            put(keep_ref, send_ref)

        @pl.when(core == 1)
        def _():
            put(send_ref, keep_ref)

        return carry

    lax.fori_loop(0, columns, column, 0)


def answer_kernel(
    columns, rows, here_ref, lower_ref, upper_ref, source_ref, keep_ref, other_ref, *refs
):
    out_ref, sweep_ref = refs[-2:]
    core = here_ref[0]
    size = lower_ref.shape[2]
    points = lower_ref.shape[4]
    half = points // 2

    def run(part, c, edge_ref):
        span = pl.ds(part * half, half)
        state = load_vector(edge_ref.at[0, c], size)
        for y in range(rows):
            state = minus(
                load_vector(source_ref.at[y, c], size, span),
                block_vector(entry(lower_ref, y, rows=span), state),
            )
            store_vector(sweep_ref.at[y], state)
        state = load_vector(edge_ref.at[1, c], size)
        for y in range(rows - 1, -1, -1):
            state = minus(
                load_vector(sweep_ref.at[y], size),
                block_vector(entry(upper_ref, y, rows=span), state),
            )
            place = pl.ds(part * (half * rows) + y, half, stride=rows)
            for r in range(2):
                for i in range(size):
                    out_ref[r, i, c, place] = state[r][i]

    def column(c, carry):
        run(core, c, keep_ref)
        run(1 - core, c, other_ref)
        return carry

    lax.fori_loop(0, columns, column, 0)


def span_kernel(span_factor, points, sources):
    count = span_factor.shape[2]
    modes = jnp.arange(count, dtype=jnp.int32)
    scale = 2.0 * math.pi / count
    angle_points = (points[:, None] * modes[None, :] % count).astype(jnp.float32) * scale
    cos_points = jnp.cos(angle_points)[None]
    sin_points = jnp.sin(angle_points)[None]
    factor_re = span_factor[0][:, None, :]
    factor_im = span_factor[1][:, None, :]
    left_re = factor_re * cos_points - factor_im * sin_points
    left_im = factor_re * sin_points + factor_im * cos_points
    flat = sources.reshape(-1)
    angle_modes = (modes[:, None] * flat[None, :] % count).astype(jnp.float32) * scale
    cos_modes = jnp.cos(angle_modes)
    sin_modes = jnp.sin(angle_modes)

    def product(left, right):
        return jnp.einsum("crk,kw->crw", left, right, precision=exact_mode)

    kernel_re = (product(left_re, cos_modes) + product(left_im, sin_modes)) / count
    kernel_im = (product(left_im, cos_modes) - product(left_re, sin_modes)) / count
    fields, own = kernel_re.shape[:2]
    split = (fields, own) + sources.shape
    kernel_re, kernel_im = kernel_re.reshape(split), kernel_im.reshape(split)
    real = jnp.stack([kernel_re, -kernel_im], axis=3)
    imag = jnp.stack([kernel_im, kernel_re], axis=3)
    whole = jnp.stack([real, imag], axis=1).reshape(fields, 2 * own, -1)
    high = lax.reduce_precision(whole, 8, 7)
    low = whole - high
    return jnp.concatenate([high, low], axis=1).astype(jnp.bfloat16)


def affine(matrix, vector, offset):
    left_re, left_im = matrix[0][None], matrix[1][None]
    right_re, right_im = vector[:, 0, None], vector[:, 1, None]
    real = jnp.sum(left_re * right_re - left_im * right_im, axis=2)
    imag = jnp.sum(left_re * right_im + left_im * right_re, axis=2)
    return offset + jnp.stack([real, imag], axis=1)


def local(forcing, span_factor, pivot_inverse, step_lower, step_upper):
    parts, fields, columns, points, rows, width = forcing.shape
    spans, walls = lax.axis_size("span"), lax.axis_size("wall")
    chips = walls // 2
    half = points // 2
    span_at, wall_at = lax.axis_index("span"), lax.axis_index("wall")
    here = jnp.stack([wall_at % 2, wall_at // 2, jnp.int32(chips // 2)]).astype(jnp.int32)

    flat = (points * rows, width)
    forcing = forcing.reshape(forcing.shape[:3] + flat)
    pivot_inverse = pivot_inverse.reshape(pivot_inverse.shape[:3] + flat)
    step_lower = step_lower.reshape(step_lower.shape[:3] + flat)
    step_upper = step_upper.reshape(step_upper.shape[:3] + flat)

    def swap(array, distance, axis):
        count = spans if axis == "span" else walls
        return lax.ppermute(array, axis, [(i, i ^ distance) for i in range(count)])

    block = jax.ShapeDtypeStruct((fields, rows, points, width), jnp.bfloat16)
    whole_block = jax.ShapeDtypeStruct((parts,) + block.shape, jnp.bfloat16)
    pieces = {}
    for chosen in CHUNKS:
        first = chosen[0]
        out = call(
            functools.partial(repack_kernel, chosen, rows),
            [whole_block] * len(chosen),
            moved=2 * forcing.size * 2 * len(chosen) // columns,
        )(lax.slice_in_dim(forcing, first, first + len(chosen), axis=2))
        for column, array in zip(chosen, out):
            pieces[column] = array
    arrived = {}
    for column in range(columns):
        mine = pieces[column]
        got = {0: mine}
        if spans == 4:
            got[1] = swap(mine, 1, "span")
            got[2] = swap(mine, 2, "span")
            if column % 2 == 0:
                got[3] = swap(got[2], 1, "span")
            else:
                got[3] = swap(got[1], 2, "span")
        else:
            for m in range(1, spans):
                got[m] = swap(mine, m, "span")
        arrived[column] = [got[m][r] for m in range(spans) for r in range(2)]

    own_points = span_at * points + jnp.arange(points, dtype=jnp.int32)
    partners = span_at ^ jnp.arange(spans, dtype=jnp.int32)
    source_points = partners[:, None] * points + jnp.arange(points, dtype=jnp.int32)[None]
    kernel = span_kernel(span_factor, own_points, source_points)

    kept = jnp.bfloat16 if half % 16 == 0 else jnp.float32
    moved_shape = jax.ShapeDtypeStruct((rows, 2, fields, fields, points, width), kept)
    plane = (half, width)
    summary = f32(3, 2, fields, fields, *plane)
    pivots, lowers, uppers, keep, send = call(
        functools.partial(prepare_kernel, rows),
        [moved_shape] * 3 + [summary] * 2,
        scratch=[pltpu.VMEM((rows, 2, fields) + plane, jnp.float32)],
        in_specs=[smem()] + [vmem()] * 3,
        flops=2 * 4500 * 8 * 1024,
        moved=12 * pivot_inverse.size,
    )(here, pivot_inverse, step_lower, step_upper)
    other = swap(send, 1, "wall")
    pair, chip_matrices, joint = call(
        pair_matrices_kernel,
        [
            f32(2, *summary.shape),
            summary,
            f32(2, fields, fields, *plane),
        ],
        in_specs=[smem()] + [vmem()] * 2,
        moved=4 * 6 * keep.size,
    )(here, keep, other)
    tree = chips == 4
    outward = [(i, i ^ 2) for i in range(walls)]
    inward = [(0, 1), (1, 0), (2, 4), (4, 2), (3, 5), (5, 3), (6, 7), (7, 6)]
    if tree:
        beside = lax.ppermute(chip_matrices[2], "wall", outward)
        upper_half = call(
            upper_half_kernel,
            f32(2, fields, fields, *plane),
            in_specs=[smem()] + [vmem()] * 2,
            moved=4 * 5 * keep.size // 3,
        )(here, chip_matrices, beside)
        upper_half = lax.ppermute(upper_half, "wall", inward)

    out = None
    for number, chosen in enumerate(CHUNKS):
        count = len(chosen)
        vectors = f32(2, count, 2, fields, *plane)
        single = f32(count, 2, fields, *plane)
        size = 2 * fields * count * half * width
        taken = [array for column in chosen for array in arrived[column]]
        source, keep, send = call(
            functools.partial(local_kernel, count, spans, rows),
            [f32(rows, count, 2, fields, points, width), vectors, vectors],
            scratch=[
                pltpu.VMEM((rows, count, 2, fields, points, width), jnp.float32),
                pltpu.VMEM((rows, 2, fields) + plane, jnp.float32),
            ],
            in_specs=[smem()] + [vmem()] * (4 + len(taken)),
            flops=2 * 400 * size,
            moved=6 * pivots.size + 4 * 16 * size,
        )(here, kernel, pivots, lowers, uppers, *taken)
        other = swap(send, 1, "wall")
        chip, inner, outgoing = call(
            functools.partial(pair_kernel, count),
            [vectors, vectors, single],
            scratch=[pltpu.VMEM((2,) + vectors.shape, jnp.float32)],
            in_specs=[smem()] + [vmem()] * 3,
            moved=4 * (pair.size + 9 * size),
        )(here, pair, keep, other)
        extra = ()
        if tree:
            came = lax.ppermute(outgoing, "wall", outward)
            mine = call(
                functools.partial(halves_kernel, count),
                single,
                in_specs=[smem()] + [vmem()] * 4,
                moved=4 * (chip_matrices.size + 4 * size),
            )(here, chip_matrices, beside, chip, came)
            across = lax.ppermute(mine, "wall", inward)
            edge, outgoing = call(
                functools.partial(middle_kernel, count),
                [vectors, single],
                in_specs=[smem()] + [vmem()] * 7,
                moved=4 * (chip_matrices.size + 8 * size),
            )(here, chip_matrices, beside, upper_half, chip, came, mine, across)
            extra = (lax.ppermute(outgoing, "wall", outward),)
        else:
            sweep = jnp.zeros(single.shape, jnp.float32)
            answer = jnp.zeros(single.shape, jnp.float32)
            upward = [(i, i + 2) for i in range(walls - 2)]
            downward = [(i + 2, i) for i in range(walls - 2)]
            for _ in range(chips - 1):
                sweep = lax.ppermute(affine(chip_matrices[0], sweep, chip[0]), "wall", upward)
            offset = affine(chip_matrices[2], sweep, chip[1])
            for _ in range(chips - 1):
                answer = lax.ppermute(affine(chip_matrices[1], answer, offset), "wall", downward)
            edge = jnp.stack([sweep, answer])
        keep, send = call(
            functools.partial(split_kernel, count, tree),
            [vectors, vectors],
            scratch=[pltpu.VMEM(vectors.shape, jnp.float32)],
            in_specs=[smem()] + [vmem()] * (4 + len(extra)),
            moved=4 * (pair.size + 9 * size),
        )(here, pair, joint, inner, edge, *extra)
        other = swap(send, 1, "wall")
        held = () if out is None else (out,)
        out = call(
            functools.partial(answer_kernel, count, rows),
            f32(2, fields, columns, *flat),
            scratch=[pltpu.VMEM((rows, 2, fields) + plane, jnp.float32)],
            grid=(1,),
            in_specs=[smem()] + [vmem()] * 5 + [pl.BlockSpec(memory_space=pl.ANY)] * len(held),
            out_specs=pl.BlockSpec(
                (2, fields, count) + flat,
                functools.partial(lambda at, step: (0, 0, at, 0, 0), chosen[0] // count),
            ),
            input_output_aliases={6: 0} if held else {},
            flops=2 * 400 * size,
            moved=4 * pivots.size + 4 * 24 * size,
        )(here, lowers, uppers, source, keep, other, *held)
    return out.reshape(2, fields, columns, points, rows, width)


def solution(mesh):
    placed = (
        P(None, None, None, "span", "wall", None),
        P(),
        P(None, None, None, "span", "wall", None),
        P(None, None, None, "span", "wall", None),
        P(None, None, None, "span", "wall", None),
    )
    return jax.shard_map(
        local,
        mesh=mesh,
        in_specs=placed,
        out_specs=P(None, None, None, "span", "wall", None),
        check_vma=False,
    )
```

time: 577 us -> 115 us (0.20)
  waiting for transfers between devices: 299 us -> 15 us
  local copies, waits for them, and re-layouts: 128 us -> 16 us
  other arithmetic: 88 us -> 0.82 us
  starting transfers between devices: 0.35 us -> 40.3 us
  Pallas kernels: 0 us -> 39.9 us
  loops' own time: 33.2 us -> 0 us
  between operations: 13.4 us -> 0.45 us
  matrix products: 10.2 us -> 1.9 us
    all_gather x5 -> x0, waiting for transfers between devices: 298 us -> none  [the longest x4 242 us: entering(): everything = jax.tree.map(lambda part: lax.all_gather(part, axis), x)]
    dynamic_update_slice x4 -> x0, local copies, waits for them, and re-layouts: 68.1 us -> none  [local(): lax.scan(local_forward, (vector_zero, identity), heights)]
    ppermute x0 -> x25, starting transfers between devices: none -> 40.3 us  [the longest x17 26.2 us: swap(): return lax.ppermute(array, axis, [(i, i ^ distance) for i in range(count)])]
    pallas_call x0 -> x17, Pallas kernels: none -> 39.9 us  [the longest x1 11.8 us: local(): call(functools.partial(prepare_kernel, rows), [moved_shape] * 3 + [summar...]
    another operation x6 -> x0, loops' own time: 33.2 us -> none  [the longest x1 8.49 us: local(): lax.scan(answer_step, arriving, (heights, sweeps), reverse=True)[1]]
    mul x80 -> x0, local copies, waits for them, and re-layouts: 22.2 us -> none  [small_product(): real = jnp.sum(left_re * right_re - left_im * right_im, axis=1)]
    select_n x16 -> x0, other arithmetic: 21.4 us -> none  [lap(): return jax.tree.map(lambda a, b: jnp.where(reached, a, b), new, before)]
    reduce_sum x44 -> x0, other arithmetic: 21.3 us -> none  [small_product(): real = jnp.sum(left_re * right_re - left_im * right_im, axis=1)]
  transfers between devices with their start and end apart: 5 -> 25, of which waited for: 5 -> 6; matrix products, arithmetic and copies ran while one was open for 1% -> 15% of each run, Pallas kernels for 0% -> 30%
where the time goes in v1:
time: 115 us; the launch traced here: 114 us
  starting transfers between devices  40.3 us (35%)
  Pallas kernels  39.9 us (35%)
  local copies, waits for them, and re-layouts  16 us (14%)
  waiting for transfers between devices  15 us (13%)
  matrix products  1.9 us (2%)
    ppermute x17, starting transfers between devices, swap(): return lax.ppermute(array, axis, [(i, i ^ distance) for i in range(count)])  26.2 us
    pallas_call x1, Pallas kernels, local(): call(functools.partial(prepare_kernel, rows), [moved_shape] * 3 + [summar...  11.8 us
    pallas_call x2, Pallas kernels, local(): call(functools.partial(local_kernel, count, spans, rows), [f32(rows, coun...  8.95 us
    squeeze x14, local copies, waits for them, and re-layouts, local(): arrived[column] = [got[m][r] for m in range(spans) for r in range(2)]  8.23 us
    pallas_call x2, Pallas kernels, local(): call(functools.partial(answer_kernel, count, rows), f32(2, fields, column...  8.16 us
    ppermute x17, waiting for transfers between devices, swap(): return lax.ppermute(array, axis, [(i, i ^ distance) for i in range(count)])  7.16 us
    ppermute x2, starting transfers between devices, local(): extra = (lax.ppermute(outgoing, 'wall', outward),)  5.18 us
    ppermute x1, waiting for transfers between devices, local(): beside = lax.ppermute(chip_matrices[2], 'wall', outward)  4.9 us
  transfers between devices with their start and end apart: 25, of which 6 were waited for; matrix products, arithmetic and copies ran while one was open for 15% of the time, Pallas kernels for 30%

profile of v1, /device:TPU:1, one launch (start us, length us, event | category | flops | bytes accessed | tf_op | source)
XLA Modules:
  0.0 114.3 jit_solution(12623925795569139169)
XLA Ops:
  0.0 1.4 %fusion.61 = (bf16[2,5,2,128,128]{4,3,2,1,0:T(8,128)(2,1)S(1)}, bf16[2,5,2,128,128]{4,3,2,1,0:T(8,128)(2,1)S(1)}) fusion(bf16[2,5,4,128,128]{4,3,2,1,0:T(8,128)(2,1)} %bitcast.94), kind=kLoop, calls=%fused_computation.113 | loop fusion | bytes 2621440 | tf_op jit(solution)/shard_map/slice | solution.py:592
  1.4 1.1 shard_map.64
  2.5 2.0 %collective-permute-start.14 = (bf16[2,5,4,32,128]{4,3,2,1,0:T(8,128)(2,1)}, bf16[2,5,4,32,128]{4,3,2,1,0:T(8,128)(2,1)}, u32[]{:S(2)}, u32[]{:S(2)}) collective-permute-start(bf16[2,5,4,32,128]{4,3,2,1,0:T(8,128)(2,1)} %get-tuple-element.57), channel_id=1, source_target_pairs={{0,8},{8,0},{16,24},{24,16},{1,9},{9,1},{17,25},{25,17},{2,10},{10... | collective-permute-start | bytes 983048 | tf_op jit(solution)/shard_map/ppermute | solution.py:581
  4.6 1.2 %collective-permute-start.15 = (bf16[2,5,4,32,128]{4,3,2,1,0:T(8,128)(2,1)}, bf16[2,5,4,32,128]{4,3,2,1,0:T(8,128)(2,1)}, u32[]{:S(2)}, u32[]{:S(2)}) collective-permute-start(bf16[2,5,4,32,128]{4,3,2,1,0:T(8,128)(2,1)} %get-tuple-element.57), channel_id=1, source_target_pairs={{0,16},{8,24},{16,0},{24,8},{1,17},{9,25},{17,1},{25,9},{2,18},{10... | collective-permute-start | bytes 983048 | tf_op jit(solution)/shard_map/ppermute | solution.py:581
  7.1 1.4 %collective-permute-start = (bf16[2,5,4,32,128]{4,3,2,1,0:T(8,128)(2,1)}, bf16[2,5,4,32,128]{4,3,2,1,0:T(8,128)(2,1)}, u32[]{:S(2)}, u32[]{:S(2)}) collective-permute-start(bf16[2,5,4,32,128]{4,3,2,1,0:T(8,128)(2,1)} %get-tuple-element.40), channel_id=1, source_target_pairs={{0,8},{8,0},{16,24},{24,16},{1,9},{9,1},{17,25},{25,17},{2,10},{10... | collective-permute-start | bytes 983048 | tf_op jit(solution)/shard_map/ppermute | solution.py:581
  9.8 2.0 %slice_bitcast_fusion.25 = (bf16[5,4,32,128]{3,2,1,0:T(8,128)(2,1)S(1)}, bf16[5,4,32,128]{3,2,1,0:T(8,128)(2,1)}, bf16[5,4,32,128]{3,2,1,0:T(8,128)(2,1)}, bf16[5,4,32,128]{3,2,1,0:T(8,128)(2,1)}) fusion(bf16[2,5,4,32,128]{4,3,2,1,0:T(8,128)(2,1)} %get-tuple-element.58, bf16[2,5,4,32,128]{4,3,2,1,0:T(8,128)(2,1)} %get-tuple-element.57), kind=kLoop, calls=%fused_computation.36 | loop fusion | bytes 1310720 | tf_op jit(solution)/shard_map/squeeze | solution.py:609
  13.6 2.1 %copy.26 = f32[5,2,32,4,2,32]{5,4,3,2,1,0:T(2,128)} copy(f32[5,2,32,4,2,32]{5,2,4,3,0,1:T(8,128)S(1)} %pad_maximum_fusion) | data formatting | bytes 655360 | tf_op jit(solution)/shard_map/stack | solution.py:551
  15.7 3.7 %reshape.112 = f32[5,64,256]{2,1,0:T(8,128)} reshape(f32[5,2,32,4,2,32]{5,4,3,2,1,0:T(2,128)} %copy.26) | data formatting | bytes 655360 | tf_op jit(solution)/shard_map/reshape | solution.py:551
  20.5 11.8 %shard_map.55 = (bf16[4,2,5,5,32,128]{5,4,3,2,1,0:T(8,128)(2,1)S(1)}, bf16[4,2,5,5,32,128]{5,4,3,2,1,0:T(8,128)(2,1)S(1)}, bf16[4,2,5,5,32,128]{5,4,3,2,1,0:T(8,...) custom-call(s32[3]{0:T(128)S(1)} %pad_add_fusion.here_ref, ...), custom_call_target="tpu_custom_call" | custom-call | flops 73728000 | bytes 9830400 | tf_op jit(solution)/shard_map/pallas_call | solution.py:620
  32.4 1.3 %collective-permute-start.1 = (bf16[2,5,4,32,128]{4,3,2,1,0:T(8,128)(2,1)}, bf16[2,5,4,32,128]{4,3,2,1,0:T(8,128)(2,1)S(1)}, u32[]{:S(2)}, u32[]{:S(2)}) collective-permute-start(bf16[2,5,4,32,128]{4,3,2,1,0:T(8,128)(2,1)} %get-tuple-element.40), channel_id=1, source_target_pairs={{0,16},{8,24},{16,0},{24,8},{1,17},{9,25},{17,1},{25,9},{2,18},{10... | collective-permute-start | bytes 983048 | tf_op jit(solution)/shard_map/ppermute | solution.py:581
  37.2 2.7 %collective-permute-start.6 = (f32[3,2,5,5,16,128]{5,4,3,2,1,0:T(8,128)S(1)}, f32[3,2,5,5,16,128]{5,4,3,2,1,0:T(8,128)S(1)}, u32[]{:S(2)}, u32[]{:S(2)}) collective-permute-start(f32[3,2,5,5,16,128]{5,4,3,2,1,0:T(8,128)S(1)} %get-tuple-element.44), channel_id=1, source_target_pairs={{0,1},{1,0},{2,3},{3,2},{4,5},{5,4},{6,7},{7,6},{8,9},{9,8},{10,11... | collective-permute-start | bytes 3686408 | tf_op jit(solution)/shard_map/ppermute | solution.py:581
  41.0 1.8 %collective-permute-start.16 = (bf16[2,5,4,32,128]{4,3,2,1,0:T(8,128)(2,1)}, bf16[2,5,4,32,128]{4,3,2,1,0:T(8,128)(2,1)S(1)}, u32[]{:S(2)}, u32[]{:S(2)}) collective-permute-start(bf16[2,5,4,32,128]{4,3,2,1,0:T(8,128)(2,1)} %collective-permute-done.15), channel_id=1, source_target_pairs={{0,8},{8,0},{16,24},{24,16},{1,9},{9,1},{17,25},{25,17},{2,10},{10... | collective-permute-start | bytes 983048 | tf_op jit(solution)/shard_map/ppermute | solution.py:581
  43.8 1.3 %collective-permute-start.19 = (bf16[2,5,4,32,128]{4,3,2,1,0:T(8,128)(2,1)}, bf16[2,5,4,32,128]{4,3,2,1,0:T(8,128)(2,1)S(1)}, u32[]{:S(2)}, u32[]{:S(2)}) collective-permute-start(bf16[2,5,4,32,128]{4,3,2,1,0:T(8,128)(2,1)} %collective-permute-done.17), channel_id=1, source_target_pairs={{0,16},{8,24},{16,0},{24,8},{1,17},{9,25},{17,1},{25,9},{2,18},{10... | collective-permute-start | bytes 983048 | tf_op jit(solution)/shard_map/ppermute | solution.py:581
  45.5 1.4 %collective-permute-done.4 = bf16[2,5,4,32,128]{4,3,2,1,0:T(8,128)(2,1)S(1)} collective-permute-done((bf16[2,5,4,32,128]{4,3,2,1,0:T(8,128)(2,1)S(1)}, bf16[2,5,4,32,128]{4,3,2,1,0:T(8,128)(2,1)S(1)}, u32[]{:S(2)}, u32[]{:S(2)}) %collective-permute-start.4) | collective-permute-done | bytes 327712 | tf_op jit(solution)/shard_map/ppermute | solution.py:581
  46.9 1.2 %collective-permute-start.5 = (bf16[2,5,4,32,128]{4,3,2,1,0:T(8,128)(2,1)S(1)}, bf16[2,5,4,32,128]{4,3,2,1,0:T(8,128)(2,1)S(1)}, u32[]{:S(2)}, u32[]{:S(2)}) collective-permute-start(bf16[2,5,4,32,128]{4,3,2,1,0:T(8,128)(2,1)S(1)} %collective-permute-done.3), channel_id=1, source_target_pairs={{0,16},{8,24},{16,0},{24,8},{1,17},{9,25},{17,1},{25,9},{2,18},{10... | collective-permute-start | bytes 983048 | tf_op jit(solution)/shard_map/ppermute | solution.py:581
  48.1 3.1 %collective-permute-done.16 = bf16[2,5,4,32,128]{4,3,2,1,0:T(8,128)(2,1)S(1)} collective-permute-done((bf16[2,5,4,32,128]{4,3,2,1,0:T(8,128)(2,1)}, bf16[2,5,4,32,128]{4,3,2,1,0:T(8,128)(2,1)S(1)}, u32[]{:S(2)}, u32[]{:S(2)}) %collective-permute-start.16) | collective-permute-done | bytes 327712 | tf_op jit(solution)/shard_map/ppermute | solution.py:581
  51.3 2.6 %collective-permute-done.19 = bf16[2,5,4,32,128]{4,3,2,1,0:T(8,128)(2,1)S(1)} collective-permute-done((bf16[2,5,4,32,128]{4,3,2,1,0:T(8,128)(2,1)}, bf16[2,5,4,32,128]{4,3,2,1,0:T(8,128)(2,1)S(1)}, u32[]{:S(2)}, u32[]{:S(2)}) %collective-permute-start.19) | collective-permute-done | bytes 327712 | tf_op jit(solution)/shard_map/ppermute | solution.py:581
  53.9 4.5 %shard_map.65 = (f32[4,2,2,5,32,128]{5,4,3,2,1,0:T(8,128)S(1)}, f32[2,2,2,5,16,128]{5,4,3,2,1,0:T(8,128)S(1)}, f32[2,2,2,5,16,128]{5,4,3,2,1,0:T(8,128)S(1)}) custom-call(s32[3]{0:T(128)S(1)} %pad_add_fusion.here_ref, bf16[5,128,256]{2,1,0:T(8,128)(2,1)S(1)} %pad_maximum_fusion.1.kernel_ref, bf16[4,2,5,5,32,128]{5,4,3,2,1,0:T(8,128)(2,1)S(1)} %get-tuple-element.39.pivot_ref, ...), custom_call_target="tpu_custom_call" | custom-call | flops 32768000 | bytes 7536640 | tf_op jit(solution)/shard_map/pallas_call | solution.py:659
  58.4 5.6 %collective-permute-start.20 = (f32[2,2,2,5,16,128]{5,4,3,2,1,0:T(8,128)S(1)}, f32[2,2,2,5,16,128]{5,4,3,2,1,0:T(8,128)S(1)}, u32[]{:S(2)}, u32[]{:S(2)}) collective-permute-start(f32[2,2,2,5,16,128]{5,4,3,2,1,0:T(8,128)S(1)} %get-tuple-element.61), channel_id=1, source_target_pairs={{0,1},{1,0},{2,3},{3,2},{4,5},{5,4},{6,7},{7,6},{8,9},{9,8},{10,11... | collective-permute-start | bytes 983048 | tf_op jit(solution)/shard_map/ppermute | solution.py:581
  64.1 1.9 %shard_map.58 = (f32[2,3,2,5,5,16,128]{6,5,4,3,2,1,0:T(8,128)S(1)}, f32[3,2,5,5,16,128]{5,4,3,2,1,0:T(8,128)S(1)}, f32[2,5,5,16,128]{4,3,2,1,0:T(8,128)S(1)}) custom-call(s32[3]{0:T(128)S(1)} %pad_add_fusion.here_ref, f32[3,2,5,5,16,128]{5,4,3,2,1,0:T(8,128)S(1)} %get-tuple-element.43.keep_ref, f32[3,2,5,5,16,128]{5,4,3,2,1,0:T(8,128)S(1)} %collective-permute-done.6.other_ref), custom_call_target="tpu_custom_call" | custom-call | bytes 7372800 | tf_op jit(solution)/shard_map/pallas_call | solution.py:629
  66.1 1.4 %collective-permute-start.8 = (f32[2,5,5,16,128]{4,3,2,1,0:T(8,128)S(1)}, f32[2,5,5,16,128]{4,3,2,1,0:T(8,128)S(1)}, u32[]{:S(2)}, u32[]{:S(2)}) collective-permute-start(f32[2,5,5,16,128]{4,3,2,1,0:T(8,128)S(1)} %slice_bitcast_fusion), channel_id=1, source_target_pairs={{0,2},{1,3},{2,0},{3,1},{4,6},{5,7},{6,4},{7,5},{8,10},{9,11},{10,... | collective-permute-start | bytes 1228808 | tf_op jit(solution)/shard_map/ppermute | solution.py:643
  67.5 4.5 %shard_map.57 = (f32[4,2,2,5,32,128]{5,4,3,2,1,0:T(8,128)S(1)}, f32[2,2,2,5,16,128]{5,4,3,2,1,0:T(8,128)S(1)}, f32[2,2,2,5,16,128]{5,4,3,2,1,0:T(8,128)S(1)}) custom-call(s32[3]{0:T(128)S(1)} %pad_add_fusion.here_ref, bf16[5,128,256]{2,1,0:T(8,128)(2,1)S(1)} %pad_maximum_fusion.1.kernel_ref, bf16[4,2,5,5,32,128]{5,4,3,2,1,0:T(8,128)(2,1)S(1)} %get-tuple-element.39.pivot_ref, ...), custom_call_target="tpu_custom_call" | custom-call | flops 32768000 | bytes 7536640 | tf_op jit(solution)/shard_map/pallas_call | solution.py:659
  72.3 4.9 %collective-permute-done.8.beside_ref = f32[2,5,5,16,128]{4,3,2,1,0:T(8,128)S(1)} collective-permute-done((f32[2,5,5,16,128]{4,3,2,1,0:T(8,128)S(1)}, f32[2,5,5,16,128]{4,3,2,1,0:T(8,128)S(1)}, u32[]{:S(2)}, u32[]{:S(2)}) %collective-permute-start.8) | collective-permute-done | bytes 409632 | tf_op jit(solution)/shard_map/ppermute | solution.py:643
  79.9 2.4 %collective-permute-start.21 = (f32[2,2,5,16,128]{4,3,2,1,0:T(8,128)S(1)}, f32[2,2,5,16,128]{4,3,2,1,0:T(8,128)S(1)}, u32[]{:S(2)}, u32[]{:S(2)}) collective-permute-start(f32[2,2,5,16,128]{4,3,2,1,0:T(8,128)S(1)} %get-tuple-element.64), channel_id=1, source_target_pairs={{0,2},{1,3},{2,0},{3,1},{4,6},{5,7},{6,4},{7,5},{8,10},{9,11},{10,... | collective-permute-start | bytes 491528 | tf_op jit(solution)/shard_map/ppermute | solution.py:680
  83.3 2.4 %collective-permute-done.21.came_ref.first_ref = f32[2,2,5,16,128]{4,3,2,1,0:T(8,128)S(1)} collective-permute-done((f32[2,2,5,16,128]{4,3,2,1,0:T(8,128)S(1)}, f32[2,2,5,16,128]{4,3,2,1,0:T(8,128)S(1)}, u32[]{:S(2)}, u32[]{:S(2)}) %collective-permute-start.21) | collective-permute-done | bytes 163872 | tf_op jit(solution)/shard_map/ppermute | solution.py:680
  86.3 2.7 %collective-permute-start.22 = (f32[2,2,5,16,128]{4,3,2,1,0:T(8,128)S(1)}, f32[2,2,5,16,128]{4,3,2,1,0:T(8,128)S(1)}, u32[]{:S(2)}, u32[]{:S(2)}) collective-permute-start(f32[2,2,5,16,128]{4,3,2,1,0:T(8,128)S(1)} %shard_map.67.mine_ref), channel_id=1, source_target_pairs={{0,1},{1,0},{2,4},{4,2},{3,5},{5,3},{6,7},{7,6},{8,9},{9,8},{10,12... | collective-permute-start | bytes 491528 | tf_op jit(solution)/shard_map/ppermute | solution.py:687
  90.1 1.4 %collective-permute-start.11 = (f32[2,2,5,16,128]{4,3,2,1,0:T(8,128)S(1)}, f32[2,2,5,16,128]{4,3,2,1,0:T(8,128)S(1)}, u32[]{:S(2)}, u32[]{:S(2)}) collective-permute-start(f32[2,2,5,16,128]{4,3,2,1,0:T(8,128)S(1)} %shard_map.61.mine_ref), channel_id=1, source_target_pairs={{0,1},{1,0},{2,4},{4,2},{3,5},{5,3},{6,7},{7,6},{8,9},{9,8},{10,12... | collective-permute-start | bytes 491528 | tf_op jit(solution)/shard_map/ppermute | solution.py:687
  92.2 1.6 %collective-permute-start.23 = (f32[2,2,5,16,128]{4,3,2,1,0:T(8,128)S(1)}, f32[2,2,5,16,128]{4,3,2,1,0:T(8,128)S(1)}, u32[]{:S(2)}, u32[]{:S(2)}) collective-permute-start(f32[2,2,5,16,128]{4,3,2,1,0:T(8,128)S(1)} %get-tuple-element.66), channel_id=1, source_target_pairs={{0,2},{1,3},{2,0},{3,1},{4,6},{5,7},{6,4},{7,5},{8,10},{9,11},{10,... | collective-permute-start | bytes 491528 | tf_op jit(solution)/shard_map/ppermute | solution.py:694
  94.3 3.6 %collective-permute-start.12 = (f32[2,2,5,16,128]{4,3,2,1,0:T(8,128)S(1)}, f32[2,2,5,16,128]{4,3,2,1,0:T(8,128)S(1)}, u32[]{:S(2)}, u32[]{:S(2)}) collective-permute-start(f32[2,2,5,16,128]{4,3,2,1,0:T(8,128)S(1)} %get-tuple-element.54), channel_id=1, source_target_pairs={{0,2},{1,3},{2,0},{3,1},{4,6},{5,7},{6,4},{7,5},{8,10},{9,11},{10,... | collective-permute-start | bytes 491528 | tf_op jit(solution)/shard_map/ppermute | solution.py:694
  98.9 5.2 %collective-permute-start.24 = (f32[2,2,2,5,16,128]{5,4,3,2,1,0:T(8,128)S(1)}, f32[2,2,2,5,16,128]{5,4,3,2,1,0:T(8,128)S(1)}, u32[]{:S(2)}, u32[]{:S(2)}) collective-permute-start(f32[2,2,2,5,16,128]{5,4,3,2,1,0:T(8,128)S(1)} %get-tuple-element.68), channel_id=1, source_target_pairs={{0,1},{1,0},{2,3},{3,2},{4,5},{5,4},{6,7},{7,6},{8,9},{9,8},{10,11... | collective-permute-start | bytes 983048 | tf_op jit(solution)/shard_map/ppermute | solution.py:581
  106.1 4.1 %shard_map.70.refs_0_ = f32[2,5,4,128,128]{4,3,2,1,0:T(8,128)} custom-call(s32[3]{0:T(128)S(1)} %pad_add_fusion.here_ref, bf16[4,2,5,5,32,128]{5,4,3,2,1,0:T(8,128)(2,1)S(1)} %get-tuple-element.37.lower_ref, bf16[4,2,5,5,32,128]{5,4,3,2,1,0:T(8,128)(2,1)S(1)} %get-tuple-element.38.upper_ref, f32[4,2,2,5,32,128]{5,4,3,2,1,0:T(8,128)S(1)} %get-tuple-element.59.source_ref, ...), custom_call_target="tpu_custom_call" | custom-call | flops 32768000 | bytes 7208960 | tf_op jit(solution)/shard_map/pallas_call | solution.py:715
  110.2 4.1 %shard_map.71 = f32[2,5,4,128,128]{4,3,2,1,0:T(8,128)} custom-call(s32[3]{0:T(128)S(1)} %pad_add_fusion.here_ref, bf16[4,2,5,5,32,128]{5,4,3,2,1,0:T(8,128)(2,1)S(1)} %get-tuple-element.37.lower_ref, bf16[4,2,5,5,32,128]{5,4,3,2,1,0:T(8,128)(2,1)S(1)} %get-tuple-element.38.upper_ref, ...), custom_call_target="tpu_custom_call", output_to_operand_aliasing={{}: (6, {})} | custom-call | flops 32768000 | bytes 7208960 | tf_op jit(solution)/shard_map/pallas_call | solution.py:715
  (89 shorter events, 21.4 us)
Async XLA Ops:
  1.4 7.2 %copy-start.7 = (f32[2,5,128]{2,0,1:T(2,128)S(1)}, f32[2,5,128]{2,0,1:T(2,128)}, u32[]{:S(2)}) copy-start(f32[2,5,128]{2,0,1:T(2,128)} %param.6) | copy-start | bytes 15364
  2.5 29.9 %collective-permute-start.14 = (bf16[2,5,4,32,128]{4,3,2,1,0:T(8,128)(2,1)}, bf16[2,5,4,32,128]{4,3,2,1,0:T(8,128)(2,1)}, u32[]{:S(2)}, u32[]{:S(2)}) collective-permute-start(bf16[2,5,4,32,128]{4,3,2,1,0:T(8,128)(2,1)} %get-tuple-element.57), channel_id=1, source_target_pairs={{0,8},{8,0},{16,24},{24,16},{1,9},{9,1},{17,25},{25,17},{2,10},{10... | collective-permute-start | bytes 983048 | tf_op jit(solution)/shard_map/ppermute | solution.py:581
  4.6 30.2 %collective-permute-start.15 = (bf16[2,5,4,32,128]{4,3,2,1,0:T(8,128)(2,1)}, bf16[2,5,4,32,128]{4,3,2,1,0:T(8,128)(2,1)}, u32[]{:S(2)}, u32[]{:S(2)}) collective-permute-start(bf16[2,5,4,32,128]{4,3,2,1,0:T(8,128)(2,1)} %get-tuple-element.57), channel_id=1, source_target_pairs={{0,16},{8,24},{16,0},{24,8},{1,17},{9,25},{17,1},{25,9},{2,18},{10... | collective-permute-start | bytes 983048 | tf_op jit(solution)/shard_map/ppermute | solution.py:581
  5.8 30.3 %collective-permute-start.17 = (bf16[2,5,4,32,128]{4,3,2,1,0:T(8,128)(2,1)}, bf16[2,5,4,32,128]{4,3,2,1,0:T(8,128)(2,1)}, u32[]{:S(2)}, u32[]{:S(2)}) collective-permute-start(bf16[2,5,4,32,128]{4,3,2,1,0:T(8,128)(2,1)} %get-tuple-element.58), channel_id=1, source_target_pairs={{0,8},{8,0},{16,24},{24,16},{1,9},{9,1},{17,25},{25,17},{2,10},{10... | collective-permute-start | bytes 983048 | tf_op jit(solution)/shard_map/ppermute | solution.py:581
  6.1 31.1 %collective-permute-start.18 = (bf16[2,5,4,32,128]{4,3,2,1,0:T(8,128)(2,1)}, bf16[2,5,4,32,128]{4,3,2,1,0:T(8,128)(2,1)}, u32[]{:S(2)}, u32[]{:S(2)}) collective-permute-start(bf16[2,5,4,32,128]{4,3,2,1,0:T(8,128)(2,1)} %get-tuple-element.58), channel_id=1, source_target_pairs={{0,16},{8,24},{16,0},{24,8},{1,17},{9,25},{17,1},{25,9},{2,18},{10... | collective-permute-start | bytes 983048 | tf_op jit(solution)/shard_map/ppermute | solution.py:581
  7.1 12.3 %copy-start.4 = (bf16[2,5,4,32,128]{4,3,2,1,0:T(8,128)(2,1)}, bf16[2,5,4,32,128]{4,3,2,1,0:T(8,128)(2,1)S(1)}, u32[]{:S(2)}) copy-start(bf16[2,5,4,32,128]{4,3,2,1,0:T(8,128)(2,1)S(1)} %get-tuple-element.41) | copy-start | bytes 983044
  7.1 33.9 %collective-permute-start = (bf16[2,5,4,32,128]{4,3,2,1,0:T(8,128)(2,1)}, bf16[2,5,4,32,128]{4,3,2,1,0:T(8,128)(2,1)}, u32[]{:S(2)}, u32[]{:S(2)}) collective-permute-start(bf16[2,5,4,32,128]{4,3,2,1,0:T(8,128)(2,1)} %get-tuple-element.40), channel_id=1, source_target_pairs={{0,8},{8,0},{16,24},{24,16},{1,9},{9,1},{17,25},{25,17},{2,10},{10... | collective-permute-start | bytes 983048 | tf_op jit(solution)/shard_map/ppermute | solution.py:581
  15.7 4.8 %copy-start = (bf16[2,5,5,32,4,128]{5,4,3,2,1,0:T(4,128)(2,1)S(1)}, bf16[2,5,5,32,4,128]{5,4,3,2,1,0:T(4,128)(2,1)}, u32[]{:S(2)}) copy-start(bf16[2,5,5,32,4,128]{5,4,3,2,1,0:T(4,128)(2,1)} %param.7) | copy-start | bytes 4915204
  20.5 11.8 %copy-start.6 = (f32[5,64,256]{2,1,0:T(8,128)S(1)}, f32[5,64,256]{2,1,0:T(8,128)}, u32[]{:S(2)}) copy-start(f32[5,64,256]{2,1,0:T(8,128)} %reshape.112) | copy-start | bytes 983044
  32.4 11.3 %collective-permute-start.1 = (bf16[2,5,4,32,128]{4,3,2,1,0:T(8,128)(2,1)}, bf16[2,5,4,32,128]{4,3,2,1,0:T(8,128)(2,1)S(1)}, u32[]{:S(2)}, u32[]{:S(2)}) collective-permute-start(bf16[2,5,4,32,128]{4,3,2,1,0:T(8,128)(2,1)} %get-tuple-element.40), channel_id=1, source_target_pairs={{0,16},{8,24},{16,0},{24,8},{1,17},{9,25},{17,1},{25,9},{2,18},{10... | collective-permute-start | bytes 983048 | tf_op jit(solution)/shard_map/ppermute | solution.py:581
  34.8 10.3 %collective-permute-start.3 = (bf16[2,5,4,32,128]{4,3,2,1,0:T(8,128)(2,1)S(1)}, bf16[2,5,4,32,128]{4,3,2,1,0:T(8,128)(2,1)S(1)}, u32[]{:S(2)}, u32[]{:S(2)}) collective-permute-start(bf16[2,5,4,32,128]{4,3,2,1,0:T(8,128)(2,1)S(1)} %copy-done.5), channel_id=1, source_target_pairs={{0,8},{8,0},{16,24},{24,16},{1,9},{9,1},{17,25},{25,17},{2,10},{10... | collective-permute-start | bytes 983048 | tf_op jit(solution)/shard_map/ppermute | solution.py:581
  36.1 10.7 %collective-permute-start.4 = (bf16[2,5,4,32,128]{4,3,2,1,0:T(8,128)(2,1)S(1)}, bf16[2,5,4,32,128]{4,3,2,1,0:T(8,128)(2,1)S(1)}, u32[]{:S(2)}, u32[]{:S(2)}) collective-permute-start(bf16[2,5,4,32,128]{4,3,2,1,0:T(8,128)(2,1)S(1)} %copy-done.5), channel_id=1, source_target_pairs={{0,16},{8,24},{16,0},{24,8},{1,17},{9,25},{17,1},{25,9},{2,18},{10... | collective-permute-start | bytes 983048 | tf_op jit(solution)/shard_map/ppermute | solution.py:581
  37.2 26.9 %collective-permute-start.6 = (f32[3,2,5,5,16,128]{5,4,3,2,1,0:T(8,128)S(1)}, f32[3,2,5,5,16,128]{5,4,3,2,1,0:T(8,128)S(1)}, u32[]{:S(2)}, u32[]{:S(2)}) collective-permute-start(f32[3,2,5,5,16,128]{5,4,3,2,1,0:T(8,128)S(1)} %get-tuple-element.44), channel_id=1, source_target_pairs={{0,1},{1,0},{2,3},{3,2},{4,5},{5,4},{6,7},{7,6},{8,9},{9,8},{10,11... | collective-permute-start | bytes 3686408 | tf_op jit(solution)/shard_map/ppermute | solution.py:581
  41.0 10.3 %collective-permute-start.16 = (bf16[2,5,4,32,128]{4,3,2,1,0:T(8,128)(2,1)}, bf16[2,5,4,32,128]{4,3,2,1,0:T(8,128)(2,1)S(1)}, u32[]{:S(2)}, u32[]{:S(2)}) collective-permute-start(bf16[2,5,4,32,128]{4,3,2,1,0:T(8,128)(2,1)} %collective-permute-done.15), channel_id=1, source_target_pairs={{0,8},{8,0},{16,24},{24,16},{1,9},{9,1},{17,25},{25,17},{2,10},{10... | collective-permute-start | bytes 983048 | tf_op jit(solution)/shard_map/ppermute | solution.py:581
  43.8 10.1 %collective-permute-start.19 = (bf16[2,5,4,32,128]{4,3,2,1,0:T(8,128)(2,1)}, bf16[2,5,4,32,128]{4,3,2,1,0:T(8,128)(2,1)S(1)}, u32[]{:S(2)}, u32[]{:S(2)}) collective-permute-start(bf16[2,5,4,32,128]{4,3,2,1,0:T(8,128)(2,1)} %collective-permute-done.17), channel_id=1, source_target_pairs={{0,16},{8,24},{16,0},{24,8},{1,17},{9,25},{17,1},{25,9},{2,18},{10... | collective-permute-start | bytes 983048 | tf_op jit(solution)/shard_map/ppermute | solution.py:581
  45.1 8.8 %copy-start.1 = (bf16[5,4,32,128]{3,2,1,0:T(8,128)(2,1)S(1)}, bf16[5,4,32,128]{3,2,1,0:T(8,128)(2,1)}, u32[]{:S(2)}) copy-start(bf16[5,4,32,128]{3,2,1,0:T(8,128)(2,1)} %get-tuple-element.78.refs_8_) | copy-start | bytes 491524
  45.1 8.8 %copy-start.2 = (bf16[5,4,32,128]{3,2,1,0:T(8,128)(2,1)S(1)}, bf16[5,4,32,128]{3,2,1,0:T(8,128)(2,1)}, u32[]{:S(2)}) copy-start(bf16[5,4,32,128]{3,2,1,0:T(8,128)(2,1)} %get-tuple-element.117.refs_0_) | copy-start | bytes 491524
  45.1 8.8 %copy-start.3 = (bf16[5,4,32,128]{3,2,1,0:T(8,128)(2,1)S(1)}, bf16[5,4,32,128]{3,2,1,0:T(8,128)(2,1)}, u32[]{:S(2)}) copy-start(bf16[5,4,32,128]{3,2,1,0:T(8,128)(2,1)} %get-tuple-element.118.refs_1_) | copy-start | bytes 491524
  45.1 18.9 %collective-permute-start.2 = (bf16[2,5,4,32,128]{4,3,2,1,0:T(8,128)(2,1)S(1)}, bf16[2,5,4,32,128]{4,3,2,1,0:T(8,128)(2,1)S(1)}, u32[]{:S(2)}, u32[]{:S(2)}) collective-permute-start(bf16[2,5,4,32,128]{4,3,2,1,0:T(8,128)(2,1)S(1)} %collective-permute-done.1), channel_id=1, source_target_pairs={{0,8},{8,0},{16,24},{24,16},{1,9},{9,1},{17,25},{25,17},{2,10},{10... | collective-permute-start | bytes 983048 | tf_op jit(solution)/shard_map/ppermute | solution.py:581
  46.9 20.6 %collective-permute-start.5 = (bf16[2,5,4,32,128]{4,3,2,1,0:T(8,128)(2,1)S(1)}, bf16[2,5,4,32,128]{4,3,2,1,0:T(8,128)(2,1)S(1)}, u32[]{:S(2)}, u32[]{:S(2)}) collective-permute-start(bf16[2,5,4,32,128]{4,3,2,1,0:T(8,128)(2,1)S(1)} %collective-permute-done.3), channel_id=1, source_target_pairs={{0,16},{8,24},{16,0},{24,8},{1,17},{9,25},{17,1},{25,9},{2,18},{10... | collective-permute-start | bytes 983048 | tf_op jit(solution)/shard_map/ppermute | solution.py:581
  58.4 20.4 %collective-permute-start.20 = (f32[2,2,2,5,16,128]{5,4,3,2,1,0:T(8,128)S(1)}, f32[2,2,2,5,16,128]{5,4,3,2,1,0:T(8,128)S(1)}, u32[]{:S(2)}, u32[]{:S(2)}) collective-permute-start(f32[2,2,2,5,16,128]{5,4,3,2,1,0:T(8,128)S(1)} %get-tuple-element.61), channel_id=1, source_target_pairs={{0,1},{1,0},{2,3},{3,2},{4,5},{5,4},{6,7},{7,6},{8,9},{9,8},{10,11... | collective-permute-start | bytes 983048 | tf_op jit(solution)/shard_map/ppermute | solution.py:581
  66.1 11.1 %collective-permute-start.8 = (f32[2,5,5,16,128]{4,3,2,1,0:T(8,128)S(1)}, f32[2,5,5,16,128]{4,3,2,1,0:T(8,128)S(1)}, u32[]{:S(2)}, u32[]{:S(2)}) collective-permute-start(f32[2,5,5,16,128]{4,3,2,1,0:T(8,128)S(1)} %slice_bitcast_fusion), channel_id=1, source_target_pairs={{0,2},{1,3},{2,0},{3,1},{4,6},{5,7},{6,4},{7,5},{8,10},{9,11},{10,... | collective-permute-start | bytes 1228808 | tf_op jit(solution)/shard_map/ppermute | solution.py:643
  72.0 10.3 %collective-permute-start.7 = (f32[2,2,2,5,16,128]{5,4,3,2,1,0:T(8,128)S(1)}, f32[2,2,2,5,16,128]{5,4,3,2,1,0:T(8,128)S(1)}, u32[]{:S(2)}, u32[]{:S(2)}) collective-permute-start(f32[2,2,2,5,16,128]{5,4,3,2,1,0:T(8,128)S(1)} %get-tuple-element.48), channel_id=1, source_target_pairs={{0,1},{1,0},{2,3},{3,2},{4,5},{5,4},{6,7},{7,6},{8,9},{9,8},{10,11... | collective-permute-start | bytes 983048 | tf_op jit(solution)/shard_map/ppermute | solution.py:581
  78.0 13.6 %collective-permute-start.9 = (f32[2,5,5,16,128]{4,3,2,1,0:T(8,128)S(1)}, f32[2,5,5,16,128]{4,3,2,1,0:T(8,128)S(1)}, u32[]{:S(2)}, u32[]{:S(2)}) collective-permute-start(f32[2,5,5,16,128]{4,3,2,1,0:T(8,128)S(1)} %shard_map.60), channel_id=1, source_target_pairs={{0,1},{1,0},{2,4},{4,2},{3,5},{5,3},{6,7},{7,6},{8,9},{9,8},{10,12... | collective-permute-start | bytes 1228808 | tf_op jit(solution)/shard_map/ppermute | solution.py:650
  79.9 5.9 %collective-permute-start.21 = (f32[2,2,5,16,128]{4,3,2,1,0:T(8,128)S(1)}, f32[2,2,5,16,128]{4,3,2,1,0:T(8,128)S(1)}, u32[]{:S(2)}, u32[]{:S(2)}) collective-permute-start(f32[2,2,5,16,128]{4,3,2,1,0:T(8,128)S(1)} %get-tuple-element.64), channel_id=1, source_target_pairs={{0,2},{1,3},{2,0},{3,1},{4,6},{5,7},{6,4},{7,5},{8,10},{9,11},{10,... | collective-permute-start | bytes 491528 | tf_op jit(solution)/shard_map/ppermute | solution.py:680
  83.3 6.3 %collective-permute-start.10 = (f32[2,2,5,16,128]{4,3,2,1,0:T(8,128)S(1)}, f32[2,2,5,16,128]{4,3,2,1,0:T(8,128)S(1)}, u32[]{:S(2)}, u32[]{:S(2)}) collective-permute-start(f32[2,2,5,16,128]{4,3,2,1,0:T(8,128)S(1)} %get-tuple-element.52), channel_id=1, source_target_pairs={{0,2},{1,3},{2,0},{3,1},{4,6},{5,7},{6,4},{7,5},{8,10},{9,11},{10,... | collective-permute-start | bytes 491528 | tf_op jit(solution)/shard_map/ppermute | solution.py:680
  86.3 5.3 %collective-permute-start.22 = (f32[2,2,5,16,128]{4,3,2,1,0:T(8,128)S(1)}, f32[2,2,5,16,128]{4,3,2,1,0:T(8,128)S(1)}, u32[]{:S(2)}, u32[]{:S(2)}) collective-permute-start(f32[2,2,5,16,128]{4,3,2,1,0:T(8,128)S(1)} %shard_map.67.mine_ref), channel_id=1, source_target_pairs={{0,1},{1,0},{2,4},{4,2},{3,5},{5,3},{6,7},{7,6},{8,9},{9,8},{10,12... | collective-permute-start | bytes 491528 | tf_op jit(solution)/shard_map/ppermute | solution.py:687
  90.1 3.6 %collective-permute-start.11 = (f32[2,2,5,16,128]{4,3,2,1,0:T(8,128)S(1)}, f32[2,2,5,16,128]{4,3,2,1,0:T(8,128)S(1)}, u32[]{:S(2)}, u32[]{:S(2)}) collective-permute-start(f32[2,2,5,16,128]{4,3,2,1,0:T(8,128)S(1)} %shard_map.61.mine_ref), channel_id=1, source_target_pairs={{0,1},{1,0},{2,4},{4,2},{3,5},{5,3},{6,7},{7,6},{8,9},{9,8},{10,12... | collective-permute-start | bytes 491528 | tf_op jit(solution)/shard_map/ppermute | solution.py:687
  92.2 5.8 %collective-permute-start.23 = (f32[2,2,5,16,128]{4,3,2,1,0:T(8,128)S(1)}, f32[2,2,5,16,128]{4,3,2,1,0:T(8,128)S(1)}, u32[]{:S(2)}, u32[]{:S(2)}) collective-permute-start(f32[2,2,5,16,128]{4,3,2,1,0:T(8,128)S(1)} %get-tuple-element.66), channel_id=1, source_target_pairs={{0,2},{1,3},{2,0},{3,1},{4,6},{5,7},{6,4},{7,5},{8,10},{9,11},{10,... | collective-permute-start | bytes 491528 | tf_op jit(solution)/shard_map/ppermute | solution.py:694
  94.3 9.8 %collective-permute-start.12 = (f32[2,2,5,16,128]{4,3,2,1,0:T(8,128)S(1)}, f32[2,2,5,16,128]{4,3,2,1,0:T(8,128)S(1)}, u32[]{:S(2)}, u32[]{:S(2)}) collective-permute-start(f32[2,2,5,16,128]{4,3,2,1,0:T(8,128)S(1)} %get-tuple-element.54), channel_id=1, source_target_pairs={{0,2},{1,3},{2,0},{3,1},{4,6},{5,7},{6,4},{7,5},{8,10},{9,11},{10,... | collective-permute-start | bytes 491528 | tf_op jit(solution)/shard_map/ppermute | solution.py:694
  98.9 7.2 %collective-permute-start.24 = (f32[2,2,2,5,16,128]{5,4,3,2,1,0:T(8,128)S(1)}, f32[2,2,2,5,16,128]{5,4,3,2,1,0:T(8,128)S(1)}, u32[]{:S(2)}, u32[]{:S(2)}) collective-permute-start(f32[2,2,2,5,16,128]{5,4,3,2,1,0:T(8,128)S(1)} %get-tuple-element.68), channel_id=1, source_target_pairs={{0,1},{1,0},{2,3},{3,2},{4,5},{5,4},{6,7},{7,6},{8,9},{9,8},{10,11... | collective-permute-start | bytes 983048 | tf_op jit(solution)/shard_map/ppermute | solution.py:581
  105.1 5.1 %collective-permute-start.13 = (f32[2,2,2,5,16,128]{5,4,3,2,1,0:T(8,128)S(1)}, f32[2,2,2,5,16,128]{5,4,3,2,1,0:T(8,128)S(1)}, u32[]{:S(2)}, u32[]{:S(2)}) collective-permute-start(f32[2,2,2,5,16,128]{5,4,3,2,1,0:T(8,128)S(1)} %get-tuple-element.56), channel_id=1, source_target_pairs={{0,1},{1,0},{2,3},{3,2},{4,5},{5,4},{6,7},{7,6},{8,9},{9,8},{10,11... | collective-permute-start | bytes 983048 | tf_op jit(solution)/shard_map/ppermute | solution.py:581
  (1 other events, 2.4 us)

commit v2 on v1

v2 whole, which is shorter than its diff:
```python
import functools
import math

import jax
import jax.numpy as jnp
from jax import lax
from jax.experimental import pallas as pl
from jax.experimental.pallas import tpu as pltpu
from jax.sharding import PartitionSpec as P

exact_mode = lax.Precision.HIGHEST
VMEM_LIMIT = 44 * 1024 * 1024
BYTES_PER_MICRO = 10_000
CHUNKS = ((0, 1), (2, 3))


def call(kernel, out_shape, scratch=(), micros=1.0, limit=VMEM_LIMIT, **options):
    plain = kernel.func if isinstance(kernel, functools.partial) else kernel
    return pl.pallas_call(
        kernel,
        name=plain.__name__,
        out_shape=out_shape,
        scratch_shapes=scratch,
        compiler_params=pltpu.CompilerParams(vmem_limit_bytes=limit),
        cost_estimate=pl.CostEstimate(
            flops=0, bytes_accessed=int(micros * BYTES_PER_MICRO), transcendentals=0
        ),
        **options,
    )


def vmem():
    return pl.BlockSpec(memory_space=pltpu.VMEM)


def f32(*shape):
    return jax.ShapeDtypeStruct(shape, jnp.float32)


def block_vectors(matrix, vectors):
    size = len(vectors[0][0])
    out = [([], []) for _ in vectors]
    for i in range(size):
        totals = [None] * len(vectors)
        for j in range(size):
            a, b = matrix(0, i, j), matrix(1, i, j)
            for place, vector in enumerate(vectors):
                c, d = vector[0][j], vector[1][j]
                term = (a * c - b * d, a * d + b * c)
                if j > 0:
                    term = (totals[place][0] + term[0], totals[place][1] + term[1])
                totals[place] = term
        for place, total in enumerate(totals):
            out[place][0].append(total[0])
            out[place][1].append(total[1])
    return out


def block_vector(matrix, vector):
    return block_vectors(matrix, [vector])[0]


def plus(left, right):
    return [[a + b for a, b in zip(x, y)] for x, y in zip(left, right)]


def minus(left, right):
    return [[a - b for a, b in zip(x, y)] for x, y in zip(left, right)]


def negative(vector):
    return [[-a for a in x] for x in vector]


def load_vector(ref, size, *where):
    return [[ref[(r, i) + where] for i in range(size)] for r in range(2)]


def store_vector(ref, vector, *where):
    for r in range(2):
        for i, plane in enumerate(vector[r]):
            ref[(r, i) + where] = plane


def entry(ref, *lead, rows=slice(None)):
    return lambda r, i, j: ref[lead + (r, i, j, rows)].astype(jnp.float32)


def reorder_matrix(points, rows, turn=0):
    size = points * rows
    to = lax.broadcasted_iota(jnp.int32, (size, size), 0)
    of = lax.broadcasted_iota(jnp.int32, (size, size), 1)
    wanted = (to % points) * rows + ((to // points) ^ turn)
    return jnp.where(of == wanted, 1.0, 0.0).astype(jnp.bfloat16)


def repack_kernel(rows, groups, forcing_ref, *out_refs):
    fields, columns = forcing_ref.shape[1:3]
    points = forcing_ref.shape[3] // rows
    each = columns // groups
    at = lax.axis_index("span")
    order = reorder_matrix(points, rows, at // groups)
    peak = jnp.zeros((points * rows, 256), jnp.float32)
    for r in range(2):
        for i in range(fields):
            for b in range(groups):
                for t in range(0, each, 2):
                    chosen = [
                        (t + side) * groups + (b ^ (at % groups)) if groups > 1 else t + side
                        for side in range(2)
                    ]
                    pair = jnp.concatenate(
                        [forcing_ref[r, i, column] for column in chosen], axis=1
                    )
                    moved = jnp.dot(order, pair, preferred_element_type=jnp.float32)
                    peak = jnp.maximum(peak, jnp.abs(moved))
                    moved = moved.astype(jnp.bfloat16)
                    for side in range(2):
                        plane = ((t + side) * 2 + r) * fields + i
                        for j in range(rows):
                            out_refs[j * groups + b][plane] = moved[
                                j * points : (j + 1) * points, side * 128 : (side + 1) * 128
                            ]
    peak = jnp.max(peak)
    for ref in out_refs:
        ref[each * 2 * fields] = jnp.full(ref.shape[1:], peak, jnp.float32).astype(jnp.bfloat16)


def filter_kernel(sources, kernel_ref, *refs):
    arrived, scale_ref, outs = refs[:sources], refs[sources], refs[sources + 1 :]
    each, fields, points = outs[0].shape[0], outs[0].shape[2], outs[0].shape[3]
    last = arrived[0].shape[0] - 1
    peak = arrived[0][last].astype(jnp.float32)
    for m in range(1, sources):
        peak = jnp.maximum(peak, arrived[m][last].astype(jnp.float32))
    peak = jnp.maximum(jnp.max(peak), 1e-30)
    scale = 2048.0 / jnp.full((8, 128), peak, jnp.float32)
    scale_ref[...] = jnp.full((8, 128), peak, jnp.float32) / 2048.0
    scale = jnp.max(scale)
    for i in range(fields):
        right = jnp.concatenate(
            [
                jnp.concatenate(
                    [
                        arrived[m][(t * 2 + r) * fields + i]
                        for m in range(sources)
                        for r in range(2)
                    ],
                    axis=0,
                )
                for t in range(each)
            ],
            axis=1,
        )
        both = jnp.dot(kernel_ref[i], right, preferred_element_type=jnp.float32)
        for m in range(sources):
            base = m * 4 * points
            total = (
                both[base : base + 2 * points] + both[base + 2 * points : base + 4 * points]
            ) * scale
            for t in range(each):
                for r in range(2):
                    outs[m][t, r, i] = total[
                        r * points : (r + 1) * points, t * 128 : (t + 1) * 128
                    ]


def reorder_kernel(rows, in_ref, after_ref, out_ref):
    size = in_ref.shape[1]
    points = in_ref.shape[3] // rows
    order = reorder_matrix(points, rows)

    def move(index, carry):
        r, i = index // size, index % size
        wide = jnp.concatenate([in_ref[r, i, j] for j in range(size)], axis=1)
        moved = jnp.dot(order, wide, preferred_element_type=jnp.float32).astype(out_ref.dtype)
        for j in range(size):
            for y in range(rows):
                out_ref[y, r, i, j] = moved[
                    y * points : (y + 1) * points, j * 128 : (j + 1) * 128
                ]
        return carry

    lax.fori_loop(0, 2 * size, move, 0)


def summary_kernel(rows, lower_ref, upper_ref, keep_ref, send_ref, held_ref):
    size = lower_ref.shape[2]
    half = lower_ref.shape[4] // 2
    core = lax.axis_index("wall") % 2

    def summarize(part, chosen):
        span = pl.ds(part * half, half)

        def column(ref, y):
            return [
                [
                    [-ref[y, r, i, j, span].astype(jnp.float32) for i in range(size)]
                    for r in range(2)
                ]
                for j in chosen
            ]

        def store(which, vectors):
            @pl.when(part == core)
            def _():
                for j, vector in zip(chosen, vectors):
                    for r in range(2):
                        for i in range(size):
                            keep_ref[which, r, i, j] = vector[r][i]

            @pl.when(part != core)
            def _():
                for j, vector in zip(chosen, vectors):
                    for r in range(2):
                        for i in range(size):
                            send_ref[which, r, i, j] = vector[r][i]

        states = column(lower_ref, 0)
        for place, state in enumerate(states):
            store_vector(held_ref.at[0, place], state)
        for y in range(1, rows):
            moved = block_vectors(entry(lower_ref, y, rows=span), states)
            states = [negative(move) for move in moved]
            for place, state in enumerate(states):
                store_vector(held_ref.at[y, place], state)
        store(0, states)
        for y in range(rows - 2, -1, -1):
            moved = block_vectors(entry(upper_ref, y, rows=span), states)
            states = [
                minus(load_vector(held_ref.at[y, place], size), move)
                for place, move in enumerate(moved)
            ]
        store(2, states)
        states = column(upper_ref, rows - 1)
        for y in range(rows - 2, -1, -1):
            moved = block_vectors(entry(upper_ref, y, rows=span), states)
            states = [negative(move) for move in moved]
        store(1, states)

    def half_of(part, carry):
        def pair(step, carry):
            summarize(part, [2 * step, 2 * step + 1])
            return carry

        lax.fori_loop(0, size // 2, pair, 0)
        if size % 2:
            summarize(part, [size - 1])
        return carry

    lax.fori_loop(0, 2, half_of, 0)


def pair_matrices_kernel(keep_ref, other_ref, pair_ref, chip_ref, joint_ref):
    core = lax.axis_index("wall") % 2
    size = keep_ref.shape[2]
    for which in range(3):
        for r in range(2):
            for i in range(size):
                for j in range(size):
                    pair_ref[core, which, r, i, j] = keep_ref[which, r, i, j]
                    pair_ref[1 - core, which, r, i, j] = other_ref[which, r, i, j]

    def column(j, carry):
        def read(*lead):
            return [[pair_ref[lead + (r, i, j)] for i in range(size)] for r in range(2)]

        def write(ref, vector, *lead):
            for r in range(2):
                for i in range(size):
                    ref[lead + (r, i, j)] = vector[r][i]

        through = read(0, 0)
        write(chip_ref, block_vector(entry(pair_ref, 1, 0), through), 0)
        write(chip_ref, block_vector(entry(pair_ref, 0, 1), read(1, 1)), 1)
        joint = block_vector(entry(pair_ref, 1, 2), through)
        write(joint_ref, joint)
        write(chip_ref, plus(read(0, 2), block_vector(entry(pair_ref, 0, 1), joint)), 2)
        return carry

    lax.fori_loop(0, size, column, 0)


def upper_half_kernel(chip_ref, beside_ref, out_ref):
    size = chip_ref.shape[2]

    chip = lax.axis_index("wall") // 2

    @pl.when(chip == 2)
    def _():
        def column(j, carry):
            state = [[chip_ref[0, r, i, j] for i in range(size)] for r in range(2)]
            state = block_vector(entry(beside_ref), state)
            state = block_vector(entry(chip_ref, 1), state)
            for r in range(2):
                for i in range(size):
                    out_ref[r, i, j] = chip_ref[2, r, i, j] + state[r][i]
            return carry

        lax.fori_loop(0, size, column, 0)

    @pl.when(chip != 2)
    def _():
        out_ref[...] = jnp.zeros_like(out_ref)


def local_kernel(
    columns, first, spans, rows, pivot_ref, lower_ref, upper_ref, scale_ref, *refs
):
    arrived = refs[:spans]
    source_ref, keep_ref, send_ref, driving_ref, sweep_ref = refs[spans:]
    size = pivot_ref.shape[2]
    points = pivot_ref.shape[4]
    half = points // 2
    groups = spans // rows
    at = lax.axis_index("span")
    scale = jnp.max(scale_ref[...])
    for m in range(spans):
        y = (m // groups) ^ (at // groups)
        for t in range(columns // groups):
            c = t * groups + ((m % groups) ^ (at % groups)) if groups > 1 else t
            driving_ref[y, c] = arrived[m][first // groups + t] * scale
    core = lax.axis_index("wall") % 2

    def solve(part, carry):
        span = pl.ds(part * half, half)
        states = None
        for y in range(rows):
            drivings = [load_vector(driving_ref.at[y, c], size, span) for c in range(columns)]
            news = block_vectors(entry(pivot_ref, y, rows=span), drivings)
            for c in range(columns):
                store_vector(source_ref.at[y, c], news[c], span)
            if states is not None:
                moved = block_vectors(entry(lower_ref, y, rows=span), states)
                news = [minus(new, move) for new, move in zip(news, moved)]
            states = news
            for c in range(columns):
                store_vector(sweep_ref.at[y, c], states[c])
        for y in range(rows - 2, -1, -1):
            moved = block_vectors(entry(upper_ref, y, rows=span), states)
            states = [
                minus(load_vector(sweep_ref.at[y, c], size), moved[c]) for c in range(columns)
            ]

        def put(ref):
            for c in range(columns):
                ref[0, c] = sweep_ref[rows - 1, c]
                store_vector(ref.at[1, c], states[c])

        @pl.when(part == core)
        def _():
            put(keep_ref)

        @pl.when(part != core)
        def _():
            put(send_ref)

        return carry

    lax.fori_loop(0, 2, solve, 0)


def pair_kernel(
    columns, chips, pair_ref, keep_ref, other_ref, chip_ref, inner_ref, send_ref, both_ref
):
    core = lax.axis_index("wall") % 2
    low = lax.axis_index("wall") // 2 < chips // 2
    size = pair_ref.shape[3]
    both_ref[core] = keep_ref[...]
    both_ref[1 - core] = other_ref[...]

    def column(c, carry):
        first = load_vector(both_ref.at[0, 0, c], size)
        forth = plus(
            load_vector(both_ref.at[1, 0, c], size), block_vector(entry(pair_ref, 1, 0), first)
        )
        entering = plus(
            load_vector(both_ref.at[1, 1, c], size), block_vector(entry(pair_ref, 1, 2), first)
        )
        back = plus(
            load_vector(both_ref.at[0, 1, c], size),
            block_vector(entry(pair_ref, 0, 1), entering),
        )
        store_vector(inner_ref.at[0, c], first)
        store_vector(inner_ref.at[1, c], entering)
        store_vector(chip_ref.at[0, c], forth)
        store_vector(chip_ref.at[1, c], back)

        @pl.when(low)
        def _():
            store_vector(send_ref.at[c], forth)

        @pl.when(jnp.logical_not(low))
        def _():
            store_vector(send_ref.at[c], back)

        return carry

    lax.fori_loop(0, columns, column, 0)


def halves_kernel(
    columns, matrices_ref, beside_ref, chip_ref, came_ref, out_ref
):
    size = beside_ref.shape[1]
    chip = lax.axis_index("wall") // 2

    @pl.when(chip == 1)
    def _():
        def column(c, carry):
            moved = block_vector(entry(matrices_ref, 0), load_vector(came_ref.at[c], size))
            store_vector(out_ref.at[c], plus(load_vector(chip_ref.at[0, c], size), moved))
            return carry

        lax.fori_loop(0, columns, column, 0)

    @pl.when(chip == 2)
    def _():
        def column(c, carry):
            forth = load_vector(chip_ref.at[0, c], size)
            moved = plus(load_vector(came_ref.at[c], size), block_vector(entry(beside_ref), forth))
            moved = block_vector(entry(matrices_ref, 1), moved)
            store_vector(out_ref.at[c], plus(load_vector(chip_ref.at[1, c], size), moved))
            return carry

        lax.fori_loop(0, columns, column, 0)

    @pl.when((chip == 0) | (chip == 3))
    def _():
        out_ref[...] = jnp.zeros_like(out_ref)


def middle_kernel(
    columns,
    matrices_ref,
    beside_ref,
    upper_ref,
    chip_ref,
    first_ref,
    mine_ref,
    came_ref,
    edge_ref,
    out_ref,
):
    size = beside_ref.shape[1]
    chip = lax.axis_index("wall") // 2

    @pl.when(chip == 1)
    def _():
        def column(c, carry):
            answer = plus(
                load_vector(came_ref.at[c], size),
                block_vector(entry(upper_ref), load_vector(mine_ref.at[c], size)),
            )
            store_vector(edge_ref.at[1, c], answer)
            onward = plus(
                load_vector(chip_ref.at[1, c], size), block_vector(entry(matrices_ref, 1), answer)
            )
            entering = load_vector(first_ref.at[c], size)
            store_vector(edge_ref.at[0, c], entering)
            store_vector(
                out_ref.at[c], plus(onward, block_vector(entry(matrices_ref, 2), entering))
            )
            return carry

        lax.fori_loop(0, columns, column, 0)

    @pl.when(chip == 2)
    def _():
        def column(c, carry):
            entering = load_vector(came_ref.at[c], size)
            store_vector(edge_ref.at[0, c], entering)
            onward = plus(
                load_vector(chip_ref.at[0, c], size),
                block_vector(entry(matrices_ref, 0), entering),
            )
            store_vector(out_ref.at[c], onward)
            store_vector(
                edge_ref.at[1, c],
                plus(
                    load_vector(first_ref.at[c], size), block_vector(entry(beside_ref), onward)
                ),
            )
            return carry

        lax.fori_loop(0, columns, column, 0)

    @pl.when((chip == 0) | (chip == 3))
    def _():
        edge_ref[...] = jnp.zeros_like(edge_ref)
        out_ref[...] = jnp.zeros_like(out_ref)


def split_kernel(
    columns, outer, pair_ref, joint_ref, inner_ref, edge_ref, *refs
):
    came_ref = refs[0] if outer else None
    keep_ref, send_ref, entry_ref = refs[-3:]
    core, chip = lax.axis_index("wall") % 2, lax.axis_index("wall") // 2
    size = pair_ref.shape[3]
    entry_ref[...] = edge_ref[...]
    if outer:

        @pl.when(chip == 0)
        def _():
            entry_ref[1] = came_ref[...]

        @pl.when(chip == 3)
        def _():
            entry_ref[0] = came_ref[...]

    def column(c, carry):
        sweep = load_vector(entry_ref.at[0, c], size)
        upper_sweep = plus(
            load_vector(inner_ref.at[0, c], size), block_vector(entry(pair_ref, 0, 0), sweep)
        )
        middle = plus(
            load_vector(inner_ref.at[1, c], size), block_vector(entry(joint_ref), sweep)
        )
        answer = load_vector(entry_ref.at[1, c], size)
        lower_answer = plus(middle, block_vector(entry(pair_ref, 1, 1), answer))

        def put(lower_target, upper_target):
            store_vector(lower_target.at[0, c], sweep)
            store_vector(lower_target.at[1, c], lower_answer)
            store_vector(upper_target.at[0, c], upper_sweep)
            store_vector(upper_target.at[1, c], answer)

        @pl.when(core == 0)
        def _():
            put(keep_ref, send_ref)

        @pl.when(core == 1)
        def _():
            put(send_ref, keep_ref)

        return carry

    lax.fori_loop(0, columns, column, 0)


def answer_kernel(
    columns, first, rows, lower_ref, upper_ref, source_ref, keep_ref, other_ref, *refs
):
    out_ref, sweep_ref, edge_ref, made_ref, done = refs[-5:]
    core = lax.axis_index("wall") % 2
    size = lower_ref.shape[2]
    points = lower_ref.shape[4]
    half = points // 2
    edge_ref[core] = keep_ref[...]
    edge_ref[1 - core] = other_ref[...]

    def copies(part):
        return [
            pltpu.make_async_copy(
                made_ref.at[part, r, i],
                out_ref.at[
                    r, i, pl.ds(first, columns), pl.ds(part * half * rows, half * rows)
                ],
                done.at[part, r, i],
            )
            for r in range(2)
            for i in range(size)
        ]

    def run(part, carry):
        span = pl.ds(part * half, half)
        states = [load_vector(edge_ref.at[part, 0, c], size) for c in range(columns)]
        for y in range(rows):
            moved = block_vectors(entry(lower_ref, y, rows=span), states)
            states = [
                minus(load_vector(source_ref.at[y, c], size, span), moved[c])
                for c in range(columns)
            ]
            for c in range(columns):
                store_vector(sweep_ref.at[y, c], states[c])
        states = [load_vector(edge_ref.at[part, 1, c], size) for c in range(columns)]
        for y in range(rows - 1, -1, -1):
            moved = block_vectors(entry(upper_ref, y, rows=span), states)
            states = [
                minus(load_vector(sweep_ref.at[y, c], size), moved[c]) for c in range(columns)
            ]
            place = pl.ds(y, half, stride=rows)
            for c in range(columns):
                for r in range(2):
                    for i in range(size):
                        made_ref[part, r, i, c, place] = states[c][r][i]
        for copy in copies(part):
            copy.start()
        return carry

    lax.fori_loop(0, 2, run, 0)
    for copy in copies(0) + copies(1):
        copy.wait()


def span_kernel(span_factor, own, span_at):
    count = span_factor.shape[2]
    fields = span_factor.shape[1]
    slot = jnp.arange(count, dtype=jnp.int32)
    points = (span_at ^ (slot // own)) * own + slot % own
    modes = jnp.arange(count, dtype=jnp.int32)
    scale = 2.0 * math.pi / count
    angle_points = (points[:, None] * modes[None, :] % count).astype(jnp.float32) * scale
    cos_points = jnp.cos(angle_points)[None]
    sin_points = jnp.sin(angle_points)[None]
    factor_re = span_factor[0][:, None, :] / count
    factor_im = span_factor[1][:, None, :] / count
    left_re = factor_re * cos_points - factor_im * sin_points
    left_im = factor_re * sin_points + factor_im * cos_points
    spans = count // own
    left = jnp.stack(
        [
            jnp.concatenate([left_re, left_im], axis=2).reshape(fields, spans, own, 2 * count),
            jnp.concatenate([left_im, -left_re], axis=2).reshape(fields, spans, own, 2 * count),
        ],
        axis=2,
    ).reshape(fields * 2 * count, 2 * count)
    quarter = count // 4
    column = jnp.arange(2 * count, dtype=jnp.int32)
    place = (span_at ^ (column // (2 * own))) * own + column % own
    turn = (column // own) % 2 * quarter
    steps = (modes[:, None] * place[None, :] + (count - turn)[None, :]) % count
    angle = steps.astype(jnp.float32) * scale
    right = jnp.concatenate([jnp.cos(angle), jnp.sin(angle)], axis=0)
    whole = jnp.dot(left, right, precision=exact_mode).reshape(fields, spans, 2 * own, -1)
    high = lax.reduce_precision(whole, 8, 7)
    low = whole - high
    both = jnp.concatenate([high, low], axis=2).astype(jnp.bfloat16)
    return both.reshape(fields, 4 * count, -1)


def affine(matrix, vector, offset):
    left_re, left_im = matrix[0][None], matrix[1][None]
    right_re, right_im = vector[:, 0, None], vector[:, 1, None]
    real = jnp.sum(left_re * right_re - left_im * right_im, axis=2)
    imag = jnp.sum(left_re * right_im + left_im * right_re, axis=2)
    return offset + jnp.stack([real, imag], axis=1)


def local(forcing, span_factor, pivot_inverse, step_lower, step_upper):
    parts, fields, columns, points, rows, width = forcing.shape
    spans, walls = lax.axis_size("span"), lax.axis_size("wall")
    chips = walls // 2
    half = points // 2
    span_at = lax.axis_index("span")

    flat = (points * rows, width)
    forcing = forcing.reshape(forcing.shape[:3] + flat)
    pivot_inverse = pivot_inverse.reshape(pivot_inverse.shape[:3] + flat)
    step_lower = step_lower.reshape(step_lower.shape[:3] + flat)
    step_upper = step_upper.reshape(step_upper.shape[:3] + flat)

    def swap(array, distance, axis, name):
        count = spans if axis == "span" else walls
        with jax.named_scope(name):
            return lax.ppermute(array, axis, [(i, i ^ distance) for i in range(count)])

    def gate(array, *earlier):
        return lax.optimization_barrier((array,) + earlier)[0]

    groups = spans // rows
    kernel = span_kernel(span_factor, points, span_at)
    block = (columns // groups * 2 * fields + 1, points, width)
    sent = call(
        functools.partial(repack_kernel, rows, groups),
        [jax.ShapeDtypeStruct(block, jnp.bfloat16)] * spans,
        micros=2.0,
        in_specs=[vmem()],
    )(forcing)
    sent = [sent[0]] + [
        swap(sent[m], m, "span", f"forcing{m}") for m in range(1, spans)
    ]

    kept = jnp.bfloat16 if half % 16 == 0 else jnp.float32
    moved_shape = jax.ShapeDtypeStruct((rows, 2, fields, fields, points, width), kept)
    plane = (half, width)
    summary = f32(3, 2, fields, fields, *plane)
    def reorder(matrix, after):
        return call(
            functools.partial(reorder_kernel, rows),
            moved_shape,
            micros=2.0,
            in_specs=[vmem(), pl.BlockSpec(memory_space=pl.ANY)],
        )(matrix, after)

    lowers, uppers = reorder(step_lower, sent[0]), reorder(step_upper, sent[0])
    keep, send = call(
        functools.partial(summary_kernel, rows),
        [summary] * 2,
            micros=8.2,
        scratch=[pltpu.VMEM((rows, 2, 2, fields) + plane, jnp.float32)],
        in_specs=[vmem()] * 2,
    )(lowers, uppers)
    scale, *outs = call(
        functools.partial(filter_kernel, spans),
        [f32(8, 128)] + [f32(columns // groups, 2, fields, points, width)] * spans,
        micros=1.0,
    )(gate(kernel, keep), *sent)
    drivings = [outs[0]] + [
        swap(outs[m].astype(jnp.float16), m, "span", f"driving{m}").astype(jnp.float32)
        for m in range(1, spans)
    ]

    pivots = reorder(pivot_inverse, outs[0])
    other = swap(send, 1, "wall", "matrices_core")
    pair, chip_matrices, joint = call(
        pair_matrices_kernel,
        [
            f32(2, *summary.shape),
            summary,
            f32(2, fields, fields, *plane),
        ],
            micros=3.6,
        in_specs=[vmem()] * 2,
    )(gate(keep, drivings[1]), other)
    tree = chips == 4
    outward = [(i, i ^ 2) for i in range(walls)]
    inward = [(0, 1), (1, 0), (2, 4), (4, 2), (3, 5), (5, 3), (6, 7), (7, 6)]
    if tree:
        with jax.named_scope("matrices_outward"):
            beside = lax.ppermute(chip_matrices[2], "wall", outward)

    out = None
    for number, chosen in enumerate(CHUNKS):
        count = len(chosen)
        vectors = f32(2, count, 2, fields, *plane)
        single = f32(count, 2, fields, *plane)
        size = 2 * fields * count * half * width
        taken = drivings
        source, keep, send = call(
            functools.partial(local_kernel, count, chosen[0], spans, rows),
            [f32(rows, count, 2, fields, points, width), vectors, vectors],
            micros=2.2 * count,
            scratch=[
                pltpu.VMEM((rows, count, 2, fields, points, width), jnp.float32),
                pltpu.VMEM((rows, count, 2, fields) + plane, jnp.float32),
            ],
            in_specs=[vmem()] * (4 + len(taken)),
        )(pivots, lowers, uppers, scale, *taken)
        other = swap(send, 1, "wall", f"chunk{number}_core")
        chip, inner, outgoing = call(
            functools.partial(pair_kernel, count, chips),
            [vectors, vectors, single],
            micros=0.5 * count,
            scratch=[pltpu.VMEM((2,) + vectors.shape, jnp.float32)],
            in_specs=[vmem()] * 3,
        )(pair, keep, other)
        extra = ()
        if tree and number == 0:
            upper_half = call(
                upper_half_kernel,
                f32(2, fields, fields, *plane),
                micros=0.7,
                in_specs=[vmem()] * 2,
            )(gate(chip_matrices, outgoing), beside)
            with jax.named_scope("matrices_inward"):
                upper_half = lax.ppermute(upper_half, "wall", inward)
        if tree:
            with jax.named_scope(f"chunk{number}_to_middle"):
                came = lax.ppermute(outgoing, "wall", outward)
            mine = call(
                functools.partial(halves_kernel, count),
                single,
            micros=0.3 * count,
                in_specs=[vmem()] * 4,
            )(chip_matrices, beside, chip, came)
            with jax.named_scope(f"chunk{number}_middle"):
                across = lax.ppermute(mine, "wall", inward)
            edge, outgoing = call(
                functools.partial(middle_kernel, count),
                [vectors, single],
            micros=0.3 * count,
                in_specs=[vmem()] * 7,
            )(chip_matrices, beside, upper_half, chip, came, mine, across)
            with jax.named_scope(f"chunk{number}_to_ends"):
                extra = (lax.ppermute(outgoing, "wall", outward),)
        else:
            sweep = jnp.zeros(single.shape, jnp.float32)
            answer = jnp.zeros(single.shape, jnp.float32)
            upward = [(i, i + 2) for i in range(walls - 2)]
            downward = [(i + 2, i) for i in range(walls - 2)]
            for _ in range(chips - 1):
                sweep = lax.ppermute(affine(chip_matrices[0], sweep, chip[0]), "wall", upward)
            offset = affine(chip_matrices[2], sweep, chip[1])
            for _ in range(chips - 1):
                answer = lax.ppermute(affine(chip_matrices[1], answer, offset), "wall", downward)
            edge = jnp.stack([sweep, answer])
        keep, send = call(
            functools.partial(split_kernel, count, tree),
            [vectors, vectors],
            micros=0.5 * count,
            scratch=[pltpu.VMEM(vectors.shape, jnp.float32)],
            in_specs=[vmem()] * (4 + len(extra)),
        )(pair, joint, inner, edge, *extra)
        other = swap(send, 1, "wall", f"chunk{number}_apart")
        held = () if out is None else (out,)
        out = call(
            functools.partial(answer_kernel, count, chosen[0], rows),
            f32(2, fields, columns, *flat),
            micros=1.2 * count,
            scratch=[
                pltpu.VMEM((rows, count, 2, fields) + plane, jnp.float32),
                pltpu.VMEM((2,) + vectors.shape, jnp.float32),
                pltpu.VMEM((2, 2, fields, count, half * rows, width), jnp.float32),
                pltpu.SemaphoreType.DMA((2, 2, fields)),
            ],
            in_specs=[vmem()] * 5 + [pl.BlockSpec(memory_space=pl.ANY)] * len(held),
            out_specs=pl.BlockSpec(memory_space=pl.ANY),
            input_output_aliases={5: 0} if held else {},
        )(lowers, uppers, source, keep, other, *held)
    return out.reshape(2, fields, columns, points, rows, width)


def solution(mesh):
    placed = (
        P(None, None, None, "span", "wall", None),
        P(),
        P(None, None, None, "span", "wall", None),
        P(None, None, None, "span", "wall", None),
        P(None, None, None, "span", "wall", None),
    )
    return jax.shard_map(
        local,
        mesh=mesh,
        in_specs=placed,
        out_specs=P(None, None, None, "span", "wall", None),
        check_vma=False,
    )
```

time: 115 us -> 86.8 us (0.75)
  local copies, waits for them, and re-layouts: 16 us -> 4.69 us
  starting transfers between devices: 40.3 us -> 31.5 us
  Pallas kernels: 39.9 us -> 33.6 us
  waiting for transfers between devices: 15 us -> 13.5 us
    ppermute x17 -> x11, starting transfers between devices: 26.2 us -> 15.8 us  [swap(): return lax.ppermute(array, axis, [(i, i ^ distance) for i in range(count)])]
    squeeze x14 -> x0, local copies, waits for them, and re-layouts: 8.23 us -> none  [local(): arrived[column] = [got[m][r] for m in range(spans) for r in range(2)]]
    pallas_call x16 -> x19, Pallas kernels: 37.9 us -> 30.8 us  [the longest x1 7.02 us: local(): call(functools.partial(summary_kernel, rows), [summary] * 2, micros=8.2,...]
    ppermute x1, waiting for transfers between devices: 4.9 us -> 0.01 us  [local(): beside = lax.ppermute(chip_matrices[2], 'wall', outward)]
    unnamed x16 -> x18, local copies, waits for them, and re-layouts: 0.03 us -> 4.65 us
    reshape x2 -> x0, local copies, waits for them, and re-layouts: 3.85 us -> none  [the longest x1 3.65 us: span_kernel(): whole = jnp.stack([real, imag], axis=1).reshape(fields, 2 * own, -1)]
    another operation x3 -> x0, local copies, waits for them, and re-layouts: 2.29 us -> none  [the longest x1 2.08 us: span_kernel(): whole = jnp.stack([real, imag], axis=1).reshape(fields, 2 * own, -1)]
    ppermute x2, starting transfers between devices: 5.18 us -> 7.24 us  [local(): extra = (lax.ppermute(outgoing, 'wall', outward),)]
  transfers between devices with their start and end apart: 25 -> 19, of which waited for: 6 -> 5; matrix products, arithmetic and copies ran while one was open for 15% -> 3% of each run, Pallas kernels for 30% -> 33%
where the time goes in v2:
time: 86.8 us; the launch traced here: 86.6 us
  Pallas kernels  33.6 us (39%)
  starting transfers between devices  31.5 us (36%)
  waiting for transfers between devices  13.5 us (16%)
  local copies, waits for them, and re-layouts  4.69 us (5%)
  other arithmetic  1.62 us (2%)
  matrix products  1.19 us (1%)
    ppermute x11, starting transfers between devices, swap(): return lax.ppermute(array, axis, [(i, i ^ distance) for i in range(count)])  15.8 us
    ppermute x11, waiting for transfers between devices, swap(): return lax.ppermute(array, axis, [(i, i ^ distance) for i in range(count)])  9.2 us
    ppermute x2, starting transfers between devices, local(): extra = (lax.ppermute(outgoing, 'wall', outward),)  7.24 us
    pallas_call x1, Pallas kernels, local(): call(functools.partial(summary_kernel, rows), [summary] * 2, micros=8.2,...  7.02 us
    pallas_call x2, Pallas kernels, local(): call(functools.partial(answer_kernel, count, chosen[0], rows), f32(2, fie...  6.14 us
    pallas_call x3, Pallas kernels, reorder(): call(functools.partial(reorder_kernel, rows), moved_shape, micros=2.0, in...  5.99 us
    pallas_call x2, Pallas kernels, local(): call(functools.partial(local_kernel, count, chosen[0], spans, rows), [f32...  5.52 us
    unnamed x18, local copies, waits for them, and re-layouts  4.65 us
  transfers between devices with their start and end apart: 19, of which 5 were waited for; matrix products, arithmetic and copies ran while one was open for 3% of the time, Pallas kernels for 33%

profile of v2, /device:TPU:1, one launch (start us, length us, event | category | flops | bytes accessed | tf_op | source)
XLA Modules:
  0.0 86.6 jit_solution(2613279973477208346)
XLA Ops:
  0.0 1.3 %copy-done.5 = bf16[2,5,4,32,4,128]{5,4,3,2,1,0:T(4,128)(2,1)S(1)} copy-done((bf16[2,5,4,32,4,128]{5,4,3,2,1,0:T(4,128)(2,1)S(1)}, bf16[2,5,4,32,4,128]{5,4,3,2,1,0:T(4,128)(2,1)}, u32[]{:S(2)}) %copy-start.5) | copy-done | bytes 1310744
  1.3 1.9 %repack_kernel.1 = (bf16[41,32,128]{2,1,0:T(8,128)(2,1)S(1)}, bf16[41,32,128]{2,1,0:T(8,128)(2,1)}, bf16[41,32,128]{2,1,0:T(8,128)(2,1)}, bf16[41,32,128]{2,1,0:T(8,128)(2,1)}) custom-call(bf16[2,5,4,128,128]{4,3,2,1,0:T(8,128)(2,1)S(1)} %bitcast.25), custom_call_target="tpu_custom_call" | custom-call | bytes 20000 | tf_op jit(solution)/shard_map/repack_kernel/pallas_call | solution.py:665
  3.3 2.0 %collective-permute-start = (bf16[41,32,128]{2,1,0:T(8,128)(2,1)}, bf16[41,32,128]{2,1,0:T(8,128)(2,1)}, u32[]{:S(2)}, u32[]{:S(2)}) collective-permute-start(bf16[41,32,128]{2,1,0:T(8,128)(2,1)} %get-tuple-element.45), channel_id=1, source_target_pairs={{0,8},{8,0},{16,24},{24,16},{1,9},{9,1},{17,25},{25,17},{2,10},{10... | collective-permute-start | bytes 1007624 | tf_op jit(solution)/shard_map/forcing1/ppermute | solution.py:657
  5.3 1.2 %collective-permute-start.1 = (bf16[41,32,128]{2,1,0:T(8,128)(2,1)}, bf16[41,32,128]{2,1,0:T(8,128)(2,1)}, u32[]{:S(2)}, u32[]{:S(2)}) collective-permute-start(bf16[41,32,128]{2,1,0:T(8,128)(2,1)} %get-tuple-element.46), channel_id=1, source_target_pairs={{0,16},{8,24},{16,0},{24,8},{1,17},{9,25},{17,1},{25,9},{2,18},{10... | collective-permute-start | bytes 1007624 | tf_op jit(solution)/shard_map/forcing2/ppermute | solution.py:657
  6.6 1.4 %copy-done.2 = bf16[2,5,5,32,4,128]{5,4,3,2,1,0:T(4,128)(2,1)S(1)} copy-done((bf16[2,5,5,32,4,128]{5,4,3,2,1,0:T(4,128)(2,1)S(1)}, bf16[2,5,5,32,4,128]{5,4,3,2,1,0:T(4,128)(2,1)}, u32[]{:S(2)}) %copy-start.2) | copy-done | bytes 1638424
  8.0 2.0 %reorder_kernel.4.upper_ref = bf16[4,2,5,5,32,128]{5,4,3,2,1,0:T(8,128)(2,1)S(1)} custom-call(bf16[2,5,5,128,128]{4,3,2,1,0:T(8,128)(2,1)S(1)} %bitcast.22, bf16[41,32,128]{2,1,0:T(8,128)(2,1)S(1)} %get-tuple-element.42.after_ref.refs_0_), custom_call_target="tpu_custom_call" | custom-call | bytes 20000 | tf_op jit(solution)/shard_map/reorder_kernel/pallas_call | solution.py:680
  10.0 2.0 %reorder_kernel.3.lower_ref = bf16[4,2,5,5,32,128]{5,4,3,2,1,0:T(8,128)(2,1)S(1)} custom-call(bf16[2,5,5,128,128]{4,3,2,1,0:T(8,128)(2,1)S(1)} %bitcast.23, bf16[41,32,128]{2,1,0:T(8,128)(2,1)S(1)} %get-tuple-element.42.after_ref.refs_0_), custom_call_target="tpu_custom_call" | custom-call | bytes 20000 | tf_op jit(solution)/shard_map/reorder_kernel/pallas_call | solution.py:680
  12.0 7.0 %summary_kernel.1 = (f32[3,2,5,5,16,128]{5,4,3,2,1,0:T(8,128)S(1)}, f32[3,2,5,5,16,128]{5,4,3,2,1,0:T(8,128)}) custom-call(bf16[4,2,5,5,32,128]{5,4,3,2,1,0:T(8,128)(2,1)S(1)} %reorder_kernel.3.lower_ref, bf16[4,2,5,5,32,128]{5,4,3,2,1,0:T(8,128)(2,1)S(1)} %reorder_kernel.4.upper_ref), custom_call_target="tpu_custom_call" | custom-call | bytes 82000 | tf_op jit(solution)/shard_map/summary_kernel/pallas_call | solution.py:688
  19.0 1.1 %copy-done.6 = f32[3,2,5,5,16,128]{5,4,3,2,1,0:T(8,128)} copy-done((f32[3,2,5,5,16,128]{5,4,3,2,1,0:T(8,128)}, f32[3,2,5,5,16,128]{5,4,3,2,1,0:T(8,128)S(1)}, u32[]{:S(2)}) %copy-start.6) | copy-done | bytes 1228824
  20.1 1.3 %collective-permute-start.6 = (f32[3,2,5,5,16,128]{5,4,3,2,1,0:T(8,128)}, f32[3,2,5,5,16,128]{5,4,3,2,1,0:T(8,128)}, u32[]{:S(2)}, u32[]{:S(2)}) collective-permute-start(f32[3,2,5,5,16,128]{5,4,3,2,1,0:T(8,128)} %get-tuple-element.55), channel_id=1, source_target_pairs={{0,1},{1,0},{2,3},{3,2},{4,5},{5,4},{6,7},{7,6},{8,9},{9,8},{10,11... | collective-permute-start | bytes 3686408 | tf_op jit(solution)/shard_map/matrices_core/ppermute | solution.py:657
  22.5 1.2 %reduce-precision_convert_fusion = (bf16[5,4,64,256]{3,2,1,0:T(8,128)(2,1)S(1)}, bf16[5,4,64,256]{3,2,1,0:T(8,128)(2,1)S(1)}) fusion(f32[5,4,64,256]{3,2,1,0:T(8,128)S(1)} %bitcast.26, f32[128,256]{1,0:T(8,128)S(1)} %get-tuple-element.87, f32[128,256]{1,0:T(8,128)S(1)} %get-tuple-element.86), kind=kOutput, calls=%fused_computation.1 | convolution fusion | flops 1008009216 | bytes 2883584 | tf_op jit(solution)/shard_map/dot_general | solution.py:626
  24.7 2.1 %filter_kernel.1 = (f32[8,128]{1,0:T(8,128)S(1)}, f32[4,2,5,32,128]{4,3,2,1,0:T(8,128)S(1)}, f32[4,2,5,32,128]{4,3,2,1,0:T(8,128)S(1)}, f32[4,2,5,32,128]{4,3,2,1,0:T(8,128)S(1)}, f32[4,2,5,32,128]{4,3,2,1,0:T(8,128)S(1)}) custom-call(bf16[5,512,256]{2,1,0:T(8,128)(2,1)S(1)} %bitcast.21, bf16[41,32,128]{2,1,0:T(8,128)(2,1)S(1)} %copy-done.1, ...), custom_call_target="tpu_custom_call" | custom-call | bytes 10000 | tf_op jit(solution)/shard_map/filter_kernel/pallas_call | solution.py:695
  26.8 1.8 %collective-permute-start.3 = (f16[4,2,5,32,128]{4,3,2,1,0:T(8,128)(2,1)S(1)}, f16[4,2,5,32,128]{4,3,2,1,0:T(8,128)(2,1)S(1)}, u32[]{:S(2)}, u32[]{:S(2)}) collective-permute-start(f16[4,2,5,32,128]{4,3,2,1,0:T(8,128)(2,1)S(1)} %convert_element_type.39), channel_id=1, source_target_pairs={{0,8},{8,0},{16,24},{24,16},{1,9},{9,1},{17,25},{25,17},{2,10},{10... | collective-permute-start | bytes 983048 | tf_op jit(solution)/shard_map/driving1/ppermute | solution.py:657
  28.7 1.3 %collective-permute-start.5 = (f16[4,2,5,32,128]{4,3,2,1,0:T(8,128)(2,1)S(1)}, f16[4,2,5,32,128]{4,3,2,1,0:T(8,128)(2,1)S(1)}, u32[]{:S(2)}, u32[]{:S(2)}) collective-permute-start(f16[4,2,5,32,128]{4,3,2,1,0:T(8,128)(2,1)S(1)} %convert_element_type.43), channel_id=1, source_target_pairs={{0,24},{8,16},{16,8},{24,0},{1,25},{9,17},{17,9},{25,1},{2,26},{10... | collective-permute-start | bytes 983048 | tf_op jit(solution)/shard_map/driving3/ppermute | solution.py:657
  30.1 6.5 %collective-permute-done.3 = f16[4,2,5,32,128]{4,3,2,1,0:T(8,128)(2,1)S(1)} collective-permute-done((f16[4,2,5,32,128]{4,3,2,1,0:T(8,128)(2,1)S(1)}, f16[4,2,5,32,128]{4,3,2,1,0:T(8,128)(2,1)S(1)}, u32[]{:S(2)}, u32[]{:S(2)}) %collective-permute-start.3) | collective-permute-done | bytes 327712 | tf_op jit(solution)/shard_map/driving1/ppermute | solution.py:657
  36.7 2.8 %pair_matrices_kernel.1 = (f32[2,3,2,5,5,16,128]{6,5,4,3,2,1,0:T(8,128)S(1)}, f32[3,2,5,5,16,128]{5,4,3,2,1,0:T(8,128)S(1)}, f32[2,5,5,16,128]{4,3,2,1,0:T(8,128)S(1)}) custom-call(f32[3,2,5,5,16,128]{5,4,3,2,1,0:T(8,128)S(1)} %copy-done.7, f32[3,2,5,5,16,128]{5,4,3,2,1,0:T(8,128)} %collective-permute-done.6.other_ref), custom_call_target="tpu_custom_call" | custom-call | bytes 36000 | tf_op jit(solution)/shard_map/pair_matrices_kernel/pallas_call | solution.py:707
  39.6 1.5 %collective-permute-start.8 = (f32[2,5,5,16,128]{4,3,2,1,0:T(8,128)S(1)}, f32[2,5,5,16,128]{4,3,2,1,0:T(8,128)S(1)}, u32[]{:S(2)}, u32[]{:S(2)}) collective-permute-start(f32[2,5,5,16,128]{4,3,2,1,0:T(8,128)S(1)} %slice_bitcast_fusion), channel_id=1, source_target_pairs={{0,2},{1,3},{2,0},{3,1},{4,6},{5,7},{6,4},{7,5},{8,10},{9,11},{10,... | collective-permute-start | bytes 1228808 | tf_op jit(solution)/shard_map/matrices_outward/ppermute | solution.py:722
  41.1 2.0 %reorder_kernel.5.pivot_ref = bf16[4,2,5,5,32,128]{5,4,3,2,1,0:T(8,128)(2,1)S(1)} custom-call(bf16[2,5,5,128,128]{4,3,2,1,0:T(8,128)(2,1)S(1)} %bitcast.24, f32[4,2,5,32,128]{4,3,2,1,0:T(8,128)S(1)} %get-tuple-element.48.after_ref.refs_0_), custom_call_target="tpu_custom_call" | custom-call | bytes 20000 | tf_op jit(solution)/shard_map/reorder_kernel/pallas_call | solution.py:680
  43.1 1.7 %collective-permute-done.5 = f16[4,2,5,32,128]{4,3,2,1,0:T(8,128)(2,1)S(1)} collective-permute-done((f16[4,2,5,32,128]{4,3,2,1,0:T(8,128)(2,1)S(1)}, f16[4,2,5,32,128]{4,3,2,1,0:T(8,128)(2,1)S(1)}, u32[]{:S(2)}, u32[]{:S(2)}) %collective-permute-start.5) | collective-permute-done | bytes 327712 | tf_op jit(solution)/shard_map/driving3/ppermute | solution.py:657
  45.9 2.8 %local_kernel.3 = (f32[4,2,2,5,32,128]{5,4,3,2,1,0:T(8,128)S(1)}, f32[2,2,2,5,16,128]{5,4,3,2,1,0:T(8,128)S(1)}, f32[2,2,2,5,16,128]{5,4,3,2,1,0:T(8,128)S(1)}) custom-call(bf16[4,2,5,5,32,128]{5,4,3,2,1,0:T(8,128)(2,1)S(1)} %reorder_kernel.5.pivot_ref, bf16[4,2,5,5,32,128]{5,4,3,2,1,0:T(8,128)(2,1)S(1)} %reorder_kernel.3.lower_ref, ...), custom_call_target="tpu_custom_call" | custom-call | bytes 44000 | tf_op jit(solution)/shard_map/local_kernel/pallas_call | solution.py:731
  48.7 1.5 %collective-permute-start.9 = (f32[2,2,2,5,16,128]{5,4,3,2,1,0:T(8,128)S(1)}, f32[2,2,2,5,16,128]{5,4,3,2,1,0:T(8,128)S(1)}, u32[]{:S(2)}, u32[]{:S(2)}) collective-permute-start(f32[2,2,2,5,16,128]{5,4,3,2,1,0:T(8,128)S(1)} %get-tuple-element.63), channel_id=1, source_target_pairs={{0,1},{1,0},{2,3},{3,2},{4,5},{5,4},{6,7},{7,6},{8,9},{9,8},{10,11... | collective-permute-start | bytes 983048 | tf_op jit(solution)/shard_map/chunk0_core/ppermute | solution.py:657
  50.1 2.8 %local_kernel.2 = (f32[4,2,2,5,32,128]{5,4,3,2,1,0:T(8,128)S(1)}, f32[2,2,2,5,16,128]{5,4,3,2,1,0:T(8,128)S(1)}, f32[2,2,2,5,16,128]{5,4,3,2,1,0:T(8,128)S(1)}) custom-call(bf16[4,2,5,5,32,128]{5,4,3,2,1,0:T(8,128)(2,1)S(1)} %reorder_kernel.5.pivot_ref, bf16[4,2,5,5,32,128]{5,4,3,2,1,0:T(8,128)(2,1)S(1)} %reorder_kernel.3.lower_ref, ...), custom_call_target="tpu_custom_call" | custom-call | bytes 44000 | tf_op jit(solution)/shard_map/local_kernel/pallas_call | solution.py:731
  54.1 2.7 %collective-permute-start.15 = (f32[2,2,5,16,128]{4,3,2,1,0:T(8,128)S(1)}, f32[2,2,5,16,128]{4,3,2,1,0:T(8,128)S(1)}, u32[]{:S(2)}, u32[]{:S(2)}) collective-permute-start(f32[2,2,5,16,128]{4,3,2,1,0:T(8,128)S(1)} %get-tuple-element.64), channel_id=1, source_target_pairs={{0,2},{1,3},{2,0},{3,1},{4,6},{5,7},{6,4},{7,5},{8,10},{9,11},{10,... | collective-permute-start | bytes 491528 | tf_op jit(solution)/shard_map/chunk0_to_middle/ppermute | solution.py:761
  57.3 3.3 %collective-permute-done.15.came_ref.first_ref = f32[2,2,5,16,128]{4,3,2,1,0:T(8,128)S(1)} collective-permute-done((f32[2,2,5,16,128]{4,3,2,1,0:T(8,128)S(1)}, f32[2,2,5,16,128]{4,3,2,1,0:T(8,128)S(1)}, u32[]{:S(2)}, u32[]{:S(2)}) %collective-permute-start.15) | collective-permute-done | bytes 163872 | tf_op jit(solution)/shard_map/chunk0_to_middle/ppermute | solution.py:761
  60.8 2.3 %collective-permute-start.16 = (f32[2,2,5,16,128]{4,3,2,1,0:T(8,128)S(1)}, f32[2,2,5,16,128]{4,3,2,1,0:T(8,128)S(1)}, u32[]{:S(2)}, u32[]{:S(2)}) collective-permute-start(f32[2,2,5,16,128]{4,3,2,1,0:T(8,128)S(1)} %halves_kernel.3.mine_ref), channel_id=1, source_target_pairs={{0,1},{1,0},{2,4},{4,2},{3,5},{5,3},{6,7},{7,6},{8,9},{9,8},{10,12... | collective-permute-start | bytes 491528 | tf_op jit(solution)/shard_map/chunk0_middle/ppermute | solution.py:769
  64.1 1.4 %collective-permute-start.12 = (f32[2,2,5,16,128]{4,3,2,1,0:T(8,128)S(1)}, f32[2,2,5,16,128]{4,3,2,1,0:T(8,128)S(1)}, u32[]{:S(2)}, u32[]{:S(2)}) collective-permute-start(f32[2,2,5,16,128]{4,3,2,1,0:T(8,128)S(1)} %halves_kernel.2.mine_ref), channel_id=1, source_target_pairs={{0,1},{1,0},{2,4},{4,2},{3,5},{5,3},{6,7},{7,6},{8,9},{9,8},{10,12... | collective-permute-start | bytes 491528 | tf_op jit(solution)/shard_map/chunk1_middle/ppermute | solution.py:769
  65.6 3.8 %collective-permute-start.17 = (f32[2,2,5,16,128]{4,3,2,1,0:T(8,128)S(1)}, f32[2,2,5,16,128]{4,3,2,1,0:T(8,128)S(1)}, u32[]{:S(2)}, u32[]{:S(2)}) collective-permute-start(f32[2,2,5,16,128]{4,3,2,1,0:T(8,128)S(1)} %get-tuple-element.76), channel_id=1, source_target_pairs={{0,2},{1,3},{2,0},{3,1},{4,6},{5,7},{6,4},{7,5},{8,10},{9,11},{10,... | collective-permute-start | bytes 491528 | tf_op jit(solution)/shard_map/chunk0_to_ends/ppermute | solution.py:777
  69.4 3.5 %collective-permute-start.13 = (f32[2,2,5,16,128]{4,3,2,1,0:T(8,128)S(1)}, f32[2,2,5,16,128]{4,3,2,1,0:T(8,128)S(1)}, u32[]{:S(2)}, u32[]{:S(2)}) collective-permute-start(f32[2,2,5,16,128]{4,3,2,1,0:T(8,128)S(1)} %get-tuple-element.69), channel_id=1, source_target_pairs={{0,2},{1,3},{2,0},{3,1},{4,6},{5,7},{6,4},{7,5},{8,10},{9,11},{10,... | collective-permute-start | bytes 491528 | tf_op jit(solution)/shard_map/chunk1_to_ends/ppermute | solution.py:777
  73.3 5.2 %collective-permute-start.18 = (f32[2,2,2,5,16,128]{5,4,3,2,1,0:T(8,128)S(1)}, f32[2,2,2,5,16,128]{5,4,3,2,1,0:T(8,128)S(1)}, u32[]{:S(2)}, u32[]{:S(2)}) collective-permute-start(f32[2,2,2,5,16,128]{5,4,3,2,1,0:T(8,128)S(1)} %get-tuple-element.78), channel_id=1, source_target_pairs={{0,1},{1,0},{2,3},{3,2},{4,5},{5,4},{6,7},{7,6},{8,9},{9,8},{10,11... | collective-permute-start | bytes 983048 | tf_op jit(solution)/shard_map/chunk0_apart/ppermute | solution.py:657
  78.9 1.3 %collective-permute-start.14 = (f32[2,2,2,5,16,128]{5,4,3,2,1,0:T(8,128)S(1)}, f32[2,2,2,5,16,128]{5,4,3,2,1,0:T(8,128)S(1)}, u32[]{:S(2)}, u32[]{:S(2)}) collective-permute-start(f32[2,2,2,5,16,128]{5,4,3,2,1,0:T(8,128)S(1)} %get-tuple-element.71), channel_id=1, source_target_pairs={{0,1},{1,0},{2,3},{3,2},{4,5},{5,4},{6,7},{7,6},{8,9},{9,8},{10,11... | collective-permute-start | bytes 983048 | tf_op jit(solution)/shard_map/chunk1_apart/ppermute | solution.py:657
  80.2 3.1 %answer_kernel.2.refs_0_ = f32[2,5,4,128,128]{4,3,2,1,0:T(8,128)} custom-call(bf16[4,2,5,5,32,128]{5,4,3,2,1,0:T(8,128)(2,1)S(1)} %reorder_kernel.3.lower_ref, bf16[4,2,5,5,32,128]{5,4,3,2,1,0:T(8,128)(2,1)S(1)} %reorder_kernel.4.upper_ref, f32[4,2,2,5,32,128]{5,4,3,2,1,0:T(8,128)S(1)} %get-tuple-element.72.source_ref, ...), custom_call_target="tpu_custom_call" | custom-call | bytes 24000 | tf_op jit(solution)/shard_map/answer_kernel/pallas_call | solution.py:798
  83.3 3.1 %answer_kernel.3 = f32[2,5,4,128,128]{4,3,2,1,0:T(8,128)} custom-call(bf16[4,2,5,5,32,128]{5,4,3,2,1,0:T(8,128)(2,1)S(1)} %reorder_kernel.3.lower_ref, bf16[4,2,5,5,32,128]{5,4,3,2,1,0:T(8,128)(2,1)S(1)} %reorder_kernel.4.upper_ref, f32[4,2,2,5,32,128]{5,4,3,2,1,0:T(8,128)S(1)} %get-tuple-element.53.source_ref, ...), custom_call_target="tpu_custom_call", output_to_operand_aliasing={{}: (5, {})} | custom-call | bytes 24000 | tf_op jit(solution)/shard_map/answer_kernel/pallas_call | solution.py:798
  (61 shorter events, 7.4 us)
Async XLA Ops:
  0.0 1.3 %copy-start.5 = (bf16[2,5,4,32,4,128]{5,4,3,2,1,0:T(4,128)(2,1)S(1)}, bf16[2,5,4,32,4,128]{5,4,3,2,1,0:T(4,128)(2,1)}, u32[]{:S(2)}) copy-start(bf16[2,5,4,32,4,128]{5,4,3,2,1,0:T(4,128)(2,1)} %param.5) | copy-start | bytes 3932164
  3.3 6.7 %copy-start = (bf16[41,32,128]{2,1,0:T(8,128)(2,1)}, bf16[41,32,128]{2,1,0:T(8,128)(2,1)S(1)}, u32[]{:S(2)}) copy-start(bf16[41,32,128]{2,1,0:T(8,128)(2,1)S(1)} %get-tuple-element.42.after_ref.refs_0_) | copy-start | bytes 1007620
  3.3 20.6 %collective-permute-start = (bf16[41,32,128]{2,1,0:T(8,128)(2,1)}, bf16[41,32,128]{2,1,0:T(8,128)(2,1)}, u32[]{:S(2)}, u32[]{:S(2)}) collective-permute-start(bf16[41,32,128]{2,1,0:T(8,128)(2,1)} %get-tuple-element.45), channel_id=1, source_target_pairs={{0,8},{8,0},{16,24},{24,16},{1,9},{9,1},{17,25},{25,17},{2,10},{10... | collective-permute-start | bytes 1007624 | tf_op jit(solution)/shard_map/forcing1/ppermute | solution.py:657
  5.3 18.6 %collective-permute-start.1 = (bf16[41,32,128]{2,1,0:T(8,128)(2,1)}, bf16[41,32,128]{2,1,0:T(8,128)(2,1)}, u32[]{:S(2)}, u32[]{:S(2)}) collective-permute-start(bf16[41,32,128]{2,1,0:T(8,128)(2,1)} %get-tuple-element.46), channel_id=1, source_target_pairs={{0,16},{8,24},{16,0},{24,8},{1,17},{9,25},{17,1},{25,9},{2,18},{10... | collective-permute-start | bytes 1007624 | tf_op jit(solution)/shard_map/forcing2/ppermute | solution.py:657
  6.5 17.4 %collective-permute-start.2 = (bf16[41,32,128]{2,1,0:T(8,128)(2,1)}, bf16[41,32,128]{2,1,0:T(8,128)(2,1)}, u32[]{:S(2)}, u32[]{:S(2)}) collective-permute-start(bf16[41,32,128]{2,1,0:T(8,128)(2,1)} %get-tuple-element.47), channel_id=1, source_target_pairs={{0,24},{8,16},{16,8},{24,0},{1,25},{9,17},{17,9},{25,1},{2,26},{10... | collective-permute-start | bytes 1007624 | tf_op jit(solution)/shard_map/forcing3/ppermute | solution.py:657
  6.6 1.4 %copy-start.2 = (bf16[2,5,5,32,4,128]{5,4,3,2,1,0:T(4,128)(2,1)S(1)}, bf16[2,5,5,32,4,128]{5,4,3,2,1,0:T(4,128)(2,1)}, u32[]{:S(2)}) copy-start(bf16[2,5,5,32,4,128]{5,4,3,2,1,0:T(4,128)(2,1)} %param.9) | copy-start | bytes 4915204
  8.0 2.0 %copy-start.3 = (bf16[2,5,5,32,4,128]{5,4,3,2,1,0:T(4,128)(2,1)S(1)}, bf16[2,5,5,32,4,128]{5,4,3,2,1,0:T(4,128)(2,1)}, u32[]{:S(2)}) copy-start(bf16[2,5,5,32,4,128]{5,4,3,2,1,0:T(4,128)(2,1)} %param.8) | copy-start | bytes 4915204
  12.0 9.4 %copy-start.8 = (f32[2,5,128]{2,0,1:T(2,128)S(1)}, f32[2,5,128]{2,0,1:T(2,128)}, u32[]{:S(2)}) copy-start(f32[2,5,128]{2,0,1:T(2,128)} %param.6) | copy-start | bytes 15364
  19.0 1.1 %copy-start.6 = (f32[3,2,5,5,16,128]{5,4,3,2,1,0:T(8,128)}, f32[3,2,5,5,16,128]{5,4,3,2,1,0:T(8,128)S(1)}, u32[]{:S(2)}) copy-start(f32[3,2,5,5,16,128]{5,4,3,2,1,0:T(8,128)S(1)} %get-tuple-element.54.keep_ref) | copy-start | bytes 3686404
  20.1 16.6 %collective-permute-start.6 = (f32[3,2,5,5,16,128]{5,4,3,2,1,0:T(8,128)}, f32[3,2,5,5,16,128]{5,4,3,2,1,0:T(8,128)}, u32[]{:S(2)}, u32[]{:S(2)}) collective-permute-start(f32[3,2,5,5,16,128]{5,4,3,2,1,0:T(8,128)} %get-tuple-element.55), channel_id=1, source_target_pairs={{0,1},{1,0},{2,3},{3,2},{4,5},{5,4},{6,7},{7,6},{8,9},{9,8},{10,11... | collective-permute-start | bytes 3686408 | tf_op jit(solution)/shard_map/matrices_core/ppermute | solution.py:657
  23.7 1.0 %copy-start.1 = (bf16[41,32,128]{2,1,0:T(8,128)(2,1)S(1)}, bf16[41,32,128]{2,1,0:T(8,128)(2,1)}, u32[]{:S(2)}) copy-start(bf16[41,32,128]{2,1,0:T(8,128)(2,1)} %copy-done) | copy-start | bytes 1007620
  26.8 9.8 %collective-permute-start.3 = (f16[4,2,5,32,128]{4,3,2,1,0:T(8,128)(2,1)S(1)}, f16[4,2,5,32,128]{4,3,2,1,0:T(8,128)(2,1)S(1)}, u32[]{:S(2)}, u32[]{:S(2)}) collective-permute-start(f16[4,2,5,32,128]{4,3,2,1,0:T(8,128)(2,1)S(1)} %convert_element_type.39), channel_id=1, source_target_pairs={{0,8},{8,0},{16,24},{24,16},{1,9},{9,1},{17,25},{25,17},{2,10},{10... | collective-permute-start | bytes 983048 | tf_op jit(solution)/shard_map/driving1/ppermute | solution.py:657
  28.6 8.1 %copy-start.7 = (f32[3,2,5,5,16,128]{5,4,3,2,1,0:T(8,128)S(1)}, f32[3,2,5,5,16,128]{5,4,3,2,1,0:T(8,128)}, u32[]{:S(2)}) copy-start(f32[3,2,5,5,16,128]{5,4,3,2,1,0:T(8,128)} %copy-done.6) | copy-start | bytes 3686404
  28.7 16.1 %collective-permute-start.5 = (f16[4,2,5,32,128]{4,3,2,1,0:T(8,128)(2,1)S(1)}, f16[4,2,5,32,128]{4,3,2,1,0:T(8,128)(2,1)S(1)}, u32[]{:S(2)}, u32[]{:S(2)}) collective-permute-start(f16[4,2,5,32,128]{4,3,2,1,0:T(8,128)(2,1)S(1)} %convert_element_type.43), channel_id=1, source_target_pairs={{0,24},{8,16},{16,8},{24,0},{1,25},{9,17},{17,9},{25,1},{2,26},{10... | collective-permute-start | bytes 983048 | tf_op jit(solution)/shard_map/driving3/ppermute | solution.py:657
  30.0 15.8 %collective-permute-start.4 = (f16[4,2,5,32,128]{4,3,2,1,0:T(8,128)(2,1)S(1)}, f16[4,2,5,32,128]{4,3,2,1,0:T(8,128)(2,1)S(1)}, u32[]{:S(2)}, u32[]{:S(2)}) collective-permute-start(f16[4,2,5,32,128]{4,3,2,1,0:T(8,128)(2,1)S(1)} %convert_element_type.41), channel_id=1, source_target_pairs={{0,16},{8,24},{16,0},{24,8},{1,17},{9,25},{17,1},{25,9},{2,18},{10... | collective-permute-start | bytes 983048 | tf_op jit(solution)/shard_map/driving2/ppermute | solution.py:657
  36.7 4.4 %copy-start.4 = (bf16[2,5,5,32,4,128]{5,4,3,2,1,0:T(4,128)(2,1)S(1)}, bf16[2,5,5,32,4,128]{5,4,3,2,1,0:T(4,128)(2,1)}, u32[]{:S(2)}) copy-start(bf16[2,5,5,32,4,128]{5,4,3,2,1,0:T(4,128)(2,1)} %param.7) | copy-start | bytes 4915204
  39.6 13.9 %collective-permute-start.8 = (f32[2,5,5,16,128]{4,3,2,1,0:T(8,128)S(1)}, f32[2,5,5,16,128]{4,3,2,1,0:T(8,128)S(1)}, u32[]{:S(2)}, u32[]{:S(2)}) collective-permute-start(f32[2,5,5,16,128]{4,3,2,1,0:T(8,128)S(1)} %slice_bitcast_fusion), channel_id=1, source_target_pairs={{0,2},{1,3},{2,0},{3,1},{4,6},{5,7},{6,4},{7,5},{8,10},{9,11},{10,... | collective-permute-start | bytes 1228808 | tf_op jit(solution)/shard_map/matrices_outward/ppermute | solution.py:722
  48.7 4.3 %collective-permute-start.9 = (f32[2,2,2,5,16,128]{5,4,3,2,1,0:T(8,128)S(1)}, f32[2,2,2,5,16,128]{5,4,3,2,1,0:T(8,128)S(1)}, u32[]{:S(2)}, u32[]{:S(2)}) collective-permute-start(f32[2,2,2,5,16,128]{5,4,3,2,1,0:T(8,128)S(1)} %get-tuple-element.63), channel_id=1, source_target_pairs={{0,1},{1,0},{2,3},{3,2},{4,5},{5,4},{6,7},{7,6},{8,9},{9,8},{10,11... | collective-permute-start | bytes 983048 | tf_op jit(solution)/shard_map/chunk0_core/ppermute | solution.py:657
  52.9 3.9 %collective-permute-start.7 = (f32[2,2,2,5,16,128]{5,4,3,2,1,0:T(8,128)S(1)}, f32[2,2,2,5,16,128]{5,4,3,2,1,0:T(8,128)S(1)}, u32[]{:S(2)}, u32[]{:S(2)}) collective-permute-start(f32[2,2,2,5,16,128]{5,4,3,2,1,0:T(8,128)S(1)} %get-tuple-element.59), channel_id=1, source_target_pairs={{0,1},{1,0},{2,3},{3,2},{4,5},{5,4},{6,7},{7,6},{8,9},{9,8},{10,11... | collective-permute-start | bytes 983048 | tf_op jit(solution)/shard_map/chunk1_core/ppermute | solution.py:657
  53.5 12.0 %collective-permute-start.10 = (f32[2,5,5,16,128]{4,3,2,1,0:T(8,128)S(1)}, f32[2,5,5,16,128]{4,3,2,1,0:T(8,128)S(1)}, u32[]{:S(2)}, u32[]{:S(2)}) collective-permute-start(f32[2,5,5,16,128]{4,3,2,1,0:T(8,128)S(1)} %upper_half_kernel.1), channel_id=1, source_target_pairs={{0,1},{1,0},{2,4},{4,2},{3,5},{5,3},{6,7},{7,6},{8,9},{9,8},{10,12... | collective-permute-start | bytes 1228808 | tf_op jit(solution)/shard_map/matrices_inward/ppermute | solution.py:758
  54.1 6.5 %collective-permute-start.15 = (f32[2,2,5,16,128]{4,3,2,1,0:T(8,128)S(1)}, f32[2,2,5,16,128]{4,3,2,1,0:T(8,128)S(1)}, u32[]{:S(2)}, u32[]{:S(2)}) collective-permute-start(f32[2,2,5,16,128]{4,3,2,1,0:T(8,128)S(1)} %get-tuple-element.64), channel_id=1, source_target_pairs={{0,2},{1,3},{2,0},{3,1},{4,6},{5,7},{6,4},{7,5},{8,10},{9,11},{10,... | collective-permute-start | bytes 491528 | tf_op jit(solution)/shard_map/chunk0_to_middle/ppermute | solution.py:761
  57.2 6.9 %collective-permute-start.11 = (f32[2,2,5,16,128]{4,3,2,1,0:T(8,128)S(1)}, f32[2,2,5,16,128]{4,3,2,1,0:T(8,128)S(1)}, u32[]{:S(2)}, u32[]{:S(2)}) collective-permute-start(f32[2,2,5,16,128]{4,3,2,1,0:T(8,128)S(1)} %get-tuple-element.67), channel_id=1, source_target_pairs={{0,2},{1,3},{2,0},{3,1},{4,6},{5,7},{6,4},{7,5},{8,10},{9,11},{10,... | collective-permute-start | bytes 491528 | tf_op jit(solution)/shard_map/chunk1_to_middle/ppermute | solution.py:761
  60.8 4.7 %collective-permute-start.16 = (f32[2,2,5,16,128]{4,3,2,1,0:T(8,128)S(1)}, f32[2,2,5,16,128]{4,3,2,1,0:T(8,128)S(1)}, u32[]{:S(2)}, u32[]{:S(2)}) collective-permute-start(f32[2,2,5,16,128]{4,3,2,1,0:T(8,128)S(1)} %halves_kernel.3.mine_ref), channel_id=1, source_target_pairs={{0,1},{1,0},{2,4},{4,2},{3,5},{5,3},{6,7},{7,6},{8,9},{9,8},{10,12... | collective-permute-start | bytes 491528 | tf_op jit(solution)/shard_map/chunk0_middle/ppermute | solution.py:769
  64.1 5.2 %collective-permute-start.12 = (f32[2,2,5,16,128]{4,3,2,1,0:T(8,128)S(1)}, f32[2,2,5,16,128]{4,3,2,1,0:T(8,128)S(1)}, u32[]{:S(2)}, u32[]{:S(2)}) collective-permute-start(f32[2,2,5,16,128]{4,3,2,1,0:T(8,128)S(1)} %halves_kernel.2.mine_ref), channel_id=1, source_target_pairs={{0,1},{1,0},{2,4},{4,2},{3,5},{5,3},{6,7},{7,6},{8,9},{9,8},{10,12... | collective-permute-start | bytes 491528 | tf_op jit(solution)/shard_map/chunk1_middle/ppermute | solution.py:769
  65.6 7.3 %collective-permute-start.17 = (f32[2,2,5,16,128]{4,3,2,1,0:T(8,128)S(1)}, f32[2,2,5,16,128]{4,3,2,1,0:T(8,128)S(1)}, u32[]{:S(2)}, u32[]{:S(2)}) collective-permute-start(f32[2,2,5,16,128]{4,3,2,1,0:T(8,128)S(1)} %get-tuple-element.76), channel_id=1, source_target_pairs={{0,2},{1,3},{2,0},{3,1},{4,6},{5,7},{6,4},{7,5},{8,10},{9,11},{10,... | collective-permute-start | bytes 491528 | tf_op jit(solution)/shard_map/chunk0_to_ends/ppermute | solution.py:777
  69.4 9.1 %collective-permute-start.13 = (f32[2,2,5,16,128]{4,3,2,1,0:T(8,128)S(1)}, f32[2,2,5,16,128]{4,3,2,1,0:T(8,128)S(1)}, u32[]{:S(2)}, u32[]{:S(2)}) collective-permute-start(f32[2,2,5,16,128]{4,3,2,1,0:T(8,128)S(1)} %get-tuple-element.69), channel_id=1, source_target_pairs={{0,2},{1,3},{2,0},{3,1},{4,6},{5,7},{6,4},{7,5},{8,10},{9,11},{10,... | collective-permute-start | bytes 491528 | tf_op jit(solution)/shard_map/chunk1_to_ends/ppermute | solution.py:777
  73.3 7.0 %collective-permute-start.18 = (f32[2,2,2,5,16,128]{5,4,3,2,1,0:T(8,128)S(1)}, f32[2,2,2,5,16,128]{5,4,3,2,1,0:T(8,128)S(1)}, u32[]{:S(2)}, u32[]{:S(2)}) collective-permute-start(f32[2,2,2,5,16,128]{5,4,3,2,1,0:T(8,128)S(1)} %get-tuple-element.78), channel_id=1, source_target_pairs={{0,1},{1,0},{2,3},{3,2},{4,5},{5,4},{6,7},{7,6},{8,9},{9,8},{10,11... | collective-permute-start | bytes 983048 | tf_op jit(solution)/shard_map/chunk0_apart/ppermute | solution.py:657
  78.9 4.4 %collective-permute-start.14 = (f32[2,2,2,5,16,128]{5,4,3,2,1,0:T(8,128)S(1)}, f32[2,2,2,5,16,128]{5,4,3,2,1,0:T(8,128)S(1)}, u32[]{:S(2)}, u32[]{:S(2)}) collective-permute-start(f32[2,2,2,5,16,128]{5,4,3,2,1,0:T(8,128)S(1)} %get-tuple-element.71), channel_id=1, source_target_pairs={{0,1},{1,0},{2,3},{3,2},{4,5},{5,4},{6,7},{7,6},{8,9},{9,8},{10,11... | collective-permute-start | bytes 983048 | tf_op jit(solution)/shard_map/chunk1_apart/ppermute | solution.py:657

commit v3 on v2

--- a/solution.py
+++ b/solution.py
@@ -9,8 +9,8 @@
 from jax.sharding import PartitionSpec as P
 
 exact_mode = lax.Precision.HIGHEST
-VMEM_LIMIT = 44 * 1024 * 1024
-BYTES_PER_MICRO = 10_000
+VMEM_LIMIT = 24 * 1024 * 1024
+BYTES_PER_MICRO = 3_600_000
 CHUNKS = ((0, 1), (2, 3))
 
 
@@ -31,6 +31,10 @@
 
 def vmem():
     return pl.BlockSpec(memory_space=pltpu.VMEM)
+
+
+def anywhere():
+    return pl.BlockSpec(memory_space=pl.ANY)
 
 
 def f32(*shape):
@@ -94,7 +98,7 @@
     return jnp.where(of == wanted, 1.0, 0.0).astype(jnp.bfloat16)
 
 
-def repack_kernel(rows, groups, forcing_ref, *out_refs):
+def repack_kernel(rows, groups, forcing_ref, mark_ref, *out_refs):
     fields, columns = forcing_ref.shape[1:3]
     points = forcing_ref.shape[3] // rows
     each = columns // groups
@@ -122,13 +126,55 @@
                                 j * points : (j + 1) * points, side * 128 : (side + 1) * 128
                             ]
     peak = jnp.max(peak)
+    mark_ref[...] = jnp.zeros_like(mark_ref)
     for ref in out_refs:
         ref[each * 2 * fields] = jnp.full(ref.shape[1:], peak, jnp.float32).astype(jnp.bfloat16)
 
 
-def filter_kernel(sources, kernel_ref, *refs):
+def table_kernel(own, factor_ref, after_ref, out_ref):
+    fields, count = factor_ref.shape[1:]
+    at = lax.axis_index("span")
+    scale = 2.0 * math.pi / count
+
+    def grid(shape, dimension):
+        return lax.broadcasted_iota(jnp.int32, shape, dimension)
+
+    def point(slot):
+        return (at ^ (slot // own)) * own + slot % own
+
+    wide = (count, 2 * count)
+    column = grid(wide, 1)
+    source = point((column // (2 * own)) * own + column % own)
+    turn = (column // own) % 2 * (count // 4)
+    steps = (grid(wide, 0) * source + count - turn) % count
+    angle = steps.astype(jnp.float32) * scale
+    right = jnp.concatenate([jnp.cos(angle), jnp.sin(angle)], axis=0)
+    square = (count, count)
+    angle = (point(grid(square, 0)) * grid(square, 1) % count).astype(jnp.float32) * scale
+    cosine, sine = jnp.cos(angle) / count, jnp.sin(angle) / count
+    for i in range(fields):
+        factor_re, factor_im = factor_ref[0, i : i + 1], factor_ref[1, i : i + 1]
+        left_re = factor_re * cosine - factor_im * sine
+        left_im = factor_re * sine + factor_im * cosine
+        for part, left in enumerate(([left_re, left_im], [left_im, -left_re])):
+            whole = jnp.dot(
+                jnp.concatenate(left, axis=1),
+                right,
+                precision=exact_mode,
+                preferred_element_type=jnp.float32,
+            )
+            high = whole.astype(jnp.bfloat16)
+            low = (whole - high.astype(jnp.float32)).astype(jnp.bfloat16)
+            for m in range(count // own):
+                base = (4 * m + part) * own
+                rows = slice(m * own, (m + 1) * own)
+                out_ref[i, base : base + own] = high[rows]
+                out_ref[i, base + 2 * own : base + 3 * own] = low[rows]
+
+
+def filter_kernel(sources, chunks, kernel_ref, *refs):
     arrived, scale_ref, outs = refs[:sources], refs[sources], refs[sources + 1 :]
-    each, fields, points = outs[0].shape[0], outs[0].shape[2], outs[0].shape[3]
+    each, fields, points = outs[0].shape[0] * chunks, outs[0].shape[2], outs[0].shape[3]
     last = arrived[0].shape[0] - 1
     peak = arrived[0][last].astype(jnp.float32)
     for m in range(1, sources):
@@ -160,7 +206,7 @@
             ) * scale
             for t in range(each):
                 for r in range(2):
-                    outs[m][t, r, i] = total[
+                    outs[t * chunks // each * sources + m][t % (each // chunks), r, i] = total[
                         r * points : (r + 1) * points, t * 128 : (t + 1) * 128
                     ]
 
@@ -184,10 +230,11 @@
     lax.fori_loop(0, 2 * size, move, 0)
 
 
-def summary_kernel(rows, lower_ref, upper_ref, keep_ref, send_ref, held_ref):
+def summary_kernel(rows, lower_ref, upper_ref, mark_ref, keep_ref, send_ref, held_ref):
     size = lower_ref.shape[2]
     half = lower_ref.shape[4] // 2
     core = lax.axis_index("wall") % 2
+    mark_ref[...] = jnp.zeros_like(mark_ref)
 
     def summarize(part, chosen):
         span = pl.ds(part * half, half)
@@ -251,7 +298,7 @@
     lax.fori_loop(0, 2, half_of, 0)
 
 
-def pair_matrices_kernel(keep_ref, other_ref, pair_ref, chip_ref, joint_ref):
+def pair_matrices_kernel(after_ref, keep_ref, other_ref, pair_ref, chip_ref, joint_ref):
     core = lax.axis_index("wall") % 2
     size = keep_ref.shape[2]
     for which in range(3):
@@ -281,7 +328,8 @@
     lax.fori_loop(0, size, column, 0)
 
 
-def upper_half_kernel(chip_ref, beside_ref, out_ref):
+def upper_half_kernel(*refs):
+    chip_ref, beside_ref, out_ref = refs[-3:]
     size = chip_ref.shape[2]
 
     chip = lax.axis_index("wall") // 2
@@ -305,7 +353,7 @@
 
 
 def local_kernel(
-    columns, first, spans, rows, pivot_ref, lower_ref, upper_ref, scale_ref, *refs
+    columns, spans, rows, pivot_ref, lower_ref, upper_ref, scale_ref, *refs
 ):
     arrived = refs[:spans]
     source_ref, keep_ref, send_ref, driving_ref, sweep_ref = refs[spans:]
@@ -319,7 +367,7 @@
         y = (m // groups) ^ (at // groups)
         for t in range(columns // groups):
             c = t * groups + ((m % groups) ^ (at % groups)) if groups > 1 else t
-            driving_ref[y, c] = arrived[m][first // groups + t] * scale
+            driving_ref[y, c] = arrived[m][t] * scale
     core = lax.axis_index("wall") % 2
 
     def solve(part, carry):
@@ -542,7 +590,10 @@
 def answer_kernel(
     columns, first, rows, lower_ref, upper_ref, source_ref, keep_ref, other_ref, *refs
 ):
-    out_ref, sweep_ref, edge_ref, made_ref, done = refs[-5:]
+    sweep_ref, edge_ref = refs[-2:]
+    last = first is not None
+    earlier = refs[: len(refs) - 5] if last else ()
+    out_ref, made_ref, done = refs[len(earlier) : -2] if last else (None, refs[0], None)
     core = lax.axis_index("wall") % 2
     size = lower_ref.shape[2]
     points = lower_ref.shape[4]
@@ -550,18 +601,30 @@
     edge_ref[core] = keep_ref[...]
     edge_ref[1 - core] = other_ref[...]
 
-    def copies(part):
+    def copies(place, part, ref):
         return [
             pltpu.make_async_copy(
-                made_ref.at[part, r, i],
+                ref.at[part, r, i],
                 out_ref.at[
-                    r, i, pl.ds(first, columns), pl.ds(part * half * rows, half * rows)
+                    r,
+                    i,
+                    pl.ds(place * columns, columns),
+                    pl.ds(part * half * rows, half * rows),
                 ],
-                done.at[part, r, i],
+                done.at[place, part, r, i],
             )
             for r in range(2)
             for i in range(size)
         ]
+
+    started = [
+        copy
+        for place, ref in enumerate(earlier)
+        for part in range(2)
+        for copy in copies(place, part, ref)
+    ]
+    for copy in started:
+        copy.start()
 
     def run(part, carry):
         span = pl.ds(part * half, half)
@@ -585,49 +648,16 @@
                 for r in range(2):
                     for i in range(size):
                         made_ref[part, r, i, c, place] = states[c][r][i]
-        for copy in copies(part):
-            copy.start()
+        if last:
+            for copy in copies(len(earlier), part, made_ref):
+                copy.start()
         return carry
 
     lax.fori_loop(0, 2, run, 0)
-    for copy in copies(0) + copies(1):
-        copy.wait()
-
-
-def span_kernel(span_factor, own, span_at):
-    count = span_factor.shape[2]
-    fields = span_factor.shape[1]
-    slot = jnp.arange(count, dtype=jnp.int32)
-    points = (span_at ^ (slot // own)) * own + slot % own
-    modes = jnp.arange(count, dtype=jnp.int32)
-    scale = 2.0 * math.pi / count
-    angle_points = (points[:, None] * modes[None, :] % count).astype(jnp.float32) * scale
-    cos_points = jnp.cos(angle_points)[None]
-    sin_points = jnp.sin(angle_points)[None]
-    factor_re = span_factor[0][:, None, :] / count
-    factor_im = span_factor[1][:, None, :] / count
-    left_re = factor_re * cos_points - factor_im * sin_points
-    left_im = factor_re * sin_points + factor_im * cos_points
-    spans = count // own
-    left = jnp.stack(
-        [
-            jnp.concatenate([left_re, left_im], axis=2).reshape(fields, spans, own, 2 * count),
-            jnp.concatenate([left_im, -left_re], axis=2).reshape(fields, spans, own, 2 * count),
-        ],
-        axis=2,
-    ).reshape(fields * 2 * count, 2 * count)
-    quarter = count // 4
-    column = jnp.arange(2 * count, dtype=jnp.int32)
-    place = (span_at ^ (column // (2 * own))) * own + column % own
-    turn = (column // own) % 2 * quarter
-    steps = (modes[:, None] * place[None, :] + (count - turn)[None, :]) % count
-    angle = steps.astype(jnp.float32) * scale
-    right = jnp.concatenate([jnp.cos(angle), jnp.sin(angle)], axis=0)
-    whole = jnp.dot(left, right, precision=exact_mode).reshape(fields, spans, 2 * own, -1)
-    high = lax.reduce_precision(whole, 8, 7)
-    low = whole - high
-    both = jnp.concatenate([high, low], axis=2).astype(jnp.bfloat16)
-    return both.reshape(fields, 4 * count, -1)
+    if last:
+        started += copies(len(earlier), 0, made_ref) + copies(len(earlier), 1, made_ref)
+        for copy in started:
+            copy.wait()
 
 
 def affine(matrix, vector, offset):
@@ -643,7 +673,6 @@
     spans, walls = lax.axis_size("span"), lax.axis_size("wall")
     chips = walls // 2
     half = points // 2
-    span_at = lax.axis_index("span")
 
     flat = (points * rows, width)
     forcing = forcing.reshape(forcing.shape[:3] + flat)
@@ -660,11 +689,11 @@
         return lax.optimization_barrier((array,) + earlier)[0]
 
     groups = spans // rows
-    kernel = span_kernel(span_factor, points, span_at)
     block = (columns // groups * 2 * fields + 1, points, width)
-    sent = call(
+    mark = f32(8, width)
+    repacked, *sent = call(
         functools.partial(repack_kernel, rows, groups),
-        [jax.ShapeDtypeStruct(block, jnp.bfloat16)] * spans,
+        [mark] + [jax.ShapeDtypeStruct(block, jnp.bfloat16)] * spans,
         micros=2.0,
         in_specs=[vmem()],
     )(forcing)
@@ -681,29 +710,46 @@
             functools.partial(reorder_kernel, rows),
             moved_shape,
             micros=2.0,
-            in_specs=[vmem(), pl.BlockSpec(memory_space=pl.ANY)],
+            in_specs=[vmem(), anywhere()],
         )(matrix, after)
 
-    lowers, uppers = reorder(step_lower, sent[0]), reorder(step_upper, sent[0])
-    keep, send = call(
+    lowers, uppers = reorder(step_lower, repacked), reorder(step_upper, repacked)
+    summarized, keep, send = call(
         functools.partial(summary_kernel, rows),
-        [summary] * 2,
-            micros=8.2,
+        [mark] + [summary] * 2,
+            micros=6.0,
         scratch=[pltpu.VMEM((rows, 2, 2, fields) + plane, jnp.float32)],
         in_specs=[vmem()] * 2,
     )(lowers, uppers)
+    kernel = call(
+        functools.partial(table_kernel, points),
+        jax.ShapeDtypeStruct((fields, 4 * spans * points, 2 * spans * points), jnp.bfloat16),
+        micros=2.0,
+        in_specs=[vmem(), anywhere()],
+    )(span_factor, summarized)
     scale, *outs = call(
-        functools.partial(filter_kernel, spans),
-        [f32(8, 128)] + [f32(columns // groups, 2, fields, points, width)] * spans,
+        functools.partial(filter_kernel, spans, len(CHUNKS)),
+        [f32(8, 128)]
+        + [f32(columns // len(CHUNKS) // groups, 2, fields, points, width)]
+        * (spans * len(CHUNKS)),
         micros=1.0,
-    )(gate(kernel, keep), *sent)
-    drivings = [outs[0]] + [
-        swap(outs[m].astype(jnp.float16), m, "span", f"driving{m}").astype(jnp.float32)
-        for m in range(1, spans)
-    ]
-
-    pivots = reorder(pivot_inverse, outs[0])
-    other = swap(send, 1, "wall", "matrices_core")
+        in_specs=[vmem()] * (1 + spans),
+    )(kernel, *sent)
+    drivings = []
+    for number in range(len(CHUNKS)):
+        own = outs[number * spans : (number + 1) * spans]
+        drivings.append(
+            [own[0]]
+            + [
+                swap(
+                    own[m].astype(jnp.float16), m, "span", f"chunk{number}_driving{m}"
+                ).astype(jnp.float32)
+                for m in range(1, spans)
+            ]
+        )
+
+    pivots = reorder(pivot_inverse, scale)
+    other = swap(gate(send, scale), 1, "wall", "matrices_core")
     pair, chip_matrices, joint = call(
         pair_matrices_kernel,
         [
@@ -711,9 +757,9 @@
             summary,
             f32(2, fields, fields, *plane),
         ],
-            micros=3.6,
-        in_specs=[vmem()] * 2,
-    )(gate(keep, drivings[1]), other)
+            micros=1.4,
+        in_specs=[anywhere()] + [vmem()] * 2,
+    )(scale, keep, other)
     tree = chips == 4
     outward = [(i, i ^ 2) for i in range(walls)]
     inward = [(0, 1), (1, 0), (2, 4), (4, 2), (3, 5), (5, 3), (6, 7), (7, 6)]
@@ -721,17 +767,17 @@
         with jax.named_scope("matrices_outward"):
             beside = lax.ppermute(chip_matrices[2], "wall", outward)
 
-    out = None
+    began, finished = [], []
     for number, chosen in enumerate(CHUNKS):
         count = len(chosen)
         vectors = f32(2, count, 2, fields, *plane)
         single = f32(count, 2, fields, *plane)
         size = 2 * fields * count * half * width
-        taken = drivings
+        taken = drivings[number]
         source, keep, send = call(
-            functools.partial(local_kernel, count, chosen[0], spans, rows),
+            functools.partial(local_kernel, count, spans, rows),
             [f32(rows, count, 2, fields, points, width), vectors, vectors],
-            micros=2.2 * count,
+            micros=1.4 * count,
             scratch=[
                 pltpu.VMEM((rows, count, 2, fields, points, width), jnp.float32),
                 pltpu.VMEM((rows, count, 2, fields) + plane, jnp.float32),
@@ -742,27 +788,34 @@
         chip, inner, outgoing = call(
             functools.partial(pair_kernel, count, chips),
             [vectors, vectors, single],
-            micros=0.5 * count,
+            micros=0.25 * count,
             scratch=[pltpu.VMEM((2,) + vectors.shape, jnp.float32)],
             in_specs=[vmem()] * 3,
         )(pair, keep, other)
+        began.append((source, chip, inner, outgoing))
+
+    if tree:
+        upper_half = call(
+            upper_half_kernel,
+            f32(2, fields, fields, *plane),
+            micros=0.7,
+            in_specs=[vmem()] * 2,
+        )(chip_matrices, beside)
+        with jax.named_scope("matrices_inward"):
+            upper_half = lax.ppermute(upper_half, "wall", inward)
+    for number, chosen in enumerate(CHUNKS):
+        count = len(chosen)
+        vectors = f32(2, count, 2, fields, *plane)
+        single = f32(count, 2, fields, *plane)
+        source, chip, inner, outgoing = began[number]
         extra = ()
-        if tree and number == 0:
-            upper_half = call(
-                upper_half_kernel,
-                f32(2, fields, fields, *plane),
-                micros=0.7,
-                in_specs=[vmem()] * 2,
-            )(gate(chip_matrices, outgoing), beside)
-            with jax.named_scope("matrices_inward"):
-                upper_half = lax.ppermute(upper_half, "wall", inward)
         if tree:
             with jax.named_scope(f"chunk{number}_to_middle"):
                 came = lax.ppermute(outgoing, "wall", outward)
             mine = call(
                 functools.partial(halves_kernel, count),
                 single,
-            micros=0.3 * count,
+                micros=0.2 * count,
                 in_specs=[vmem()] * 4,
             )(chip_matrices, beside, chip, came)
             with jax.named_scope(f"chunk{number}_middle"):
@@ -770,7 +823,7 @@
             edge, outgoing = call(
                 functools.partial(middle_kernel, count),
                 [vectors, single],
-            micros=0.3 * count,
+                micros=0.2 * count,
                 in_specs=[vmem()] * 7,
             )(chip_matrices, beside, upper_half, chip, came, mine, across)
             with jax.named_scope(f"chunk{number}_to_ends"):
@@ -789,26 +842,33 @@
         keep, send = call(
             functools.partial(split_kernel, count, tree),
             [vectors, vectors],
-            micros=0.5 * count,
+            micros=0.25 * count,
             scratch=[pltpu.VMEM(vectors.shape, jnp.float32)],
             in_specs=[vmem()] * (4 + len(extra)),
         )(pair, joint, inner, edge, *extra)
         other = swap(send, 1, "wall", f"chunk{number}_apart")
-        held = () if out is None else (out,)
-        out = call(
-            functools.partial(answer_kernel, count, chosen[0], rows),
-            f32(2, fields, columns, *flat),
-            micros=1.2 * count,
-            scratch=[
-                pltpu.VMEM((rows, count, 2, fields) + plane, jnp.float32),
-                pltpu.VMEM((2,) + vectors.shape, jnp.float32),
-                pltpu.VMEM((2, 2, fields, count, half * rows, width), jnp.float32),
-                pltpu.SemaphoreType.DMA((2, 2, fields)),
-            ],
-            in_specs=[vmem()] * 5 + [pl.BlockSpec(memory_space=pl.ANY)] * len(held),
-            out_specs=pl.BlockSpec(memory_space=pl.ANY),
-            input_output_aliases={5: 0} if held else {},
-        )(lowers, uppers, source, keep, other, *held)
+        final = number == len(CHUNKS) - 1
+        made = (2, 2, fields, count, half * rows, width)
+        scratch = [
+            pltpu.VMEM((rows, count, 2, fields) + plane, jnp.float32),
+            pltpu.VMEM((2,) + vectors.shape, jnp.float32),
+        ]
+        if final:
+            scratch = [
+                pltpu.VMEM(made, jnp.float32),
+                pltpu.SemaphoreType.DMA((len(CHUNKS), 2, 2, fields)),
+            ] + scratch
+        finished.append(
+            call(
+                functools.partial(answer_kernel, count, chosen[0] if final else None, rows),
+                f32(2, fields, columns, *flat) if final else f32(*made),
+                micros=1.5 * count,
+                scratch=scratch,
+                in_specs=[vmem()] * (5 + (len(finished) if final else 0)),
+                out_specs=anywhere() if final else vmem(),
+            )(lowers, uppers, source, keep, other, *(finished if final else ()))
+        )
+    out = finished[-1]
     return out.reshape(2, fields, columns, points, rows, width)
 
 

time: 86.8 us -> 75.7 us (0.87)
  waiting for transfers between devices: 13.5 us -> 6.56 us
  starting transfers between devices: 31.5 us -> 35.2 us
  Pallas kernels: 33.6 us -> 30.2 us
  local copies, waits for them, and re-layouts: 4.69 us -> 2.79 us
  other arithmetic: 1.62 us -> 0.33 us
  matrix products: 1.19 us -> 0 us
    ppermute x11 -> x14, waiting for transfers between devices: 9.2 us -> 4.29 us  [swap(): return lax.ppermute(array, axis, [(i, i ^ distance) for i in range(count)])]
    ppermute x11 -> x14, starting transfers between devices: 15.8 us -> 18.7 us  [swap(): return lax.ppermute(array, axis, [(i, i ^ distance) for i in range(count)])]
    ppermute x2, starting transfers between devices: 3.73 us -> 6.24 us  [local(): across = lax.ppermute(mine, 'wall', inward)]
    ppermute x2, waiting for transfers between devices: 4.25 us -> 2.15 us  [local(): came = lax.ppermute(outgoing, 'wall', outward)]
    pallas_call x9 -> x10, Pallas kernels: 22.9 us -> 21 us  [the longest x1 6.05 us: local(): call(functools.partial(summary_kernel, rows), [mark] + [summary] * 2, mic...]
    unnamed x18 -> x11, local copies, waits for them, and re-layouts: 4.65 us -> 2.76 us
    ppermute x2, starting transfers between devices: 7.24 us -> 5.6 us  [local(): extra = (lax.ppermute(outgoing, 'wall', outward),)]
    pallas_call x1, Pallas kernels: 2.81 us -> 1.39 us  [local(): call(pair_matrices_kernel, [f32(2, *summary.shape), summary, f32(2, field...]
  transfers between devices with their start and end apart: 19 -> 22, of which waited for: 5 -> 5; matrix products, arithmetic and copies ran while one was open for 3% -> 0% of each run, Pallas kernels for 33% -> 33%
where the time goes in v3:
time: 75.7 us; the launch traced here: 75.6 us
  starting transfers between devices  35.2 us (46%)
  Pallas kernels  30.2 us (40%)
  waiting for transfers between devices  6.56 us (9%)
  local copies, waits for them, and re-layouts  2.79 us (4%)
    ppermute x14, starting transfers between devices, swap(): return lax.ppermute(array, axis, [(i, i ^ distance) for i in range(count)])  18.7 us
    ppermute x2, starting transfers between devices, local(): across = lax.ppermute(mine, 'wall', inward)  6.24 us
    pallas_call x1, Pallas kernels, local(): call(functools.partial(summary_kernel, rows), [mark] + [summary] * 2, mic...  6.05 us
    pallas_call x3, Pallas kernels, reorder(): call(functools.partial(reorder_kernel, rows), moved_shape, micros=2.0, in...  6 us
    ppermute x2, starting transfers between devices, local(): extra = (lax.ppermute(outgoing, 'wall', outward),)  5.6 us
    pallas_call x2, Pallas kernels, local(): call(functools.partial(local_kernel, count, spans, rows), [f32(rows, coun...  5.56 us
    pallas_call x2, Pallas kernels, local(): call(functools.partial(answer_kernel, count, chosen[0] if final else None...  5.38 us
    ppermute x14, waiting for transfers between devices, swap(): return lax.ppermute(array, axis, [(i, i ^ distance) for i in range(count)])  4.29 us
  transfers between devices with their start and end apart: 22, of which 5 were waited for; matrix products, arithmetic and copies ran while one was open for 0% of the time, Pallas kernels for 33%

profile of v3, /device:TPU:1, one launch (start us, length us, event | category | flops | bytes accessed | tf_op | source)
XLA Modules:
  0.0 75.6 jit_solution(15158715553039806226)
XLA Ops:
  0.0 1.3 %copy-done.3 = bf16[2,5,4,32,4,128]{5,4,3,2,1,0:T(4,128)(2,1)S(1)} copy-done((bf16[2,5,4,32,4,128]{5,4,3,2,1,0:T(4,128)(2,1)S(1)}, bf16[2,5,4,32,4,128]{5,4,3,2,1,0:T(4,128)(2,1)}, u32[]{:S(2)}) %copy-start.3) | copy-done | bytes 1310744
  1.3 1.0 %repack_kernel.1 = (f32[8,128]{1,0:T(8,128)S(1)}, bf16[41,32,128]{2,1,0:T(8,128)(2,1)S(1)}, bf16[41,32,128]{2,1,0:T(8,128)(2,1)S(1)}, bf16[41,32,128]{2,1,0:T(8,128)(2,1)S(1)}, bf16[41,32,128]{2,1,0:T(8,128)(2,1)S(1)}) custom-call(bf16[2,5,4,128,128]{4,3,2,1,0:T(8,128)(2,1)S(1)} %bitcast.10), custom_call_target="tpu_custom_call" | custom-call | bytes 7200000 | tf_op jit(solution)/shard_map/repack_kernel/pallas_call | solution.py:694
  2.3 2.1 %collective-permute-start = (bf16[41,32,128]{2,1,0:T(8,128)(2,1)S(1)}, bf16[41,32,128]{2,1,0:T(8,128)(2,1)S(1)}, u32[]{:S(2)}, u32[]{:S(2)}) collective-permute-start(bf16[41,32,128]{2,1,0:T(8,128)(2,1)S(1)} %get-tuple-element.49), channel_id=1, source_target_pairs={{0,8},{8,0},{16,24},{24,16},{1,9},{9,1},{17,25},{25,17},{2,10},{10... | collective-permute-start | bytes 1007624 | tf_op jit(solution)/shard_map/forcing1/ppermute | solution.py:686
  4.4 1.2 %collective-permute-start.1 = (bf16[41,32,128]{2,1,0:T(8,128)(2,1)S(1)}, bf16[41,32,128]{2,1,0:T(8,128)(2,1)S(1)}, u32[]{:S(2)}, u32[]{:S(2)}) collective-permute-start(bf16[41,32,128]{2,1,0:T(8,128)(2,1)S(1)} %get-tuple-element.50), channel_id=1, source_target_pairs={{0,16},{8,24},{16,0},{24,8},{1,17},{9,25},{17,1},{25,9},{2,18},{10... | collective-permute-start | bytes 1007624 | tf_op jit(solution)/shard_map/forcing2/ppermute | solution.py:686
  5.7 1.4 %copy-done = bf16[2,5,5,32,4,128]{5,4,3,2,1,0:T(4,128)(2,1)S(1)} copy-done((bf16[2,5,5,32,4,128]{5,4,3,2,1,0:T(4,128)(2,1)S(1)}, bf16[2,5,5,32,4,128]{5,4,3,2,1,0:T(4,128)(2,1)}, u32[]{:S(2)}) %copy-start) | copy-done | bytes 1638424
  7.1 2.0 %reorder_kernel.4.upper_ref = bf16[4,2,5,5,32,128]{5,4,3,2,1,0:T(8,128)(2,1)S(1)} custom-call(bf16[2,5,5,128,128]{4,3,2,1,0:T(8,128)(2,1)S(1)} %bitcast.7, f32[8,128]{1,0:T(8,128)S(1)} %get-tuple-element.46.after_ref), custom_call_target="tpu_custom_call" | custom-call | bytes 7200000 | tf_op jit(solution)/shard_map/reorder_kernel/pallas_call | solution.py:709
  9.1 2.0 %reorder_kernel.3.lower_ref = bf16[4,2,5,5,32,128]{5,4,3,2,1,0:T(8,128)(2,1)S(1)} custom-call(bf16[2,5,5,128,128]{4,3,2,1,0:T(8,128)(2,1)S(1)} %bitcast.8, f32[8,128]{1,0:T(8,128)S(1)} %get-tuple-element.46.after_ref), custom_call_target="tpu_custom_call" | custom-call | bytes 7200000 | tf_op jit(solution)/shard_map/reorder_kernel/pallas_call | solution.py:709
  11.1 6.0 %summary_kernel.1 = (f32[8,128]{1,0:T(8,128)S(1)}, f32[3,2,5,5,16,128]{5,4,3,2,1,0:T(8,128)S(1)}, f32[3,2,5,5,16,128]{5,4,3,2,1,0:T(8,128)S(1)}) custom-call(bf16[4,2,5,5,32,128]{5,4,3,2,1,0:T(8,128)(2,1)S(1)} %reorder_kernel.3.lower_ref, bf16[4,2,5,5,32,128]{5,4,3,2,1,0:T(8,128)(2,1)S(1)} %reorder_kernel.4.upper_ref), custom_call_target="tpu_custom_call" | custom-call | bytes 21600000 | tf_op jit(solution)/shard_map/summary_kernel/pallas_call | solution.py:717
  17.2 2.1 %table_kernel.1.kernel_ref = bf16[5,512,256]{2,1,0:T(8,128)(2,1)S(1)} custom-call(f32[2,5,128]{2,1,0:T(8,128)S(1)} %copy.6.factor_ref, f32[8,128]{1,0:T(8,128)S(1)} %get-tuple-element.47.after_ref), custom_call_target="tpu_custom_call" | custom-call | bytes 7200000 | tf_op jit(solution)/shard_map/table_kernel/pallas_call | solution.py:724
  21.0 1.8 %collective-permute-start.6 = (f32[3,2,5,5,16,128]{5,4,3,2,1,0:T(8,128)S(1)}, f32[3,2,5,5,16,128]{5,4,3,2,1,0:T(8,128)S(1)}, u32[]{:S(2)}, u32[]{:S(2)}) collective-permute-start(f32[3,2,5,5,16,128]{5,4,3,2,1,0:T(8,128)S(1)} %get-tuple-element.60), channel_id=1, source_target_pairs={{0,1},{1,0},{2,3},{3,2},{4,5},{5,4},{6,7},{7,6},{8,9},{9,8},{10,11... | collective-permute-start | bytes 3686408 | tf_op jit(solution)/shard_map/matrices_core/ppermute | solution.py:686
  22.9 1.4 %collective-permute-start.16 = (f16[2,2,5,32,128]{4,3,2,1,0:T(8,128)(2,1)S(1)}, f16[2,2,5,32,128]{4,3,2,1,0:T(8,128)(2,1)S(1)}, u32[]{:S(2)}, u32[]{:S(2)}) collective-permute-start(f16[2,2,5,32,128]{4,3,2,1,0:T(8,128)(2,1)S(1)} %convert_element_type.46), channel_id=1, source_target_pairs={{0,24},{8,16},{16,8},{24,0},{1,25},{9,17},{17,9},{25,1},{2,26},{10... | collective-permute-start | bytes 491528 | tf_op jit(solution)/shard_map/chunk0_driving3/ppermute | solution.py:686
  24.4 0.9 %collective-permute-start.15 = (f16[2,2,5,32,128]{4,3,2,1,0:T(8,128)(2,1)S(1)}, f16[2,2,5,32,128]{4,3,2,1,0:T(8,128)(2,1)S(1)}, u32[]{:S(2)}, u32[]{:S(2)}) collective-permute-start(f16[2,2,5,32,128]{4,3,2,1,0:T(8,128)(2,1)S(1)} %convert_element_type.44), channel_id=1, source_target_pairs={{0,16},{8,24},{16,0},{24,8},{1,17},{9,25},{17,1},{25,9},{2,18},{10... | collective-permute-start | bytes 491528 | tf_op jit(solution)/shard_map/chunk0_driving2/ppermute | solution.py:686
  25.8 1.3 %collective-permute-start.5 = (f16[2,2,5,32,128]{4,3,2,1,0:T(8,128)(2,1)S(1)}, f16[2,2,5,32,128]{4,3,2,1,0:T(8,128)(2,1)S(1)}, u32[]{:S(2)}, u32[]{:S(2)}) collective-permute-start(f16[2,2,5,32,128]{4,3,2,1,0:T(8,128)(2,1)S(1)} %convert_element_type.40), channel_id=1, source_target_pairs={{0,24},{8,16},{16,8},{24,0},{1,25},{9,17},{17,9},{25,1},{2,26},{10... | collective-permute-start | bytes 491528 | tf_op jit(solution)/shard_map/chunk1_driving3/ppermute | solution.py:686
  28.0 1.4 %pair_matrices_kernel.1 = (f32[2,3,2,5,5,16,128]{6,5,4,3,2,1,0:T(8,128)S(1)}, f32[3,2,5,5,16,128]{5,4,3,2,1,0:T(8,128)S(1)}, f32[2,5,5,16,128]{4,3,2,1,0:T(8,128)S(1)}) custom-call(f32[8,128]{1,0:T(8,128)S(1)} %get-tuple-element.52.after_ref.scale_ref, f32[3,2,5,5,16,128]{5,4,3,2,1,0:T(8,128)S(1)} %get-tuple-element.58.keep_ref, ...), custom_call_target="tpu_custom_call" | custom-call | bytes 5040000 | tf_op jit(solution)/shard_map/pair_matrices_kernel/pallas_call | solution.py:753
  29.7 1.0 %collective-permute-start.3 = (f16[2,2,5,32,128]{4,3,2,1,0:T(8,128)(2,1)S(1)}, f16[2,2,5,32,128]{4,3,2,1,0:T(8,128)(2,1)S(1)}, u32[]{:S(2)}, u32[]{:S(2)}) collective-permute-start(f16[2,2,5,32,128]{4,3,2,1,0:T(8,128)(2,1)S(1)} %convert_element_type.36), channel_id=1, source_target_pairs={{0,8},{8,0},{16,24},{24,16},{1,9},{9,1},{17,25},{25,17},{2,10},{10... | collective-permute-start | bytes 491528 | tf_op jit(solution)/shard_map/chunk1_driving1/ppermute | solution.py:686
  30.7 3.1 %collective-permute-done.15 = f16[2,2,5,32,128]{4,3,2,1,0:T(8,128)(2,1)S(1)} collective-permute-done((f16[2,2,5,32,128]{4,3,2,1,0:T(8,128)(2,1)S(1)}, f16[2,2,5,32,128]{4,3,2,1,0:T(8,128)(2,1)S(1)}, u32[]{:S(2)}, u32[]{:S(2)}) %collective-permute-start.15) | collective-permute-done | bytes 163872 | tf_op jit(solution)/shard_map/chunk0_driving2/ppermute | solution.py:686
  33.8 1.3 %collective-permute-start.8 = (f32[2,5,5,16,128]{4,3,2,1,0:T(8,128)S(1)}, f32[2,5,5,16,128]{4,3,2,1,0:T(8,128)S(1)}, u32[]{:S(2)}, u32[]{:S(2)}) collective-permute-start(f32[2,5,5,16,128]{4,3,2,1,0:T(8,128)S(1)} %slice_bitcast_fusion), channel_id=1, source_target_pairs={{0,2},{1,3},{2,0},{3,1},{4,6},{5,7},{6,4},{7,5},{8,10},{9,11},{10,... | collective-permute-start | bytes 1228808 | tf_op jit(solution)/shard_map/matrices_outward/ppermute | solution.py:768
  35.1 2.0 %reorder_kernel.5.pivot_ref = bf16[4,2,5,5,32,128]{5,4,3,2,1,0:T(8,128)(2,1)S(1)} custom-call(bf16[2,5,5,128,128]{4,3,2,1,0:T(8,128)(2,1)S(1)} %bitcast.9, f32[8,128]{1,0:T(8,128)S(1)} %get-tuple-element.52.after_ref.scale_ref), custom_call_target="tpu_custom_call" | custom-call | bytes 7200000 | tf_op jit(solution)/shard_map/reorder_kernel/pallas_call | solution.py:709
  37.2 2.8 %local_kernel.3 = (f32[4,2,2,5,32,128]{5,4,3,2,1,0:T(8,128)S(1)}, f32[2,2,2,5,16,128]{5,4,3,2,1,0:T(8,128)S(1)}, f32[2,2,2,5,16,128]{5,4,3,2,1,0:T(8,128)S(1)}) custom-call(bf16[4,2,5,5,32,128]{5,4,3,2,1,0:T(8,128)(2,1)S(1)} %reorder_kernel.5.pivot_ref, bf16[4,2,5,5,32,128]{5,4,3,2,1,0:T(8,128)(2,1)S(1)} %reorder_kernel.3.lower_ref, ...), custom_call_target="tpu_custom_call" | custom-call | bytes 10080000 | tf_op jit(solution)/shard_map/local_kernel/pallas_call | solution.py:777
  40.0 1.0 %collective-permute-start.17 = (f32[2,2,2,5,16,128]{5,4,3,2,1,0:T(8,128)S(1)}, f32[2,2,2,5,16,128]{5,4,3,2,1,0:T(8,128)S(1)}, u32[]{:S(2)}, u32[]{:S(2)}) collective-permute-start(f32[2,2,2,5,16,128]{5,4,3,2,1,0:T(8,128)S(1)} %get-tuple-element.79), channel_id=1, source_target_pairs={{0,1},{1,0},{2,3},{3,2},{4,5},{5,4},{6,7},{7,6},{8,9},{9,8},{10,11... | collective-permute-start | bytes 983048 | tf_op jit(solution)/shard_map/chunk0_core/ppermute | solution.py:686
  41.1 2.8 %local_kernel.2 = (f32[4,2,2,5,32,128]{5,4,3,2,1,0:T(8,128)S(1)}, f32[2,2,2,5,16,128]{5,4,3,2,1,0:T(8,128)S(1)}, f32[2,2,2,5,16,128]{5,4,3,2,1,0:T(8,128)S(1)}) custom-call(bf16[4,2,5,5,32,128]{5,4,3,2,1,0:T(8,128)(2,1)S(1)} %reorder_kernel.5.pivot_ref, bf16[4,2,5,5,32,128]{5,4,3,2,1,0:T(8,128)(2,1)S(1)} %reorder_kernel.3.lower_ref, ...), custom_call_target="tpu_custom_call" | custom-call | bytes 10080000 | tf_op jit(solution)/shard_map/local_kernel/pallas_call | solution.py:777
  44.2 1.6 %collective-permute-start.9 = (f32[2,5,5,16,128]{4,3,2,1,0:T(8,128)S(1)}, f32[2,5,5,16,128]{4,3,2,1,0:T(8,128)S(1)}, u32[]{:S(2)}, u32[]{:S(2)}) collective-permute-start(f32[2,5,5,16,128]{4,3,2,1,0:T(8,128)S(1)} %upper_half_kernel.1), channel_id=1, source_target_pairs={{0,1},{1,0},{2,4},{4,2},{3,5},{5,3},{6,7},{7,6},{8,9},{9,8},{10,12... | collective-permute-start | bytes 1228808 | tf_op jit(solution)/shard_map/matrices_inward/ppermute | solution.py:805
  46.2 1.7 %collective-permute-start.18 = (f32[2,2,5,16,128]{4,3,2,1,0:T(8,128)S(1)}, f32[2,2,5,16,128]{4,3,2,1,0:T(8,128)S(1)}, u32[]{:S(2)}, u32[]{:S(2)}) collective-permute-start(f32[2,2,5,16,128]{4,3,2,1,0:T(8,128)S(1)} %get-tuple-element.82), channel_id=1, source_target_pairs={{0,2},{1,3},{2,0},{3,1},{4,6},{5,7},{6,4},{7,5},{8,10},{9,11},{10,... | collective-permute-start | bytes 491528 | tf_op jit(solution)/shard_map/chunk0_to_middle/ppermute | solution.py:814
  48.5 2.1 %collective-permute-done.18.came_ref.first_ref = f32[2,2,5,16,128]{4,3,2,1,0:T(8,128)S(1)} collective-permute-done((f32[2,2,5,16,128]{4,3,2,1,0:T(8,128)S(1)}, f32[2,2,5,16,128]{4,3,2,1,0:T(8,128)S(1)}, u32[]{:S(2)}, u32[]{:S(2)}) %collective-permute-start.18) | collective-permute-done | bytes 163872 | tf_op jit(solution)/shard_map/chunk0_to_middle/ppermute | solution.py:814
  50.7 4.5 %collective-permute-start.19 = (f32[2,2,5,16,128]{4,3,2,1,0:T(8,128)S(1)}, f32[2,2,5,16,128]{4,3,2,1,0:T(8,128)S(1)}, u32[]{:S(2)}, u32[]{:S(2)}) collective-permute-start(f32[2,2,5,16,128]{4,3,2,1,0:T(8,128)S(1)} %halves_kernel.3.mine_ref), channel_id=1, source_target_pairs={{0,1},{1,0},{2,4},{4,2},{3,5},{5,3},{6,7},{7,6},{8,9},{9,8},{10,12... | collective-permute-start | bytes 491528 | tf_op jit(solution)/shard_map/chunk0_middle/ppermute | solution.py:822
  55.2 1.8 %collective-permute-start.11 = (f32[2,2,5,16,128]{4,3,2,1,0:T(8,128)S(1)}, f32[2,2,5,16,128]{4,3,2,1,0:T(8,128)S(1)}, u32[]{:S(2)}, u32[]{:S(2)}) collective-permute-start(f32[2,2,5,16,128]{4,3,2,1,0:T(8,128)S(1)} %halves_kernel.2.mine_ref), channel_id=1, source_target_pairs={{0,1},{1,0},{2,4},{4,2},{3,5},{5,3},{6,7},{7,6},{8,9},{9,8},{10,12... | collective-permute-start | bytes 491528 | tf_op jit(solution)/shard_map/chunk1_middle/ppermute | solution.py:822
  57.0 2.7 %collective-permute-start.20 = (f32[2,2,5,16,128]{4,3,2,1,0:T(8,128)S(1)}, f32[2,2,5,16,128]{4,3,2,1,0:T(8,128)S(1)}, u32[]{:S(2)}, u32[]{:S(2)}) collective-permute-start(f32[2,2,5,16,128]{4,3,2,1,0:T(8,128)S(1)} %get-tuple-element.84), channel_id=1, source_target_pairs={{0,2},{1,3},{2,0},{3,1},{4,6},{5,7},{6,4},{7,5},{8,10},{9,11},{10,... | collective-permute-start | bytes 491528 | tf_op jit(solution)/shard_map/chunk0_to_ends/ppermute | solution.py:830
  59.7 2.9 %collective-permute-start.12 = (f32[2,2,5,16,128]{4,3,2,1,0:T(8,128)S(1)}, f32[2,2,5,16,128]{4,3,2,1,0:T(8,128)S(1)}, u32[]{:S(2)}, u32[]{:S(2)}) collective-permute-start(f32[2,2,5,16,128]{4,3,2,1,0:T(8,128)S(1)} %get-tuple-element.70), channel_id=1, source_target_pairs={{0,2},{1,3},{2,0},{3,1},{4,6},{5,7},{6,4},{7,5},{8,10},{9,11},{10,... | collective-permute-start | bytes 491528 | tf_op jit(solution)/shard_map/chunk1_to_ends/ppermute | solution.py:830
  63.0 5.2 %collective-permute-start.21 = (f32[2,2,2,5,16,128]{5,4,3,2,1,0:T(8,128)S(1)}, f32[2,2,2,5,16,128]{5,4,3,2,1,0:T(8,128)S(1)}, u32[]{:S(2)}, u32[]{:S(2)}) collective-permute-start(f32[2,2,2,5,16,128]{5,4,3,2,1,0:T(8,128)S(1)} %get-tuple-element.86), channel_id=1, source_target_pairs={{0,1},{1,0},{2,3},{3,2},{4,5},{5,4},{6,7},{7,6},{8,9},{9,8},{10,11... | collective-permute-start | bytes 983048 | tf_op jit(solution)/shard_map/chunk0_apart/ppermute | solution.py:686
  68.7 1.3 %collective-permute-start.13 = (f32[2,2,2,5,16,128]{5,4,3,2,1,0:T(8,128)S(1)}, f32[2,2,2,5,16,128]{5,4,3,2,1,0:T(8,128)S(1)}, u32[]{:S(2)}, u32[]{:S(2)}) collective-permute-start(f32[2,2,2,5,16,128]{5,4,3,2,1,0:T(8,128)S(1)} %get-tuple-element.72), channel_id=1, source_target_pairs={{0,1},{1,0},{2,3},{3,2},{4,5},{5,4},{6,7},{7,6},{8,9},{9,8},{10,11... | collective-permute-start | bytes 983048 | tf_op jit(solution)/shard_map/chunk1_apart/ppermute | solution.py:686
  70.0 2.1 %answer_kernel.2.refs_0_ = f32[2,2,5,2,64,128]{5,4,3,2,1,0:T(8,128)S(1)} custom-call(bf16[4,2,5,5,32,128]{5,4,3,2,1,0:T(8,128)(2,1)S(1)} %reorder_kernel.3.lower_ref, bf16[4,2,5,5,32,128]{5,4,3,2,1,0:T(8,128)(2,1)S(1)} %reorder_kernel.4.upper_ref, f32[4,2,2,5,32,128]{5,4,3,2,1,0:T(8,128)S(1)} %get-tuple-element.77.source_ref, ...), custom_call_target="tpu_custom_call" | custom-call | bytes 10800000 | tf_op jit(solution)/shard_map/answer_kernel/pallas_call | solution.py:862
  72.1 3.3 %answer_kernel.3 = f32[2,5,4,128,128]{4,3,2,1,0:T(8,128)} custom-call(bf16[4,2,5,5,32,128]{5,4,3,2,1,0:T(8,128)(2,1)S(1)} %reorder_kernel.3.lower_ref, bf16[4,2,5,5,32,128]{5,4,3,2,1,0:T(8,128)(2,1)S(1)} %reorder_kernel.4.upper_ref, f32[4,2,2,5,32,128]{5,4,3,2,1,0:T(8,128)S(1)} %get-tuple-element.57.source_ref, ...), custom_call_target="tpu_custom_call" | custom-call | bytes 10800000 | tf_op jit(solution)/shard_map/answer_kernel/pallas_call | solution.py:862
  (57 shorter events, 6.0 us)
Async XLA Ops:
  0.0 1.3 %copy-start.3 = (bf16[2,5,4,32,4,128]{5,4,3,2,1,0:T(4,128)(2,1)S(1)}, bf16[2,5,4,32,4,128]{5,4,3,2,1,0:T(4,128)(2,1)}, u32[]{:S(2)}) copy-start(bf16[2,5,4,32,4,128]{5,4,3,2,1,0:T(4,128)(2,1)} %param.5) | copy-start | bytes 3932164
  1.3 4.3 %copy-start.4 = (f32[2,5,128]{2,0,1:T(2,128)S(1)}, f32[2,5,128]{2,0,1:T(2,128)}, u32[]{:S(2)}) copy-start(f32[2,5,128]{2,0,1:T(2,128)} %param.6) | copy-start | bytes 15364
  2.3 17.0 %collective-permute-start = (bf16[41,32,128]{2,1,0:T(8,128)(2,1)S(1)}, bf16[41,32,128]{2,1,0:T(8,128)(2,1)S(1)}, u32[]{:S(2)}, u32[]{:S(2)}) collective-permute-start(bf16[41,32,128]{2,1,0:T(8,128)(2,1)S(1)} %get-tuple-element.49), channel_id=1, source_target_pairs={{0,8},{8,0},{16,24},{24,16},{1,9},{9,1},{17,25},{25,17},{2,10},{10... | collective-permute-start | bytes 1007624 | tf_op jit(solution)/shard_map/forcing1/ppermute | solution.py:686
  4.4 14.9 %collective-permute-start.1 = (bf16[41,32,128]{2,1,0:T(8,128)(2,1)S(1)}, bf16[41,32,128]{2,1,0:T(8,128)(2,1)S(1)}, u32[]{:S(2)}, u32[]{:S(2)}) collective-permute-start(bf16[41,32,128]{2,1,0:T(8,128)(2,1)S(1)} %get-tuple-element.50), channel_id=1, source_target_pairs={{0,16},{8,24},{16,0},{24,8},{1,17},{9,25},{17,1},{25,9},{2,18},{10... | collective-permute-start | bytes 1007624 | tf_op jit(solution)/shard_map/forcing2/ppermute | solution.py:686
  5.6 14.5 %collective-permute-start.2 = (bf16[41,32,128]{2,1,0:T(8,128)(2,1)S(1)}, bf16[41,32,128]{2,1,0:T(8,128)(2,1)S(1)}, u32[]{:S(2)}, u32[]{:S(2)}) collective-permute-start(bf16[41,32,128]{2,1,0:T(8,128)(2,1)S(1)} %get-tuple-element.51), channel_id=1, source_target_pairs={{0,24},{8,16},{16,8},{24,0},{1,25},{9,17},{17,9},{25,1},{2,26},{10... | collective-permute-start | bytes 1007624 | tf_op jit(solution)/shard_map/forcing3/ppermute | solution.py:686
  5.7 1.4 %copy-start = (bf16[2,5,5,32,4,128]{5,4,3,2,1,0:T(4,128)(2,1)S(1)}, bf16[2,5,5,32,4,128]{5,4,3,2,1,0:T(4,128)(2,1)}, u32[]{:S(2)}) copy-start(bf16[2,5,5,32,4,128]{5,4,3,2,1,0:T(4,128)(2,1)} %param.9) | copy-start | bytes 4915204
  7.1 2.0 %copy-start.1 = (bf16[2,5,5,32,4,128]{5,4,3,2,1,0:T(4,128)(2,1)S(1)}, bf16[2,5,5,32,4,128]{5,4,3,2,1,0:T(4,128)(2,1)}, u32[]{:S(2)}) copy-start(bf16[2,5,5,32,4,128]{5,4,3,2,1,0:T(4,128)(2,1)} %param.8) | copy-start | bytes 4915204
  21.0 6.1 %collective-permute-start.6 = (f32[3,2,5,5,16,128]{5,4,3,2,1,0:T(8,128)S(1)}, f32[3,2,5,5,16,128]{5,4,3,2,1,0:T(8,128)S(1)}, u32[]{:S(2)}, u32[]{:S(2)}) collective-permute-start(f32[3,2,5,5,16,128]{5,4,3,2,1,0:T(8,128)S(1)} %get-tuple-element.60), channel_id=1, source_target_pairs={{0,1},{1,0},{2,3},{3,2},{4,5},{5,4},{6,7},{7,6},{8,9},{9,8},{10,11... | collective-permute-start | bytes 3686408 | tf_op jit(solution)/shard_map/matrices_core/ppermute | solution.py:686
  22.9 6.8 %collective-permute-start.16 = (f16[2,2,5,32,128]{4,3,2,1,0:T(8,128)(2,1)S(1)}, f16[2,2,5,32,128]{4,3,2,1,0:T(8,128)(2,1)S(1)}, u32[]{:S(2)}, u32[]{:S(2)}) collective-permute-start(f16[2,2,5,32,128]{4,3,2,1,0:T(8,128)(2,1)S(1)} %convert_element_type.46), channel_id=1, source_target_pairs={{0,24},{8,16},{16,8},{24,0},{1,25},{9,17},{17,9},{25,1},{2,26},{10... | collective-permute-start | bytes 491528 | tf_op jit(solution)/shard_map/chunk0_driving3/ppermute | solution.py:686
  24.4 9.4 %collective-permute-start.15 = (f16[2,2,5,32,128]{4,3,2,1,0:T(8,128)(2,1)S(1)}, f16[2,2,5,32,128]{4,3,2,1,0:T(8,128)(2,1)S(1)}, u32[]{:S(2)}, u32[]{:S(2)}) collective-permute-start(f16[2,2,5,32,128]{4,3,2,1,0:T(8,128)(2,1)S(1)} %convert_element_type.44), channel_id=1, source_target_pairs={{0,16},{8,24},{16,0},{24,8},{1,17},{9,25},{17,1},{25,9},{2,18},{10... | collective-permute-start | bytes 491528 | tf_op jit(solution)/shard_map/chunk0_driving2/ppermute | solution.py:686
  25.3 11.9 %collective-permute-start.14 = (f16[2,2,5,32,128]{4,3,2,1,0:T(8,128)(2,1)S(1)}, f16[2,2,5,32,128]{4,3,2,1,0:T(8,128)(2,1)S(1)}, u32[]{:S(2)}, u32[]{:S(2)}) collective-permute-start(f16[2,2,5,32,128]{4,3,2,1,0:T(8,128)(2,1)S(1)} %convert_element_type.42), channel_id=1, source_target_pairs={{0,8},{8,0},{16,24},{24,16},{1,9},{9,1},{17,25},{25,17},{2,10},{10... | collective-permute-start | bytes 491528 | tf_op jit(solution)/shard_map/chunk0_driving1/ppermute | solution.py:686
  25.8 15.2 %collective-permute-start.5 = (f16[2,2,5,32,128]{4,3,2,1,0:T(8,128)(2,1)S(1)}, f16[2,2,5,32,128]{4,3,2,1,0:T(8,128)(2,1)S(1)}, u32[]{:S(2)}, u32[]{:S(2)}) collective-permute-start(f16[2,2,5,32,128]{4,3,2,1,0:T(8,128)(2,1)S(1)} %convert_element_type.40), channel_id=1, source_target_pairs={{0,24},{8,16},{16,8},{24,0},{1,25},{9,17},{17,9},{25,1},{2,26},{10... | collective-permute-start | bytes 491528 | tf_op jit(solution)/shard_map/chunk1_driving3/ppermute | solution.py:686
  27.1 13.9 %collective-permute-start.4 = (f16[2,2,5,32,128]{4,3,2,1,0:T(8,128)(2,1)S(1)}, f16[2,2,5,32,128]{4,3,2,1,0:T(8,128)(2,1)S(1)}, u32[]{:S(2)}, u32[]{:S(2)}) collective-permute-start(f16[2,2,5,32,128]{4,3,2,1,0:T(8,128)(2,1)S(1)} %convert_element_type.38), channel_id=1, source_target_pairs={{0,16},{8,24},{16,0},{24,8},{1,17},{9,25},{17,1},{25,9},{2,18},{10... | collective-permute-start | bytes 491528 | tf_op jit(solution)/shard_map/chunk1_driving2/ppermute | solution.py:686
  28.0 7.1 %copy-start.2 = (bf16[2,5,5,32,4,128]{5,4,3,2,1,0:T(4,128)(2,1)S(1)}, bf16[2,5,5,32,4,128]{5,4,3,2,1,0:T(4,128)(2,1)}, u32[]{:S(2)}) copy-start(bf16[2,5,5,32,4,128]{5,4,3,2,1,0:T(4,128)(2,1)} %param.7) | copy-start | bytes 4915204
  29.7 11.4 %collective-permute-start.3 = (f16[2,2,5,32,128]{4,3,2,1,0:T(8,128)(2,1)S(1)}, f16[2,2,5,32,128]{4,3,2,1,0:T(8,128)(2,1)S(1)}, u32[]{:S(2)}, u32[]{:S(2)}) collective-permute-start(f16[2,2,5,32,128]{4,3,2,1,0:T(8,128)(2,1)S(1)} %convert_element_type.36), channel_id=1, source_target_pairs={{0,8},{8,0},{16,24},{24,16},{1,9},{9,1},{17,25},{25,17},{2,10},{10... | collective-permute-start | bytes 491528 | tf_op jit(solution)/shard_map/chunk1_driving1/ppermute | solution.py:686
  33.8 10.4 %collective-permute-start.8 = (f32[2,5,5,16,128]{4,3,2,1,0:T(8,128)S(1)}, f32[2,5,5,16,128]{4,3,2,1,0:T(8,128)S(1)}, u32[]{:S(2)}, u32[]{:S(2)}) collective-permute-start(f32[2,5,5,16,128]{4,3,2,1,0:T(8,128)S(1)} %slice_bitcast_fusion), channel_id=1, source_target_pairs={{0,2},{1,3},{2,0},{3,1},{4,6},{5,7},{6,4},{7,5},{8,10},{9,11},{10,... | collective-permute-start | bytes 1228808 | tf_op jit(solution)/shard_map/matrices_outward/ppermute | solution.py:768
  40.0 5.8 %collective-permute-start.17 = (f32[2,2,2,5,16,128]{5,4,3,2,1,0:T(8,128)S(1)}, f32[2,2,2,5,16,128]{5,4,3,2,1,0:T(8,128)S(1)}, u32[]{:S(2)}, u32[]{:S(2)}) collective-permute-start(f32[2,2,2,5,16,128]{5,4,3,2,1,0:T(8,128)S(1)} %get-tuple-element.79), channel_id=1, source_target_pairs={{0,1},{1,0},{2,3},{3,2},{4,5},{5,4},{6,7},{7,6},{8,9},{9,8},{10,11... | collective-permute-start | bytes 983048 | tf_op jit(solution)/shard_map/chunk0_core/ppermute | solution.py:686
  43.9 4.0 %collective-permute-start.7 = (f32[2,2,2,5,16,128]{5,4,3,2,1,0:T(8,128)S(1)}, f32[2,2,2,5,16,128]{5,4,3,2,1,0:T(8,128)S(1)}, u32[]{:S(2)}, u32[]{:S(2)}) collective-permute-start(f32[2,2,2,5,16,128]{5,4,3,2,1,0:T(8,128)S(1)} %get-tuple-element.64), channel_id=1, source_target_pairs={{0,1},{1,0},{2,3},{3,2},{4,5},{5,4},{6,7},{7,6},{8,9},{9,8},{10,11... | collective-permute-start | bytes 983048 | tf_op jit(solution)/shard_map/chunk1_core/ppermute | solution.py:686
  44.2 12.8 %collective-permute-start.9 = (f32[2,5,5,16,128]{4,3,2,1,0:T(8,128)S(1)}, f32[2,5,5,16,128]{4,3,2,1,0:T(8,128)S(1)}, u32[]{:S(2)}, u32[]{:S(2)}) collective-permute-start(f32[2,5,5,16,128]{4,3,2,1,0:T(8,128)S(1)} %upper_half_kernel.1), channel_id=1, source_target_pairs={{0,1},{1,0},{2,4},{4,2},{3,5},{5,3},{6,7},{7,6},{8,9},{9,8},{10,12... | collective-permute-start | bytes 1228808 | tf_op jit(solution)/shard_map/matrices_inward/ppermute | solution.py:805
  46.2 4.4 %collective-permute-start.18 = (f32[2,2,5,16,128]{4,3,2,1,0:T(8,128)S(1)}, f32[2,2,5,16,128]{4,3,2,1,0:T(8,128)S(1)}, u32[]{:S(2)}, u32[]{:S(2)}) collective-permute-start(f32[2,2,5,16,128]{4,3,2,1,0:T(8,128)S(1)} %get-tuple-element.82), channel_id=1, source_target_pairs={{0,2},{1,3},{2,0},{3,1},{4,6},{5,7},{6,4},{7,5},{8,10},{9,11},{10,... | collective-permute-start | bytes 491528 | tf_op jit(solution)/shard_map/chunk0_to_middle/ppermute | solution.py:814
  48.4 6.7 %collective-permute-start.10 = (f32[2,2,5,16,128]{4,3,2,1,0:T(8,128)S(1)}, f32[2,2,5,16,128]{4,3,2,1,0:T(8,128)S(1)}, u32[]{:S(2)}, u32[]{:S(2)}) collective-permute-start(f32[2,2,5,16,128]{4,3,2,1,0:T(8,128)S(1)} %get-tuple-element.68), channel_id=1, source_target_pairs={{0,2},{1,3},{2,0},{3,1},{4,6},{5,7},{6,4},{7,5},{8,10},{9,11},{10,... | collective-permute-start | bytes 491528 | tf_op jit(solution)/shard_map/chunk1_to_middle/ppermute | solution.py:814
  50.7 6.3 %collective-permute-start.19 = (f32[2,2,5,16,128]{4,3,2,1,0:T(8,128)S(1)}, f32[2,2,5,16,128]{4,3,2,1,0:T(8,128)S(1)}, u32[]{:S(2)}, u32[]{:S(2)}) collective-permute-start(f32[2,2,5,16,128]{4,3,2,1,0:T(8,128)S(1)} %halves_kernel.3.mine_ref), channel_id=1, source_target_pairs={{0,1},{1,0},{2,4},{4,2},{3,5},{5,3},{6,7},{7,6},{8,9},{9,8},{10,12... | collective-permute-start | bytes 491528 | tf_op jit(solution)/shard_map/chunk0_middle/ppermute | solution.py:822
  55.2 4.5 %collective-permute-start.11 = (f32[2,2,5,16,128]{4,3,2,1,0:T(8,128)S(1)}, f32[2,2,5,16,128]{4,3,2,1,0:T(8,128)S(1)}, u32[]{:S(2)}, u32[]{:S(2)}) collective-permute-start(f32[2,2,5,16,128]{4,3,2,1,0:T(8,128)S(1)} %halves_kernel.2.mine_ref), channel_id=1, source_target_pairs={{0,1},{1,0},{2,4},{4,2},{3,5},{5,3},{6,7},{7,6},{8,9},{9,8},{10,12... | collective-permute-start | bytes 491528 | tf_op jit(solution)/shard_map/chunk1_middle/ppermute | solution.py:822
  57.0 5.6 %collective-permute-start.20 = (f32[2,2,5,16,128]{4,3,2,1,0:T(8,128)S(1)}, f32[2,2,5,16,128]{4,3,2,1,0:T(8,128)S(1)}, u32[]{:S(2)}, u32[]{:S(2)}) collective-permute-start(f32[2,2,5,16,128]{4,3,2,1,0:T(8,128)S(1)} %get-tuple-element.84), channel_id=1, source_target_pairs={{0,2},{1,3},{2,0},{3,1},{4,6},{5,7},{6,4},{7,5},{8,10},{9,11},{10,... | collective-permute-start | bytes 491528 | tf_op jit(solution)/shard_map/chunk0_to_ends/ppermute | solution.py:830
  59.7 8.5 %collective-permute-start.12 = (f32[2,2,5,16,128]{4,3,2,1,0:T(8,128)S(1)}, f32[2,2,5,16,128]{4,3,2,1,0:T(8,128)S(1)}, u32[]{:S(2)}, u32[]{:S(2)}) collective-permute-start(f32[2,2,5,16,128]{4,3,2,1,0:T(8,128)S(1)} %get-tuple-element.70), channel_id=1, source_target_pairs={{0,2},{1,3},{2,0},{3,1},{4,6},{5,7},{6,4},{7,5},{8,10},{9,11},{10,... | collective-permute-start | bytes 491528 | tf_op jit(solution)/shard_map/chunk1_to_ends/ppermute | solution.py:830
  63.0 7.0 %collective-permute-start.21 = (f32[2,2,2,5,16,128]{5,4,3,2,1,0:T(8,128)S(1)}, f32[2,2,2,5,16,128]{5,4,3,2,1,0:T(8,128)S(1)}, u32[]{:S(2)}, u32[]{:S(2)}) collective-permute-start(f32[2,2,2,5,16,128]{5,4,3,2,1,0:T(8,128)S(1)} %get-tuple-element.86), channel_id=1, source_target_pairs={{0,1},{1,0},{2,3},{3,2},{4,5},{5,4},{6,7},{7,6},{8,9},{9,8},{10,11... | collective-permute-start | bytes 983048 | tf_op jit(solution)/shard_map/chunk0_apart/ppermute | solution.py:686
  68.7 3.4 %collective-permute-start.13 = (f32[2,2,2,5,16,128]{5,4,3,2,1,0:T(8,128)S(1)}, f32[2,2,2,5,16,128]{5,4,3,2,1,0:T(8,128)S(1)}, u32[]{:S(2)}, u32[]{:S(2)}) collective-permute-start(f32[2,2,2,5,16,128]{5,4,3,2,1,0:T(8,128)S(1)} %get-tuple-element.72), channel_id=1, source_target_pairs={{0,1},{1,0},{2,3},{3,2},{4,5},{5,4},{6,7},{7,6},{8,9},{9,8},{10,11... | collective-permute-start | bytes 983048 | tf_op jit(solution)/shard_map/chunk1_apart/ppermute | solution.py:686

commit v4 on v3

--- a/solution.py
+++ b/solution.py
@@ -173,7 +173,7 @@
 
 
 def filter_kernel(sources, chunks, kernel_ref, *refs):
-    arrived, scale_ref, outs = refs[:sources], refs[sources], refs[sources + 1 :]
+    arrived, scale_ref, outs = refs[:1] + refs[1:sources][::-1], refs[sources], refs[sources + 1 :]
     each, fields, points = outs[0].shape[0] * chunks, outs[0].shape[2], outs[0].shape[3]
     last = arrived[0].shape[0] - 1
     peak = arrived[0][last].astype(jnp.float32)
@@ -298,7 +298,10 @@
     lax.fori_loop(0, 2, half_of, 0)
 
 
-def pair_matrices_kernel(after_ref, keep_ref, other_ref, pair_ref, chip_ref, joint_ref):
+def pair_matrices_kernel(
+    after_ref, keep_ref, other_ref, mark_ref, pair_ref, chip_ref, joint_ref
+):
+    mark_ref[...] = jnp.zeros_like(mark_ref)
     core = lax.axis_index("wall") % 2
     size = keep_ref.shape[2]
     for which in range(3):
@@ -697,9 +700,8 @@
         micros=2.0,
         in_specs=[vmem()],
     )(forcing)
-    sent = [sent[0]] + [
-        swap(sent[m], m, "span", f"forcing{m}") for m in range(1, spans)
-    ]
+    back = [swap(sent[m], m, "span", f"forcing{m}") for m in range(spans - 1, 0, -1)]
+    sent = [sent[0]] + back[::-1]
 
     kept = jnp.bfloat16 if half % 16 == 0 else jnp.float32
     moved_shape = jax.ShapeDtypeStruct((rows, 2, fields, fields, points, width), kept)
@@ -734,25 +736,13 @@
         * (spans * len(CHUNKS)),
         micros=1.0,
         in_specs=[vmem()] * (1 + spans),
-    )(kernel, *sent)
-    drivings = []
-    for number in range(len(CHUNKS)):
-        own = outs[number * spans : (number + 1) * spans]
-        drivings.append(
-            [own[0]]
-            + [
-                swap(
-                    own[m].astype(jnp.float16), m, "span", f"chunk{number}_driving{m}"
-                ).astype(jnp.float32)
-                for m in range(1, spans)
-            ]
-        )
-
+    )(kernel, sent[0], *sent[:0:-1])
     pivots = reorder(pivot_inverse, scale)
     other = swap(gate(send, scale), 1, "wall", "matrices_core")
-    pair, chip_matrices, joint = call(
+    paired, pair, chip_matrices, joint = call(
         pair_matrices_kernel,
         [
+            mark,
             f32(2, *summary.shape),
             summary,
             f32(2, fields, fields, *plane),
@@ -760,6 +750,20 @@
             micros=1.4,
         in_specs=[anywhere()] + [vmem()] * 2,
     )(scale, keep, other)
+    drivings = []
+    for number in range(len(CHUNKS)):
+        own = outs[number * spans : (number + 1) * spans]
+        narrow = [array.astype(jnp.float16) for array in own]
+        if number > 0:
+            narrow = [gate(array, paired) for array in narrow]
+        drivings.append(
+            [own[0]]
+            + [
+                swap(narrow[m], m, "span", f"chunk{number}_driving{m}").astype(jnp.float32)
+                for m in range(1, spans)
+            ]
+        )
+
     tree = chips == 4
     outward = [(i, i ^ 2) for i in range(walls)]
     inward = [(0, 1), (1, 0), (2, 4), (4, 2), (3, 5), (5, 3), (6, 7), (7, 6)]

time: 75.7 us -> 75.4 us (level)
  transfers between devices with their start and end apart: 22 -> 22, of which waited for: 5 -> 5; matrix products, arithmetic and copies ran while one was open for 0% -> 0% of each run, Pallas kernels for 33% -> 34%
where the time goes in v4:
time: 75.4 us; the launch traced here: 75.2 us
  starting transfers between devices  34.7 us (46%)
  Pallas kernels  30.8 us (41%)
  waiting for transfers between devices  6.16 us (8%)
  local copies, waits for them, and re-layouts  2.79 us (4%)
    ppermute x14, starting transfers between devices, swap(): return lax.ppermute(array, axis, [(i, i ^ distance) for i in range(count)])  18.2 us
    ppermute x2, starting transfers between devices, local(): across = lax.ppermute(mine, 'wall', inward)  6.09 us
    pallas_call x1, Pallas kernels, local(): call(functools.partial(summary_kernel, rows), [mark] + [summary] * 2, mic...  6.05 us
    pallas_call x3, Pallas kernels, reorder(): call(functools.partial(reorder_kernel, rows), moved_shape, micros=2.0, in...  5.99 us
    ppermute x2, starting transfers between devices, local(): extra = (lax.ppermute(outgoing, 'wall', outward),)  5.75 us
    pallas_call x2, Pallas kernels, local(): call(functools.partial(local_kernel, count, spans, rows), [f32(rows, coun...  5.56 us
    pallas_call x2, Pallas kernels, local(): call(functools.partial(answer_kernel, count, chosen[0] if final else None...  5.38 us
    ppermute x14, waiting for transfers between devices, swap(): return lax.ppermute(array, axis, [(i, i ^ distance) for i in range(count)])  3.92 us
  transfers between devices with their start and end apart: 22, of which 5 were waited for; matrix products, arithmetic and copies ran while one was open for 0% of the time, Pallas kernels for 34%

profile of v4, /device:TPU:1, one launch (start us, length us, event | category | flops | bytes accessed | tf_op | source)
XLA Modules:
  0.0 75.2 jit_solution(10073861028909495406)
XLA Ops:
  0.0 1.3 %copy-done.3 = bf16[2,5,4,32,4,128]{5,4,3,2,1,0:T(4,128)(2,1)S(1)} copy-done((bf16[2,5,4,32,4,128]{5,4,3,2,1,0:T(4,128)(2,1)S(1)}, bf16[2,5,4,32,4,128]{5,4,3,2,1,0:T(4,128)(2,1)}, u32[]{:S(2)}) %copy-start.3) | copy-done | bytes 1310744
  1.3 1.0 %repack_kernel.1 = (f32[8,128]{1,0:T(8,128)S(1)}, bf16[41,32,128]{2,1,0:T(8,128)(2,1)S(1)}, bf16[41,32,128]{2,1,0:T(8,128)(2,1)S(1)}, bf16[41,32,128]{2,1,0:T(8,128)(2,1)S(1)}, bf16[41,32,128]{2,1,0:T(8,128)(2,1)S(1)}) custom-call(bf16[2,5,4,128,128]{4,3,2,1,0:T(8,128)(2,1)S(1)} %bitcast.10), custom_call_target="tpu_custom_call" | custom-call | bytes 7200000 | tf_op jit(solution)/shard_map/repack_kernel/pallas_call | solution.py:697
  2.3 3.1 %collective-permute-start = (bf16[41,32,128]{2,1,0:T(8,128)(2,1)S(1)}, bf16[41,32,128]{2,1,0:T(8,128)(2,1)S(1)}, u32[]{:S(2)}, u32[]{:S(2)}) collective-permute-start(bf16[41,32,128]{2,1,0:T(8,128)(2,1)S(1)} %get-tuple-element.53), channel_id=1, source_target_pairs={{0,24},{8,16},{16,8},{24,0},{1,25},{9,17},{17,9},{25,1},{2,26},{10... | collective-permute-start | bytes 1007624 | tf_op jit(solution)/shard_map/forcing3/ppermute | solution.py:689
  5.7 1.4 %copy-done = bf16[2,5,5,32,4,128]{5,4,3,2,1,0:T(4,128)(2,1)S(1)} copy-done((bf16[2,5,5,32,4,128]{5,4,3,2,1,0:T(4,128)(2,1)S(1)}, bf16[2,5,5,32,4,128]{5,4,3,2,1,0:T(4,128)(2,1)}, u32[]{:S(2)}) %copy-start) | copy-done | bytes 1638424
  7.2 2.0 %reorder_kernel.4.upper_ref = bf16[4,2,5,5,32,128]{5,4,3,2,1,0:T(8,128)(2,1)S(1)} custom-call(bf16[2,5,5,128,128]{4,3,2,1,0:T(8,128)(2,1)S(1)} %bitcast.7, f32[8,128]{1,0:T(8,128)S(1)} %get-tuple-element.50.after_ref), custom_call_target="tpu_custom_call" | custom-call | bytes 7200000 | tf_op jit(solution)/shard_map/reorder_kernel/pallas_call | solution.py:711
  9.2 2.0 %reorder_kernel.3.lower_ref = bf16[4,2,5,5,32,128]{5,4,3,2,1,0:T(8,128)(2,1)S(1)} custom-call(bf16[2,5,5,128,128]{4,3,2,1,0:T(8,128)(2,1)S(1)} %bitcast.8, f32[8,128]{1,0:T(8,128)S(1)} %get-tuple-element.50.after_ref), custom_call_target="tpu_custom_call" | custom-call | bytes 7200000 | tf_op jit(solution)/shard_map/reorder_kernel/pallas_call | solution.py:711
  11.2 6.0 %summary_kernel.1 = (f32[8,128]{1,0:T(8,128)S(1)}, f32[3,2,5,5,16,128]{5,4,3,2,1,0:T(8,128)S(1)}, f32[3,2,5,5,16,128]{5,4,3,2,1,0:T(8,128)S(1)}) custom-call(bf16[4,2,5,5,32,128]{5,4,3,2,1,0:T(8,128)(2,1)S(1)} %reorder_kernel.3.lower_ref, bf16[4,2,5,5,32,128]{5,4,3,2,1,0:T(8,128)(2,1)S(1)} %reorder_kernel.4.upper_ref), custom_call_target="tpu_custom_call" | custom-call | bytes 21600000 | tf_op jit(solution)/shard_map/summary_kernel/pallas_call | solution.py:719
  17.2 2.1 %table_kernel.1.kernel_ref = bf16[5,512,256]{2,1,0:T(8,128)(2,1)S(1)} custom-call(f32[2,5,128]{2,1,0:T(8,128)S(1)} %copy.6.factor_ref, f32[8,128]{1,0:T(8,128)S(1)} %get-tuple-element.51.after_ref), custom_call_target="tpu_custom_call" | custom-call | bytes 7200000 | tf_op jit(solution)/shard_map/table_kernel/pallas_call | solution.py:726
  19.4 1.5 %collective-permute-done.1.refs_2_ = bf16[41,32,128]{2,1,0:T(8,128)(2,1)S(1)} collective-permute-done((bf16[41,32,128]{2,1,0:T(8,128)(2,1)S(1)}, bf16[41,32,128]{2,1,0:T(8,128)(2,1)S(1)}, u32[]{:S(2)}, u32[]{:S(2)}) %collective-permute-start.1) | collective-permute-done | bytes 335904 | tf_op jit(solution)/shard_map/forcing2/ppermute | solution.py:689
  20.9 0.9 %filter_kernel.1 = (f32[8,128]{1,0:T(8,128)S(1)}, f32[2,2,5,32,128]{4,3,2,1,0:T(8,128)S(1)}, f32[2,2,5,32,128]{4,3,2,1,0:T(8,128)S(1)}, f32[2,2,5,32,128]{4,3,2,...) custom-call(bf16[5,512,256]{2,1,0:T(8,128)(2,1)S(1)} %table_kernel.1, ...), custom_call_target="tpu_custom_call" | custom-call | bytes 3600000 | tf_op jit(solution)/shard_map/filter_kernel/pallas_call | solution.py:732
  22.7 1.6 %collective-permute-start.16 = (f16[2,2,5,32,128]{4,3,2,1,0:T(8,128)(2,1)S(1)}, f16[2,2,5,32,128]{4,3,2,1,0:T(8,128)(2,1)S(1)}, u32[]{:S(2)}, u32[]{:S(2)}) collective-permute-start(f16[2,2,5,32,128]{4,3,2,1,0:T(8,128)(2,1)S(1)} %convert_element_type.46), channel_id=1, source_target_pairs={{0,24},{8,16},{16,8},{24,0},{1,25},{9,17},{17,9},{25,1},{2,26},{10... | collective-permute-start | bytes 491528 | tf_op jit(solution)/shard_map/chunk0_driving3/ppermute | solution.py:689
  24.4 1.0 %collective-permute-start.15 = (f16[2,2,5,32,128]{4,3,2,1,0:T(8,128)(2,1)S(1)}, f16[2,2,5,32,128]{4,3,2,1,0:T(8,128)(2,1)S(1)}, u32[]{:S(2)}, u32[]{:S(2)}) collective-permute-start(f16[2,2,5,32,128]{4,3,2,1,0:T(8,128)(2,1)S(1)} %convert_element_type.44), channel_id=1, source_target_pairs={{0,16},{8,24},{16,0},{24,8},{1,17},{9,25},{17,1},{25,9},{2,18},{10... | collective-permute-start | bytes 491528 | tf_op jit(solution)/shard_map/chunk0_driving2/ppermute | solution.py:689
  25.6 2.0 %pair_matrices_kernel.1 = (f32[8,128]{1,0:T(8,128)}, f32[2,3,2,5,5,16,128]{6,5,4,3,2,1,0:T(8,128)S(1)}, f32[3,2,5,5,16,128]{5,4,3,2,1,0:T(8,128)S(1)}, f32[2,5,5,16,128]{4,3,2,1,0:T(8,128)S(1)}) custom-call(f32[8,128]{1,0:T(8,128)S(1)} %get-tuple-element.56.after_ref.scale_ref, f32[3,2,5,5,16,128]{5,4,3,2,1,0:T(8,128)S(1)} %get-tuple-element.59.keep_ref, ...), custom_call_target="tpu_custom_call" | custom-call | bytes 5040000 | tf_op jit(solution)/shard_map/pair_matrices_kernel/pallas_call | solution.py:742
  27.6 1.2 %collective-permute-start.4 = (f16[2,2,5,32,128]{4,3,2,1,0:T(8,128)(2,1)S(1)}, f16[2,2,5,32,128]{4,3,2,1,0:T(8,128)(2,1)S(1)}, u32[]{:S(2)}, u32[]{:S(2)}) collective-permute-start(f16[2,2,5,32,128]{4,3,2,1,0:T(8,128)(2,1)S(1)} %convert_element_type.36), channel_id=1, source_target_pairs={{0,8},{8,0},{16,24},{24,16},{1,9},{9,1},{17,25},{25,17},{2,10},{10... | collective-permute-start | bytes 491528 | tf_op jit(solution)/shard_map/chunk1_driving1/ppermute | solution.py:689
  29.5 1.5 %collective-permute-start.6 = (f16[2,2,5,32,128]{4,3,2,1,0:T(8,128)(2,1)S(1)}, f16[2,2,5,32,128]{4,3,2,1,0:T(8,128)(2,1)S(1)}, u32[]{:S(2)}, u32[]{:S(2)}) collective-permute-start(f16[2,2,5,32,128]{4,3,2,1,0:T(8,128)(2,1)S(1)} %convert_element_type.40), channel_id=1, source_target_pairs={{0,24},{8,16},{16,8},{24,0},{1,25},{9,17},{17,9},{25,1},{2,26},{10... | collective-permute-start | bytes 491528 | tf_op jit(solution)/shard_map/chunk1_driving3/ppermute | solution.py:689
  31.0 2.3 %collective-permute-done.15 = f16[2,2,5,32,128]{4,3,2,1,0:T(8,128)(2,1)S(1)} collective-permute-done((f16[2,2,5,32,128]{4,3,2,1,0:T(8,128)(2,1)S(1)}, f16[2,2,5,32,128]{4,3,2,1,0:T(8,128)(2,1)S(1)}, u32[]{:S(2)}, u32[]{:S(2)}) %collective-permute-start.15) | collective-permute-done | bytes 163872 | tf_op jit(solution)/shard_map/chunk0_driving2/ppermute | solution.py:689
  33.3 1.3 %collective-permute-start.8 = (f32[2,5,5,16,128]{4,3,2,1,0:T(8,128)S(1)}, f32[2,5,5,16,128]{4,3,2,1,0:T(8,128)S(1)}, u32[]{:S(2)}, u32[]{:S(2)}) collective-permute-start(f32[2,5,5,16,128]{4,3,2,1,0:T(8,128)S(1)} %slice_bitcast_fusion), channel_id=1, source_target_pairs={{0,2},{1,3},{2,0},{3,1},{4,6},{5,7},{6,4},{7,5},{8,10},{9,11},{10,... | collective-permute-start | bytes 1228808 | tf_op jit(solution)/shard_map/matrices_outward/ppermute | solution.py:772
  34.6 2.0 %reorder_kernel.5.pivot_ref = bf16[4,2,5,5,32,128]{5,4,3,2,1,0:T(8,128)(2,1)S(1)} custom-call(bf16[2,5,5,128,128]{4,3,2,1,0:T(8,128)(2,1)S(1)} %bitcast.9, f32[8,128]{1,0:T(8,128)S(1)} %get-tuple-element.56.after_ref.scale_ref), custom_call_target="tpu_custom_call" | custom-call | bytes 7200000 | tf_op jit(solution)/shard_map/reorder_kernel/pallas_call | solution.py:711
  36.7 2.8 %local_kernel.3 = (f32[4,2,2,5,32,128]{5,4,3,2,1,0:T(8,128)S(1)}, f32[2,2,2,5,16,128]{5,4,3,2,1,0:T(8,128)S(1)}, f32[2,2,2,5,16,128]{5,4,3,2,1,0:T(8,128)S(1)}) custom-call(bf16[4,2,5,5,32,128]{5,4,3,2,1,0:T(8,128)(2,1)S(1)} %reorder_kernel.5.pivot_ref, bf16[4,2,5,5,32,128]{5,4,3,2,1,0:T(8,128)(2,1)S(1)} %reorder_kernel.3.lower_ref, ...), custom_call_target="tpu_custom_call" | custom-call | bytes 10080000 | tf_op jit(solution)/shard_map/local_kernel/pallas_call | solution.py:781
  39.5 0.9 %collective-permute-start.17 = (f32[2,2,2,5,16,128]{5,4,3,2,1,0:T(8,128)S(1)}, f32[2,2,2,5,16,128]{5,4,3,2,1,0:T(8,128)S(1)}, u32[]{:S(2)}, u32[]{:S(2)}) collective-permute-start(f32[2,2,2,5,16,128]{5,4,3,2,1,0:T(8,128)S(1)} %get-tuple-element.87), channel_id=1, source_target_pairs={{0,1},{1,0},{2,3},{3,2},{4,5},{5,4},{6,7},{7,6},{8,9},{9,8},{10,11... | collective-permute-start | bytes 983048 | tf_op jit(solution)/shard_map/chunk0_core/ppermute | solution.py:689
  40.5 2.8 %local_kernel.2 = (f32[4,2,2,5,32,128]{5,4,3,2,1,0:T(8,128)S(1)}, f32[2,2,2,5,16,128]{5,4,3,2,1,0:T(8,128)S(1)}, f32[2,2,2,5,16,128]{5,4,3,2,1,0:T(8,128)S(1)}) custom-call(bf16[4,2,5,5,32,128]{5,4,3,2,1,0:T(8,128)(2,1)S(1)} %reorder_kernel.5.pivot_ref, bf16[4,2,5,5,32,128]{5,4,3,2,1,0:T(8,128)(2,1)S(1)} %reorder_kernel.3.lower_ref, ...), custom_call_target="tpu_custom_call" | custom-call | bytes 10080000 | tf_op jit(solution)/shard_map/local_kernel/pallas_call | solution.py:781
  43.8 1.4 %collective-permute-start.9 = (f32[2,5,5,16,128]{4,3,2,1,0:T(8,128)S(1)}, f32[2,5,5,16,128]{4,3,2,1,0:T(8,128)S(1)}, u32[]{:S(2)}, u32[]{:S(2)}) collective-permute-start(f32[2,5,5,16,128]{4,3,2,1,0:T(8,128)S(1)} %upper_half_kernel.1), channel_id=1, source_target_pairs={{0,1},{1,0},{2,4},{4,2},{3,5},{5,3},{6,7},{7,6},{8,9},{9,8},{10,12... | collective-permute-start | bytes 1228808 | tf_op jit(solution)/shard_map/matrices_inward/ppermute | solution.py:809
  45.7 1.8 %collective-permute-start.18 = (f32[2,2,5,16,128]{4,3,2,1,0:T(8,128)S(1)}, f32[2,2,5,16,128]{4,3,2,1,0:T(8,128)S(1)}, u32[]{:S(2)}, u32[]{:S(2)}) collective-permute-start(f32[2,2,5,16,128]{4,3,2,1,0:T(8,128)S(1)} %get-tuple-element.90), channel_id=1, source_target_pairs={{0,2},{1,3},{2,0},{3,1},{4,6},{5,7},{6,4},{7,5},{8,10},{9,11},{10,... | collective-permute-start | bytes 491528 | tf_op jit(solution)/shard_map/chunk0_to_middle/ppermute | solution.py:818
  48.2 2.1 %collective-permute-done.18.came_ref.first_ref = f32[2,2,5,16,128]{4,3,2,1,0:T(8,128)S(1)} collective-permute-done((f32[2,2,5,16,128]{4,3,2,1,0:T(8,128)S(1)}, f32[2,2,5,16,128]{4,3,2,1,0:T(8,128)S(1)}, u32[]{:S(2)}, u32[]{:S(2)}) %collective-permute-start.18) | collective-permute-done | bytes 163872 | tf_op jit(solution)/shard_map/chunk0_to_middle/ppermute | solution.py:818
  50.3 4.2 %collective-permute-start.19 = (f32[2,2,5,16,128]{4,3,2,1,0:T(8,128)S(1)}, f32[2,2,5,16,128]{4,3,2,1,0:T(8,128)S(1)}, u32[]{:S(2)}, u32[]{:S(2)}) collective-permute-start(f32[2,2,5,16,128]{4,3,2,1,0:T(8,128)S(1)} %halves_kernel.3.mine_ref), channel_id=1, source_target_pairs={{0,1},{1,0},{2,4},{4,2},{3,5},{5,3},{6,7},{7,6},{8,9},{9,8},{10,12... | collective-permute-start | bytes 491528 | tf_op jit(solution)/shard_map/chunk0_middle/ppermute | solution.py:826
  54.5 1.9 %collective-permute-start.11 = (f32[2,2,5,16,128]{4,3,2,1,0:T(8,128)S(1)}, f32[2,2,5,16,128]{4,3,2,1,0:T(8,128)S(1)}, u32[]{:S(2)}, u32[]{:S(2)}) collective-permute-start(f32[2,2,5,16,128]{4,3,2,1,0:T(8,128)S(1)} %halves_kernel.2.mine_ref), channel_id=1, source_target_pairs={{0,1},{1,0},{2,4},{4,2},{3,5},{5,3},{6,7},{7,6},{8,9},{9,8},{10,12... | collective-permute-start | bytes 491528 | tf_op jit(solution)/shard_map/chunk1_middle/ppermute | solution.py:826
  56.5 2.7 %collective-permute-start.20 = (f32[2,2,5,16,128]{4,3,2,1,0:T(8,128)S(1)}, f32[2,2,5,16,128]{4,3,2,1,0:T(8,128)S(1)}, u32[]{:S(2)}, u32[]{:S(2)}) collective-permute-start(f32[2,2,5,16,128]{4,3,2,1,0:T(8,128)S(1)} %get-tuple-element.92), channel_id=1, source_target_pairs={{0,2},{1,3},{2,0},{3,1},{4,6},{5,7},{6,4},{7,5},{8,10},{9,11},{10,... | collective-permute-start | bytes 491528 | tf_op jit(solution)/shard_map/chunk0_to_ends/ppermute | solution.py:834
  59.2 3.0 %collective-permute-start.12 = (f32[2,2,5,16,128]{4,3,2,1,0:T(8,128)S(1)}, f32[2,2,5,16,128]{4,3,2,1,0:T(8,128)S(1)}, u32[]{:S(2)}, u32[]{:S(2)}) collective-permute-start(f32[2,2,5,16,128]{4,3,2,1,0:T(8,128)S(1)} %get-tuple-element.78), channel_id=1, source_target_pairs={{0,2},{1,3},{2,0},{3,1},{4,6},{5,7},{6,4},{7,5},{8,10},{9,11},{10,... | collective-permute-start | bytes 491528 | tf_op jit(solution)/shard_map/chunk1_to_ends/ppermute | solution.py:834
  62.7 5.2 %collective-permute-start.21 = (f32[2,2,2,5,16,128]{5,4,3,2,1,0:T(8,128)S(1)}, f32[2,2,2,5,16,128]{5,4,3,2,1,0:T(8,128)S(1)}, u32[]{:S(2)}, u32[]{:S(2)}) collective-permute-start(f32[2,2,2,5,16,128]{5,4,3,2,1,0:T(8,128)S(1)} %get-tuple-element.94), channel_id=1, source_target_pairs={{0,1},{1,0},{2,3},{3,2},{4,5},{5,4},{6,7},{7,6},{8,9},{9,8},{10,11... | collective-permute-start | bytes 983048 | tf_op jit(solution)/shard_map/chunk0_apart/ppermute | solution.py:689
  68.3 1.3 %collective-permute-start.13 = (f32[2,2,2,5,16,128]{5,4,3,2,1,0:T(8,128)S(1)}, f32[2,2,2,5,16,128]{5,4,3,2,1,0:T(8,128)S(1)}, u32[]{:S(2)}, u32[]{:S(2)}) collective-permute-start(f32[2,2,2,5,16,128]{5,4,3,2,1,0:T(8,128)S(1)} %get-tuple-element.80), channel_id=1, source_target_pairs={{0,1},{1,0},{2,3},{3,2},{4,5},{5,4},{6,7},{7,6},{8,9},{9,8},{10,11... | collective-permute-start | bytes 983048 | tf_op jit(solution)/shard_map/chunk1_apart/ppermute | solution.py:689
  69.7 2.1 %answer_kernel.2.refs_0_ = f32[2,2,5,2,64,128]{5,4,3,2,1,0:T(8,128)S(1)} custom-call(bf16[4,2,5,5,32,128]{5,4,3,2,1,0:T(8,128)(2,1)S(1)} %reorder_kernel.3.lower_ref, bf16[4,2,5,5,32,128]{5,4,3,2,1,0:T(8,128)(2,1)S(1)} %reorder_kernel.4.upper_ref, f32[4,2,2,5,32,128]{5,4,3,2,1,0:T(8,128)S(1)} %get-tuple-element.85.source_ref, ...), custom_call_target="tpu_custom_call" | custom-call | bytes 10800000 | tf_op jit(solution)/shard_map/answer_kernel/pallas_call | solution.py:866
  71.8 3.3 %answer_kernel.3 = f32[2,5,4,128,128]{4,3,2,1,0:T(8,128)} custom-call(bf16[4,2,5,5,32,128]{5,4,3,2,1,0:T(8,128)(2,1)S(1)} %reorder_kernel.3.lower_ref, bf16[4,2,5,5,32,128]{5,4,3,2,1,0:T(8,128)(2,1)S(1)} %reorder_kernel.4.upper_ref, f32[4,2,2,5,32,128]{5,4,3,2,1,0:T(8,128)S(1)} %get-tuple-element.68.source_ref, ...), custom_call_target="tpu_custom_call" | custom-call | bytes 10800000 | tf_op jit(solution)/shard_map/answer_kernel/pallas_call | solution.py:866
  (57 shorter events, 5.0 us)
Async XLA Ops:
  0.0 1.3 %copy-start.3 = (bf16[2,5,4,32,4,128]{5,4,3,2,1,0:T(4,128)(2,1)S(1)}, bf16[2,5,4,32,4,128]{5,4,3,2,1,0:T(4,128)(2,1)}, u32[]{:S(2)}) copy-start(bf16[2,5,4,32,4,128]{5,4,3,2,1,0:T(4,128)(2,1)} %param.5) | copy-start | bytes 3932164
  1.3 4.4 %copy-start.4 = (f32[2,5,128]{2,0,1:T(2,128)S(1)}, f32[2,5,128]{2,0,1:T(2,128)}, u32[]{:S(2)}) copy-start(f32[2,5,128]{2,0,1:T(2,128)} %param.6) | copy-start | bytes 15364
  2.3 17.1 %collective-permute-start = (bf16[41,32,128]{2,1,0:T(8,128)(2,1)S(1)}, bf16[41,32,128]{2,1,0:T(8,128)(2,1)S(1)}, u32[]{:S(2)}, u32[]{:S(2)}) collective-permute-start(bf16[41,32,128]{2,1,0:T(8,128)(2,1)S(1)} %get-tuple-element.53), channel_id=1, source_target_pairs={{0,24},{8,16},{16,8},{24,0},{1,25},{9,17},{17,9},{25,1},{2,26},{10... | collective-permute-start | bytes 1007624 | tf_op jit(solution)/shard_map/forcing3/ppermute | solution.py:689
  5.4 15.5 %collective-permute-start.1 = (bf16[41,32,128]{2,1,0:T(8,128)(2,1)S(1)}, bf16[41,32,128]{2,1,0:T(8,128)(2,1)S(1)}, u32[]{:S(2)}, u32[]{:S(2)}) collective-permute-start(bf16[41,32,128]{2,1,0:T(8,128)(2,1)S(1)} %get-tuple-element.54), channel_id=1, source_target_pairs={{0,16},{8,24},{16,0},{24,8},{1,17},{9,25},{17,1},{25,9},{2,18},{10... | collective-permute-start | bytes 1007624 | tf_op jit(solution)/shard_map/forcing2/ppermute | solution.py:689
  5.6 15.3 %collective-permute-start.2 = (bf16[41,32,128]{2,1,0:T(8,128)(2,1)S(1)}, bf16[41,32,128]{2,1,0:T(8,128)(2,1)S(1)}, u32[]{:S(2)}, u32[]{:S(2)}) collective-permute-start(bf16[41,32,128]{2,1,0:T(8,128)(2,1)S(1)} %get-tuple-element.55), channel_id=1, source_target_pairs={{0,8},{8,0},{16,24},{24,16},{1,9},{9,1},{17,25},{25,17},{2,10},{10... | collective-permute-start | bytes 1007624 | tf_op jit(solution)/shard_map/forcing1/ppermute | solution.py:689
  5.7 1.4 %copy-start = (bf16[2,5,5,32,4,128]{5,4,3,2,1,0:T(4,128)(2,1)S(1)}, bf16[2,5,5,32,4,128]{5,4,3,2,1,0:T(4,128)(2,1)}, u32[]{:S(2)}) copy-start(bf16[2,5,5,32,4,128]{5,4,3,2,1,0:T(4,128)(2,1)} %param.9) | copy-start | bytes 4915204
  7.2 2.0 %copy-start.1 = (bf16[2,5,5,32,4,128]{5,4,3,2,1,0:T(4,128)(2,1)S(1)}, bf16[2,5,5,32,4,128]{5,4,3,2,1,0:T(4,128)(2,1)}, u32[]{:S(2)}) copy-start(bf16[2,5,5,32,4,128]{5,4,3,2,1,0:T(4,128)(2,1)} %param.8) | copy-start | bytes 4915204
  21.8 3.8 %collective-permute-start.3 = (f32[3,2,5,5,16,128]{5,4,3,2,1,0:T(8,128)S(1)}, f32[3,2,5,5,16,128]{5,4,3,2,1,0:T(8,128)S(1)}, u32[]{:S(2)}, u32[]{:S(2)}) collective-permute-start(f32[3,2,5,5,16,128]{5,4,3,2,1,0:T(8,128)S(1)} %get-tuple-element.61), channel_id=1, source_target_pairs={{0,1},{1,0},{2,3},{3,2},{4,5},{5,4},{6,7},{7,6},{8,9},{9,8},{10,11... | collective-permute-start | bytes 3686408 | tf_op jit(solution)/shard_map/matrices_core/ppermute | solution.py:689
  22.7 6.8 %collective-permute-start.16 = (f16[2,2,5,32,128]{4,3,2,1,0:T(8,128)(2,1)S(1)}, f16[2,2,5,32,128]{4,3,2,1,0:T(8,128)(2,1)S(1)}, u32[]{:S(2)}, u32[]{:S(2)}) collective-permute-start(f16[2,2,5,32,128]{4,3,2,1,0:T(8,128)(2,1)S(1)} %convert_element_type.46), channel_id=1, source_target_pairs={{0,24},{8,16},{16,8},{24,0},{1,25},{9,17},{17,9},{25,1},{2,26},{10... | collective-permute-start | bytes 491528 | tf_op jit(solution)/shard_map/chunk0_driving3/ppermute | solution.py:689
  24.4 8.9 %collective-permute-start.15 = (f16[2,2,5,32,128]{4,3,2,1,0:T(8,128)(2,1)S(1)}, f16[2,2,5,32,128]{4,3,2,1,0:T(8,128)(2,1)S(1)}, u32[]{:S(2)}, u32[]{:S(2)}) collective-permute-start(f16[2,2,5,32,128]{4,3,2,1,0:T(8,128)(2,1)S(1)} %convert_element_type.44), channel_id=1, source_target_pairs={{0,16},{8,24},{16,0},{24,8},{1,17},{9,25},{17,1},{25,9},{2,18},{10... | collective-permute-start | bytes 491528 | tf_op jit(solution)/shard_map/chunk0_driving2/ppermute | solution.py:689
  25.4 11.3 %collective-permute-start.14 = (f16[2,2,5,32,128]{4,3,2,1,0:T(8,128)(2,1)S(1)}, f16[2,2,5,32,128]{4,3,2,1,0:T(8,128)(2,1)S(1)}, u32[]{:S(2)}, u32[]{:S(2)}) collective-permute-start(f16[2,2,5,32,128]{4,3,2,1,0:T(8,128)(2,1)S(1)} %convert_element_type.42), channel_id=1, source_target_pairs={{0,8},{8,0},{16,24},{24,16},{1,9},{9,1},{17,25},{25,17},{2,10},{10... | collective-permute-start | bytes 491528 | tf_op jit(solution)/shard_map/chunk0_driving1/ppermute | solution.py:689
  25.6 9.0 %copy-start.2 = (bf16[2,5,5,32,4,128]{5,4,3,2,1,0:T(4,128)(2,1)S(1)}, bf16[2,5,5,32,4,128]{5,4,3,2,1,0:T(4,128)(2,1)}, u32[]{:S(2)}) copy-start(bf16[2,5,5,32,4,128]{5,4,3,2,1,0:T(4,128)(2,1)} %param.7) | copy-start | bytes 4915204
  27.6 12.8 %collective-permute-start.4 = (f16[2,2,5,32,128]{4,3,2,1,0:T(8,128)(2,1)S(1)}, f16[2,2,5,32,128]{4,3,2,1,0:T(8,128)(2,1)S(1)}, u32[]{:S(2)}, u32[]{:S(2)}) collective-permute-start(f16[2,2,5,32,128]{4,3,2,1,0:T(8,128)(2,1)S(1)} %convert_element_type.36), channel_id=1, source_target_pairs={{0,8},{8,0},{16,24},{24,16},{1,9},{9,1},{17,25},{25,17},{2,10},{10... | collective-permute-start | bytes 491528 | tf_op jit(solution)/shard_map/chunk1_driving1/ppermute | solution.py:689
  28.8 11.6 %collective-permute-start.5 = (f16[2,2,5,32,128]{4,3,2,1,0:T(8,128)(2,1)S(1)}, f16[2,2,5,32,128]{4,3,2,1,0:T(8,128)(2,1)S(1)}, u32[]{:S(2)}, u32[]{:S(2)}) collective-permute-start(f16[2,2,5,32,128]{4,3,2,1,0:T(8,128)(2,1)S(1)} %convert_element_type.38), channel_id=1, source_target_pairs={{0,16},{8,24},{16,0},{24,8},{1,17},{9,25},{17,1},{25,9},{2,18},{10... | collective-permute-start | bytes 491528 | tf_op jit(solution)/shard_map/chunk1_driving2/ppermute | solution.py:689
  29.5 11.0 %collective-permute-start.6 = (f16[2,2,5,32,128]{4,3,2,1,0:T(8,128)(2,1)S(1)}, f16[2,2,5,32,128]{4,3,2,1,0:T(8,128)(2,1)S(1)}, u32[]{:S(2)}, u32[]{:S(2)}) collective-permute-start(f16[2,2,5,32,128]{4,3,2,1,0:T(8,128)(2,1)S(1)} %convert_element_type.40), channel_id=1, source_target_pairs={{0,24},{8,16},{16,8},{24,0},{1,25},{9,17},{17,9},{25,1},{2,26},{10... | collective-permute-start | bytes 491528 | tf_op jit(solution)/shard_map/chunk1_driving3/ppermute | solution.py:689
  33.3 10.5 %collective-permute-start.8 = (f32[2,5,5,16,128]{4,3,2,1,0:T(8,128)S(1)}, f32[2,5,5,16,128]{4,3,2,1,0:T(8,128)S(1)}, u32[]{:S(2)}, u32[]{:S(2)}) collective-permute-start(f32[2,5,5,16,128]{4,3,2,1,0:T(8,128)S(1)} %slice_bitcast_fusion), channel_id=1, source_target_pairs={{0,2},{1,3},{2,0},{3,1},{4,6},{5,7},{6,4},{7,5},{8,10},{9,11},{10,... | collective-permute-start | bytes 1228808 | tf_op jit(solution)/shard_map/matrices_outward/ppermute | solution.py:772
  39.5 5.8 %collective-permute-start.17 = (f32[2,2,2,5,16,128]{5,4,3,2,1,0:T(8,128)S(1)}, f32[2,2,2,5,16,128]{5,4,3,2,1,0:T(8,128)S(1)}, u32[]{:S(2)}, u32[]{:S(2)}) collective-permute-start(f32[2,2,2,5,16,128]{5,4,3,2,1,0:T(8,128)S(1)} %get-tuple-element.87), channel_id=1, source_target_pairs={{0,1},{1,0},{2,3},{3,2},{4,5},{5,4},{6,7},{7,6},{8,9},{9,8},{10,11... | collective-permute-start | bytes 983048 | tf_op jit(solution)/shard_map/chunk0_core/ppermute | solution.py:689
  43.3 4.3 %collective-permute-start.7 = (f32[2,2,2,5,16,128]{5,4,3,2,1,0:T(8,128)S(1)}, f32[2,2,2,5,16,128]{5,4,3,2,1,0:T(8,128)S(1)}, u32[]{:S(2)}, u32[]{:S(2)}) collective-permute-start(f32[2,2,2,5,16,128]{5,4,3,2,1,0:T(8,128)S(1)} %get-tuple-element.72), channel_id=1, source_target_pairs={{0,1},{1,0},{2,3},{3,2},{4,5},{5,4},{6,7},{7,6},{8,9},{9,8},{10,11... | collective-permute-start | bytes 983048 | tf_op jit(solution)/shard_map/chunk1_core/ppermute | solution.py:689
  43.8 12.6 %collective-permute-start.9 = (f32[2,5,5,16,128]{4,3,2,1,0:T(8,128)S(1)}, f32[2,5,5,16,128]{4,3,2,1,0:T(8,128)S(1)}, u32[]{:S(2)}, u32[]{:S(2)}) collective-permute-start(f32[2,5,5,16,128]{4,3,2,1,0:T(8,128)S(1)} %upper_half_kernel.1), channel_id=1, source_target_pairs={{0,1},{1,0},{2,4},{4,2},{3,5},{5,3},{6,7},{7,6},{8,9},{9,8},{10,12... | collective-permute-start | bytes 1228808 | tf_op jit(solution)/shard_map/matrices_inward/ppermute | solution.py:809
  45.7 4.6 %collective-permute-start.18 = (f32[2,2,5,16,128]{4,3,2,1,0:T(8,128)S(1)}, f32[2,2,5,16,128]{4,3,2,1,0:T(8,128)S(1)}, u32[]{:S(2)}, u32[]{:S(2)}) collective-permute-start(f32[2,2,5,16,128]{4,3,2,1,0:T(8,128)S(1)} %get-tuple-element.90), channel_id=1, source_target_pairs={{0,2},{1,3},{2,0},{3,1},{4,6},{5,7},{6,4},{7,5},{8,10},{9,11},{10,... | collective-permute-start | bytes 491528 | tf_op jit(solution)/shard_map/chunk0_to_middle/ppermute | solution.py:818
  48.1 6.4 %collective-permute-start.10 = (f32[2,2,5,16,128]{4,3,2,1,0:T(8,128)S(1)}, f32[2,2,5,16,128]{4,3,2,1,0:T(8,128)S(1)}, u32[]{:S(2)}, u32[]{:S(2)}) collective-permute-start(f32[2,2,5,16,128]{4,3,2,1,0:T(8,128)S(1)} %get-tuple-element.76), channel_id=1, source_target_pairs={{0,2},{1,3},{2,0},{3,1},{4,6},{5,7},{6,4},{7,5},{8,10},{9,11},{10,... | collective-permute-start | bytes 491528 | tf_op jit(solution)/shard_map/chunk1_to_middle/ppermute | solution.py:818
  50.3 6.1 %collective-permute-start.19 = (f32[2,2,5,16,128]{4,3,2,1,0:T(8,128)S(1)}, f32[2,2,5,16,128]{4,3,2,1,0:T(8,128)S(1)}, u32[]{:S(2)}, u32[]{:S(2)}) collective-permute-start(f32[2,2,5,16,128]{4,3,2,1,0:T(8,128)S(1)} %halves_kernel.3.mine_ref), channel_id=1, source_target_pairs={{0,1},{1,0},{2,4},{4,2},{3,5},{5,3},{6,7},{7,6},{8,9},{9,8},{10,12... | collective-permute-start | bytes 491528 | tf_op jit(solution)/shard_map/chunk0_middle/ppermute | solution.py:826
  54.5 4.7 %collective-permute-start.11 = (f32[2,2,5,16,128]{4,3,2,1,0:T(8,128)S(1)}, f32[2,2,5,16,128]{4,3,2,1,0:T(8,128)S(1)}, u32[]{:S(2)}, u32[]{:S(2)}) collective-permute-start(f32[2,2,5,16,128]{4,3,2,1,0:T(8,128)S(1)} %halves_kernel.2.mine_ref), channel_id=1, source_target_pairs={{0,1},{1,0},{2,4},{4,2},{3,5},{5,3},{6,7},{7,6},{8,9},{9,8},{10,12... | collective-permute-start | bytes 491528 | tf_op jit(solution)/shard_map/chunk1_middle/ppermute | solution.py:826
  56.5 5.8 %collective-permute-start.20 = (f32[2,2,5,16,128]{4,3,2,1,0:T(8,128)S(1)}, f32[2,2,5,16,128]{4,3,2,1,0:T(8,128)S(1)}, u32[]{:S(2)}, u32[]{:S(2)}) collective-permute-start(f32[2,2,5,16,128]{4,3,2,1,0:T(8,128)S(1)} %get-tuple-element.92), channel_id=1, source_target_pairs={{0,2},{1,3},{2,0},{3,1},{4,6},{5,7},{6,4},{7,5},{8,10},{9,11},{10,... | collective-permute-start | bytes 491528 | tf_op jit(solution)/shard_map/chunk0_to_ends/ppermute | solution.py:834
  59.2 8.7 %collective-permute-start.12 = (f32[2,2,5,16,128]{4,3,2,1,0:T(8,128)S(1)}, f32[2,2,5,16,128]{4,3,2,1,0:T(8,128)S(1)}, u32[]{:S(2)}, u32[]{:S(2)}) collective-permute-start(f32[2,2,5,16,128]{4,3,2,1,0:T(8,128)S(1)} %get-tuple-element.78), channel_id=1, source_target_pairs={{0,2},{1,3},{2,0},{3,1},{4,6},{5,7},{6,4},{7,5},{8,10},{9,11},{10,... | collective-permute-start | bytes 491528 | tf_op jit(solution)/shard_map/chunk1_to_ends/ppermute | solution.py:834
  62.7 7.0 %collective-permute-start.21 = (f32[2,2,2,5,16,128]{5,4,3,2,1,0:T(8,128)S(1)}, f32[2,2,2,5,16,128]{5,4,3,2,1,0:T(8,128)S(1)}, u32[]{:S(2)}, u32[]{:S(2)}) collective-permute-start(f32[2,2,2,5,16,128]{5,4,3,2,1,0:T(8,128)S(1)} %get-tuple-element.94), channel_id=1, source_target_pairs={{0,1},{1,0},{2,3},{3,2},{4,5},{5,4},{6,7},{7,6},{8,9},{9,8},{10,11... | collective-permute-start | bytes 983048 | tf_op jit(solution)/shard_map/chunk0_apart/ppermute | solution.py:689
  68.3 3.4 %collective-permute-start.13 = (f32[2,2,2,5,16,128]{5,4,3,2,1,0:T(8,128)S(1)}, f32[2,2,2,5,16,128]{5,4,3,2,1,0:T(8,128)S(1)}, u32[]{:S(2)}, u32[]{:S(2)}) collective-permute-start(f32[2,2,2,5,16,128]{5,4,3,2,1,0:T(8,128)S(1)} %get-tuple-element.80), channel_id=1, source_target_pairs={{0,1},{1,0},{2,3},{3,2},{4,5},{5,4},{6,7},{7,6},{8,9},{9,8},{10,11... | collective-permute-start | bytes 983048 | tf_op jit(solution)/shard_map/chunk1_apart/ppermute | solution.py:689

commit v5 on v4

--- a/solution.py
+++ b/solution.py
@@ -359,28 +359,30 @@
     columns, spans, rows, pivot_ref, lower_ref, upper_ref, scale_ref, *refs
 ):
     arrived = refs[:spans]
-    source_ref, keep_ref, send_ref, driving_ref, sweep_ref = refs[spans:]
+    source_ref, keep_ref, send_ref, sweep_ref = refs[spans:]
     size = pivot_ref.shape[2]
     points = pivot_ref.shape[4]
     half = points // 2
     groups = spans // rows
+    each = columns // groups
     at = lax.axis_index("span")
     scale = jnp.max(scale_ref[...])
-    for m in range(spans):
-        y = (m // groups) ^ (at // groups)
-        for t in range(columns // groups):
-            c = t * groups + ((m % groups) ^ (at % groups)) if groups > 1 else t
-            driving_ref[y, c] = arrived[m][t] * scale
     core = lax.axis_index("wall") % 2
 
     def solve(part, carry):
         span = pl.ds(part * half, half)
+        for m in range(spans):
+            y = (m // groups) ^ (at // groups)
+            drivings = [
+                [[plane * scale for plane in side] for side in load_vector(ref, size, span)]
+                for ref in (arrived[m].at[t] for t in range(each))
+            ]
+            for t, new in enumerate(block_vectors(entry(pivot_ref, y, rows=span), drivings)):
+                c = t * groups + ((m % groups) ^ (at % groups)) if groups > 1 else t
+                store_vector(source_ref.at[y, c], new, span)
         states = None
         for y in range(rows):
-            drivings = [load_vector(driving_ref.at[y, c], size, span) for c in range(columns)]
-            news = block_vectors(entry(pivot_ref, y, rows=span), drivings)
-            for c in range(columns):
-                store_vector(source_ref.at[y, c], news[c], span)
+            news = [load_vector(source_ref.at[y, c], size, span) for c in range(columns)]
             if states is not None:
                 moved = block_vectors(entry(lower_ref, y, rows=span), states)
                 news = [minus(new, move) for new, move in zip(news, moved)]
@@ -783,7 +785,6 @@
             [f32(rows, count, 2, fields, points, width), vectors, vectors],
             micros=1.4 * count,
             scratch=[
-                pltpu.VMEM((rows, count, 2, fields, points, width), jnp.float32),
                 pltpu.VMEM((rows, count, 2, fields) + plane, jnp.float32),
             ],
             in_specs=[vmem()] * (4 + len(taken)),

time: 75.4 us -> 75.4 us (level)
  no operation moved by 1% of the time
where the time goes in v5:
time: 75.4 us; the launch traced here: 75.2 us
  starting transfers between devices  34.7 us (46%)
  Pallas kernels  30.7 us (41%)
  waiting for transfers between devices  6.21 us (8%)
  local copies, waits for them, and re-layouts  2.79 us (4%)
    ppermute x14, starting transfers between devices, swap(): return lax.ppermute(array, axis, [(i, i ^ distance) for i in range(count)])  18.2 us
    ppermute x2, starting transfers between devices, local(): across = lax.ppermute(mine, 'wall', inward)  6.09 us
    pallas_call x1, Pallas kernels, local(): call(functools.partial(summary_kernel, rows), [mark] + [summary] * 2, mic...  6.05 us
    pallas_call x3, Pallas kernels, reorder(): call(functools.partial(reorder_kernel, rows), moved_shape, micros=2.0, in...  5.99 us
    ppermute x2, starting transfers between devices, local(): extra = (lax.ppermute(outgoing, 'wall', outward),)  5.75 us
    pallas_call x2, Pallas kernels, local(): call(functools.partial(local_kernel, count, spans, rows), [f32(rows, coun...  5.47 us
    pallas_call x2, Pallas kernels, local(): call(functools.partial(answer_kernel, count, chosen[0] if final else None...  5.38 us
    ppermute x14, waiting for transfers between devices, swap(): return lax.ppermute(array, axis, [(i, i ^ distance) for i in range(count)])  3.92 us
  transfers between devices with their start and end apart: 22, of which 5 were waited for; matrix products, arithmetic and copies ran while one was open for 0% of the time, Pallas kernels for 34%

profile of v5, /device:TPU:1, one launch (start us, length us, event | category | flops | bytes accessed | tf_op | source)
XLA Modules:
  0.0 75.2 jit_solution(13838019031305484930)
XLA Ops:
  0.0 1.3 %copy-done.3 = bf16[2,5,4,32,4,128]{5,4,3,2,1,0:T(4,128)(2,1)S(1)} copy-done((bf16[2,5,4,32,4,128]{5,4,3,2,1,0:T(4,128)(2,1)S(1)}, bf16[2,5,4,32,4,128]{5,4,3,2,1,0:T(4,128)(2,1)}, u32[]{:S(2)}) %copy-start.3) | copy-done | bytes 1310744
  1.3 1.0 %repack_kernel.1 = (f32[8,128]{1,0:T(8,128)S(1)}, bf16[41,32,128]{2,1,0:T(8,128)(2,1)S(1)}, bf16[41,32,128]{2,1,0:T(8,128)(2,1)S(1)}, bf16[41,32,128]{2,1,0:T(8,128)(2,1)S(1)}, bf16[41,32,128]{2,1,0:T(8,128)(2,1)S(1)}) custom-call(bf16[2,5,4,128,128]{4,3,2,1,0:T(8,128)(2,1)S(1)} %bitcast.10), custom_call_target="tpu_custom_call" | custom-call | bytes 7200000 | tf_op jit(solution)/shard_map/repack_kernel/pallas_call | solution.py:699
  2.3 3.1 %collective-permute-start = (bf16[41,32,128]{2,1,0:T(8,128)(2,1)S(1)}, bf16[41,32,128]{2,1,0:T(8,128)(2,1)S(1)}, u32[]{:S(2)}, u32[]{:S(2)}) collective-permute-start(bf16[41,32,128]{2,1,0:T(8,128)(2,1)S(1)} %get-tuple-element.53), channel_id=1, source_target_pairs={{0,24},{8,16},{16,8},{24,0},{1,25},{9,17},{17,9},{25,1},{2,26},{10... | collective-permute-start | bytes 1007624 | tf_op jit(solution)/shard_map/forcing3/ppermute | solution.py:691
  5.7 1.4 %copy-done = bf16[2,5,5,32,4,128]{5,4,3,2,1,0:T(4,128)(2,1)S(1)} copy-done((bf16[2,5,5,32,4,128]{5,4,3,2,1,0:T(4,128)(2,1)S(1)}, bf16[2,5,5,32,4,128]{5,4,3,2,1,0:T(4,128)(2,1)}, u32[]{:S(2)}) %copy-start) | copy-done | bytes 1638424
  7.2 2.0 %reorder_kernel.4.upper_ref = bf16[4,2,5,5,32,128]{5,4,3,2,1,0:T(8,128)(2,1)S(1)} custom-call(bf16[2,5,5,128,128]{4,3,2,1,0:T(8,128)(2,1)S(1)} %bitcast.7, f32[8,128]{1,0:T(8,128)S(1)} %get-tuple-element.50.after_ref), custom_call_target="tpu_custom_call" | custom-call | bytes 7200000 | tf_op jit(solution)/shard_map/reorder_kernel/pallas_call | solution.py:713
  9.2 2.0 %reorder_kernel.3.lower_ref = bf16[4,2,5,5,32,128]{5,4,3,2,1,0:T(8,128)(2,1)S(1)} custom-call(bf16[2,5,5,128,128]{4,3,2,1,0:T(8,128)(2,1)S(1)} %bitcast.8, f32[8,128]{1,0:T(8,128)S(1)} %get-tuple-element.50.after_ref), custom_call_target="tpu_custom_call" | custom-call | bytes 7200000 | tf_op jit(solution)/shard_map/reorder_kernel/pallas_call | solution.py:713
  11.2 6.0 %summary_kernel.1 = (f32[8,128]{1,0:T(8,128)S(1)}, f32[3,2,5,5,16,128]{5,4,3,2,1,0:T(8,128)S(1)}, f32[3,2,5,5,16,128]{5,4,3,2,1,0:T(8,128)S(1)}) custom-call(bf16[4,2,5,5,32,128]{5,4,3,2,1,0:T(8,128)(2,1)S(1)} %reorder_kernel.3.lower_ref, bf16[4,2,5,5,32,128]{5,4,3,2,1,0:T(8,128)(2,1)S(1)} %reorder_kernel.4.upper_ref), custom_call_target="tpu_custom_call" | custom-call | bytes 21600000 | tf_op jit(solution)/shard_map/summary_kernel/pallas_call | solution.py:721
  17.2 2.1 %table_kernel.1.kernel_ref = bf16[5,512,256]{2,1,0:T(8,128)(2,1)S(1)} custom-call(f32[2,5,128]{2,1,0:T(8,128)S(1)} %copy.6.factor_ref, f32[8,128]{1,0:T(8,128)S(1)} %get-tuple-element.51.after_ref), custom_call_target="tpu_custom_call" | custom-call | bytes 7200000 | tf_op jit(solution)/shard_map/table_kernel/pallas_call | solution.py:728
  19.4 1.5 %collective-permute-done.1.refs_2_ = bf16[41,32,128]{2,1,0:T(8,128)(2,1)S(1)} collective-permute-done((bf16[41,32,128]{2,1,0:T(8,128)(2,1)S(1)}, bf16[41,32,128]{2,1,0:T(8,128)(2,1)S(1)}, u32[]{:S(2)}, u32[]{:S(2)}) %collective-permute-start.1) | collective-permute-done | bytes 335904 | tf_op jit(solution)/shard_map/forcing2/ppermute | solution.py:691
  20.9 0.9 %filter_kernel.1 = (f32[8,128]{1,0:T(8,128)S(1)}, f32[2,2,5,32,128]{4,3,2,1,0:T(8,128)S(1)}, f32[2,2,5,32,128]{4,3,2,1,0:T(8,128)S(1)}, f32[2,2,5,32,128]{4,3,2,...) custom-call(bf16[5,512,256]{2,1,0:T(8,128)(2,1)S(1)} %table_kernel.1, ...), custom_call_target="tpu_custom_call" | custom-call | bytes 3600000 | tf_op jit(solution)/shard_map/filter_kernel/pallas_call | solution.py:734
  22.7 1.6 %collective-permute-start.16 = (f16[2,2,5,32,128]{4,3,2,1,0:T(8,128)(2,1)S(1)}, f16[2,2,5,32,128]{4,3,2,1,0:T(8,128)(2,1)S(1)}, u32[]{:S(2)}, u32[]{:S(2)}) collective-permute-start(f16[2,2,5,32,128]{4,3,2,1,0:T(8,128)(2,1)S(1)} %convert_element_type.46), channel_id=1, source_target_pairs={{0,24},{8,16},{16,8},{24,0},{1,25},{9,17},{17,9},{25,1},{2,26},{10... | collective-permute-start | bytes 491528 | tf_op jit(solution)/shard_map/chunk0_driving3/ppermute | solution.py:691
  24.4 1.0 %collective-permute-start.15 = (f16[2,2,5,32,128]{4,3,2,1,0:T(8,128)(2,1)S(1)}, f16[2,2,5,32,128]{4,3,2,1,0:T(8,128)(2,1)S(1)}, u32[]{:S(2)}, u32[]{:S(2)}) collective-permute-start(f16[2,2,5,32,128]{4,3,2,1,0:T(8,128)(2,1)S(1)} %convert_element_type.44), channel_id=1, source_target_pairs={{0,16},{8,24},{16,0},{24,8},{1,17},{9,25},{17,1},{25,9},{2,18},{10... | collective-permute-start | bytes 491528 | tf_op jit(solution)/shard_map/chunk0_driving2/ppermute | solution.py:691
  25.6 2.0 %pair_matrices_kernel.1 = (f32[8,128]{1,0:T(8,128)}, f32[2,3,2,5,5,16,128]{6,5,4,3,2,1,0:T(8,128)S(1)}, f32[3,2,5,5,16,128]{5,4,3,2,1,0:T(8,128)S(1)}, f32[2,5,5,16,128]{4,3,2,1,0:T(8,128)S(1)}) custom-call(f32[8,128]{1,0:T(8,128)S(1)} %get-tuple-element.56.after_ref.scale_ref, f32[3,2,5,5,16,128]{5,4,3,2,1,0:T(8,128)S(1)} %get-tuple-element.59.keep_ref, ...), custom_call_target="tpu_custom_call" | custom-call | bytes 5040000 | tf_op jit(solution)/shard_map/pair_matrices_kernel/pallas_call | solution.py:744
  27.6 1.2 %collective-permute-start.4 = (f16[2,2,5,32,128]{4,3,2,1,0:T(8,128)(2,1)S(1)}, f16[2,2,5,32,128]{4,3,2,1,0:T(8,128)(2,1)S(1)}, u32[]{:S(2)}, u32[]{:S(2)}) collective-permute-start(f16[2,2,5,32,128]{4,3,2,1,0:T(8,128)(2,1)S(1)} %convert_element_type.36), channel_id=1, source_target_pairs={{0,8},{8,0},{16,24},{24,16},{1,9},{9,1},{17,25},{25,17},{2,10},{10... | collective-permute-start | bytes 491528 | tf_op jit(solution)/shard_map/chunk1_driving1/ppermute | solution.py:691
  29.5 1.5 %collective-permute-start.6 = (f16[2,2,5,32,128]{4,3,2,1,0:T(8,128)(2,1)S(1)}, f16[2,2,5,32,128]{4,3,2,1,0:T(8,128)(2,1)S(1)}, u32[]{:S(2)}, u32[]{:S(2)}) collective-permute-start(f16[2,2,5,32,128]{4,3,2,1,0:T(8,128)(2,1)S(1)} %convert_element_type.40), channel_id=1, source_target_pairs={{0,24},{8,16},{16,8},{24,0},{1,25},{9,17},{17,9},{25,1},{2,26},{10... | collective-permute-start | bytes 491528 | tf_op jit(solution)/shard_map/chunk1_driving3/ppermute | solution.py:691
  31.0 2.3 %collective-permute-done.15 = f16[2,2,5,32,128]{4,3,2,1,0:T(8,128)(2,1)S(1)} collective-permute-done((f16[2,2,5,32,128]{4,3,2,1,0:T(8,128)(2,1)S(1)}, f16[2,2,5,32,128]{4,3,2,1,0:T(8,128)(2,1)S(1)}, u32[]{:S(2)}, u32[]{:S(2)}) %collective-permute-start.15) | collective-permute-done | bytes 163872 | tf_op jit(solution)/shard_map/chunk0_driving2/ppermute | solution.py:691
  33.3 1.3 %collective-permute-start.8 = (f32[2,5,5,16,128]{4,3,2,1,0:T(8,128)S(1)}, f32[2,5,5,16,128]{4,3,2,1,0:T(8,128)S(1)}, u32[]{:S(2)}, u32[]{:S(2)}) collective-permute-start(f32[2,5,5,16,128]{4,3,2,1,0:T(8,128)S(1)} %slice_bitcast_fusion), channel_id=1, source_target_pairs={{0,2},{1,3},{2,0},{3,1},{4,6},{5,7},{6,4},{7,5},{8,10},{9,11},{10,... | collective-permute-start | bytes 1228808 | tf_op jit(solution)/shard_map/matrices_outward/ppermute | solution.py:774
  34.6 2.0 %reorder_kernel.5.pivot_ref = bf16[4,2,5,5,32,128]{5,4,3,2,1,0:T(8,128)(2,1)S(1)} custom-call(bf16[2,5,5,128,128]{4,3,2,1,0:T(8,128)(2,1)S(1)} %bitcast.9, f32[8,128]{1,0:T(8,128)S(1)} %get-tuple-element.56.after_ref.scale_ref), custom_call_target="tpu_custom_call" | custom-call | bytes 7200000 | tf_op jit(solution)/shard_map/reorder_kernel/pallas_call | solution.py:713
  36.7 2.7 %local_kernel.3 = (f32[4,2,2,5,32,128]{5,4,3,2,1,0:T(8,128)S(1)}, f32[2,2,2,5,16,128]{5,4,3,2,1,0:T(8,128)S(1)}, f32[2,2,2,5,16,128]{5,4,3,2,1,0:T(8,128)S(1)}) custom-call(bf16[4,2,5,5,32,128]{5,4,3,2,1,0:T(8,128)(2,1)S(1)} %reorder_kernel.5.pivot_ref, bf16[4,2,5,5,32,128]{5,4,3,2,1,0:T(8,128)(2,1)S(1)} %reorder_kernel.3.lower_ref, ...), custom_call_target="tpu_custom_call" | custom-call | bytes 10080000 | tf_op jit(solution)/shard_map/local_kernel/pallas_call | solution.py:783
  39.5 0.9 %collective-permute-start.17 = (f32[2,2,2,5,16,128]{5,4,3,2,1,0:T(8,128)S(1)}, f32[2,2,2,5,16,128]{5,4,3,2,1,0:T(8,128)S(1)}, u32[]{:S(2)}, u32[]{:S(2)}) collective-permute-start(f32[2,2,2,5,16,128]{5,4,3,2,1,0:T(8,128)S(1)} %get-tuple-element.87), channel_id=1, source_target_pairs={{0,1},{1,0},{2,3},{3,2},{4,5},{5,4},{6,7},{7,6},{8,9},{9,8},{10,11... | collective-permute-start | bytes 983048 | tf_op jit(solution)/shard_map/chunk0_core/ppermute | solution.py:691
  40.5 2.7 %local_kernel.2 = (f32[4,2,2,5,32,128]{5,4,3,2,1,0:T(8,128)S(1)}, f32[2,2,2,5,16,128]{5,4,3,2,1,0:T(8,128)S(1)}, f32[2,2,2,5,16,128]{5,4,3,2,1,0:T(8,128)S(1)}) custom-call(bf16[4,2,5,5,32,128]{5,4,3,2,1,0:T(8,128)(2,1)S(1)} %reorder_kernel.5.pivot_ref, bf16[4,2,5,5,32,128]{5,4,3,2,1,0:T(8,128)(2,1)S(1)} %reorder_kernel.3.lower_ref, ...), custom_call_target="tpu_custom_call" | custom-call | bytes 10080000 | tf_op jit(solution)/shard_map/local_kernel/pallas_call | solution.py:783
  43.8 1.4 %collective-permute-start.9 = (f32[2,5,5,16,128]{4,3,2,1,0:T(8,128)S(1)}, f32[2,5,5,16,128]{4,3,2,1,0:T(8,128)S(1)}, u32[]{:S(2)}, u32[]{:S(2)}) collective-permute-start(f32[2,5,5,16,128]{4,3,2,1,0:T(8,128)S(1)} %upper_half_kernel.1), channel_id=1, source_target_pairs={{0,1},{1,0},{2,4},{4,2},{3,5},{5,3},{6,7},{7,6},{8,9},{9,8},{10,12... | collective-permute-start | bytes 1228808 | tf_op jit(solution)/shard_map/matrices_inward/ppermute | solution.py:810
  45.7 1.8 %collective-permute-start.18 = (f32[2,2,5,16,128]{4,3,2,1,0:T(8,128)S(1)}, f32[2,2,5,16,128]{4,3,2,1,0:T(8,128)S(1)}, u32[]{:S(2)}, u32[]{:S(2)}) collective-permute-start(f32[2,2,5,16,128]{4,3,2,1,0:T(8,128)S(1)} %get-tuple-element.90), channel_id=1, source_target_pairs={{0,2},{1,3},{2,0},{3,1},{4,6},{5,7},{6,4},{7,5},{8,10},{9,11},{10,... | collective-permute-start | bytes 491528 | tf_op jit(solution)/shard_map/chunk0_to_middle/ppermute | solution.py:819
  48.2 2.1 %collective-permute-done.18.came_ref.first_ref = f32[2,2,5,16,128]{4,3,2,1,0:T(8,128)S(1)} collective-permute-done((f32[2,2,5,16,128]{4,3,2,1,0:T(8,128)S(1)}, f32[2,2,5,16,128]{4,3,2,1,0:T(8,128)S(1)}, u32[]{:S(2)}, u32[]{:S(2)}) %collective-permute-start.18) | collective-permute-done | bytes 163872 | tf_op jit(solution)/shard_map/chunk0_to_middle/ppermute | solution.py:819
  50.3 4.2 %collective-permute-start.19 = (f32[2,2,5,16,128]{4,3,2,1,0:T(8,128)S(1)}, f32[2,2,5,16,128]{4,3,2,1,0:T(8,128)S(1)}, u32[]{:S(2)}, u32[]{:S(2)}) collective-permute-start(f32[2,2,5,16,128]{4,3,2,1,0:T(8,128)S(1)} %halves_kernel.3.mine_ref), channel_id=1, source_target_pairs={{0,1},{1,0},{2,4},{4,2},{3,5},{5,3},{6,7},{7,6},{8,9},{9,8},{10,12... | collective-permute-start | bytes 491528 | tf_op jit(solution)/shard_map/chunk0_middle/ppermute | solution.py:827
  54.5 1.9 %collective-permute-start.11 = (f32[2,2,5,16,128]{4,3,2,1,0:T(8,128)S(1)}, f32[2,2,5,16,128]{4,3,2,1,0:T(8,128)S(1)}, u32[]{:S(2)}, u32[]{:S(2)}) collective-permute-start(f32[2,2,5,16,128]{4,3,2,1,0:T(8,128)S(1)} %halves_kernel.2.mine_ref), channel_id=1, source_target_pairs={{0,1},{1,0},{2,4},{4,2},{3,5},{5,3},{6,7},{7,6},{8,9},{9,8},{10,12... | collective-permute-start | bytes 491528 | tf_op jit(solution)/shard_map/chunk1_middle/ppermute | solution.py:827
  56.5 2.7 %collective-permute-start.20 = (f32[2,2,5,16,128]{4,3,2,1,0:T(8,128)S(1)}, f32[2,2,5,16,128]{4,3,2,1,0:T(8,128)S(1)}, u32[]{:S(2)}, u32[]{:S(2)}) collective-permute-start(f32[2,2,5,16,128]{4,3,2,1,0:T(8,128)S(1)} %get-tuple-element.92), channel_id=1, source_target_pairs={{0,2},{1,3},{2,0},{3,1},{4,6},{5,7},{6,4},{7,5},{8,10},{9,11},{10,... | collective-permute-start | bytes 491528 | tf_op jit(solution)/shard_map/chunk0_to_ends/ppermute | solution.py:835
  59.2 3.0 %collective-permute-start.12 = (f32[2,2,5,16,128]{4,3,2,1,0:T(8,128)S(1)}, f32[2,2,5,16,128]{4,3,2,1,0:T(8,128)S(1)}, u32[]{:S(2)}, u32[]{:S(2)}) collective-permute-start(f32[2,2,5,16,128]{4,3,2,1,0:T(8,128)S(1)} %get-tuple-element.78), channel_id=1, source_target_pairs={{0,2},{1,3},{2,0},{3,1},{4,6},{5,7},{6,4},{7,5},{8,10},{9,11},{10,... | collective-permute-start | bytes 491528 | tf_op jit(solution)/shard_map/chunk1_to_ends/ppermute | solution.py:835
  62.7 5.2 %collective-permute-start.21 = (f32[2,2,2,5,16,128]{5,4,3,2,1,0:T(8,128)S(1)}, f32[2,2,2,5,16,128]{5,4,3,2,1,0:T(8,128)S(1)}, u32[]{:S(2)}, u32[]{:S(2)}) collective-permute-start(f32[2,2,2,5,16,128]{5,4,3,2,1,0:T(8,128)S(1)} %get-tuple-element.94), channel_id=1, source_target_pairs={{0,1},{1,0},{2,3},{3,2},{4,5},{5,4},{6,7},{7,6},{8,9},{9,8},{10,11... | collective-permute-start | bytes 983048 | tf_op jit(solution)/shard_map/chunk0_apart/ppermute | solution.py:691
  68.3 1.3 %collective-permute-start.13 = (f32[2,2,2,5,16,128]{5,4,3,2,1,0:T(8,128)S(1)}, f32[2,2,2,5,16,128]{5,4,3,2,1,0:T(8,128)S(1)}, u32[]{:S(2)}, u32[]{:S(2)}) collective-permute-start(f32[2,2,2,5,16,128]{5,4,3,2,1,0:T(8,128)S(1)} %get-tuple-element.80), channel_id=1, source_target_pairs={{0,1},{1,0},{2,3},{3,2},{4,5},{5,4},{6,7},{7,6},{8,9},{9,8},{10,11... | collective-permute-start | bytes 983048 | tf_op jit(solution)/shard_map/chunk1_apart/ppermute | solution.py:691
  69.7 2.1 %answer_kernel.2.refs_0_ = f32[2,2,5,2,64,128]{5,4,3,2,1,0:T(8,128)S(1)} custom-call(bf16[4,2,5,5,32,128]{5,4,3,2,1,0:T(8,128)(2,1)S(1)} %reorder_kernel.3.lower_ref, bf16[4,2,5,5,32,128]{5,4,3,2,1,0:T(8,128)(2,1)S(1)} %reorder_kernel.4.upper_ref, f32[4,2,2,5,32,128]{5,4,3,2,1,0:T(8,128)S(1)} %get-tuple-element.85.source_ref, ...), custom_call_target="tpu_custom_call" | custom-call | bytes 10800000 | tf_op jit(solution)/shard_map/answer_kernel/pallas_call | solution.py:867
  71.8 3.3 %answer_kernel.3 = f32[2,5,4,128,128]{4,3,2,1,0:T(8,128)} custom-call(bf16[4,2,5,5,32,128]{5,4,3,2,1,0:T(8,128)(2,1)S(1)} %reorder_kernel.3.lower_ref, bf16[4,2,5,5,32,128]{5,4,3,2,1,0:T(8,128)(2,1)S(1)} %reorder_kernel.4.upper_ref, f32[4,2,2,5,32,128]{5,4,3,2,1,0:T(8,128)S(1)} %get-tuple-element.68.source_ref, ...), custom_call_target="tpu_custom_call" | custom-call | bytes 10800000 | tf_op jit(solution)/shard_map/answer_kernel/pallas_call | solution.py:867
  (57 shorter events, 5.1 us)
Async XLA Ops:
  0.0 1.3 %copy-start.3 = (bf16[2,5,4,32,4,128]{5,4,3,2,1,0:T(4,128)(2,1)S(1)}, bf16[2,5,4,32,4,128]{5,4,3,2,1,0:T(4,128)(2,1)}, u32[]{:S(2)}) copy-start(bf16[2,5,4,32,4,128]{5,4,3,2,1,0:T(4,128)(2,1)} %param.5) | copy-start | bytes 3932164
  1.3 4.4 %copy-start.4 = (f32[2,5,128]{2,0,1:T(2,128)S(1)}, f32[2,5,128]{2,0,1:T(2,128)}, u32[]{:S(2)}) copy-start(f32[2,5,128]{2,0,1:T(2,128)} %param.6) | copy-start | bytes 15364
  2.3 17.1 %collective-permute-start = (bf16[41,32,128]{2,1,0:T(8,128)(2,1)S(1)}, bf16[41,32,128]{2,1,0:T(8,128)(2,1)S(1)}, u32[]{:S(2)}, u32[]{:S(2)}) collective-permute-start(bf16[41,32,128]{2,1,0:T(8,128)(2,1)S(1)} %get-tuple-element.53), channel_id=1, source_target_pairs={{0,24},{8,16},{16,8},{24,0},{1,25},{9,17},{17,9},{25,1},{2,26},{10... | collective-permute-start | bytes 1007624 | tf_op jit(solution)/shard_map/forcing3/ppermute | solution.py:691
  5.4 15.5 %collective-permute-start.1 = (bf16[41,32,128]{2,1,0:T(8,128)(2,1)S(1)}, bf16[41,32,128]{2,1,0:T(8,128)(2,1)S(1)}, u32[]{:S(2)}, u32[]{:S(2)}) collective-permute-start(bf16[41,32,128]{2,1,0:T(8,128)(2,1)S(1)} %get-tuple-element.54), channel_id=1, source_target_pairs={{0,16},{8,24},{16,0},{24,8},{1,17},{9,25},{17,1},{25,9},{2,18},{10... | collective-permute-start | bytes 1007624 | tf_op jit(solution)/shard_map/forcing2/ppermute | solution.py:691
  5.6 15.3 %collective-permute-start.2 = (bf16[41,32,128]{2,1,0:T(8,128)(2,1)S(1)}, bf16[41,32,128]{2,1,0:T(8,128)(2,1)S(1)}, u32[]{:S(2)}, u32[]{:S(2)}) collective-permute-start(bf16[41,32,128]{2,1,0:T(8,128)(2,1)S(1)} %get-tuple-element.55), channel_id=1, source_target_pairs={{0,8},{8,0},{16,24},{24,16},{1,9},{9,1},{17,25},{25,17},{2,10},{10... | collective-permute-start | bytes 1007624 | tf_op jit(solution)/shard_map/forcing1/ppermute | solution.py:691
  5.7 1.4 %copy-start = (bf16[2,5,5,32,4,128]{5,4,3,2,1,0:T(4,128)(2,1)S(1)}, bf16[2,5,5,32,4,128]{5,4,3,2,1,0:T(4,128)(2,1)}, u32[]{:S(2)}) copy-start(bf16[2,5,5,32,4,128]{5,4,3,2,1,0:T(4,128)(2,1)} %param.9) | copy-start | bytes 4915204
  7.2 2.0 %copy-start.1 = (bf16[2,5,5,32,4,128]{5,4,3,2,1,0:T(4,128)(2,1)S(1)}, bf16[2,5,5,32,4,128]{5,4,3,2,1,0:T(4,128)(2,1)}, u32[]{:S(2)}) copy-start(bf16[2,5,5,32,4,128]{5,4,3,2,1,0:T(4,128)(2,1)} %param.8) | copy-start | bytes 4915204
  21.8 3.8 %collective-permute-start.3 = (f32[3,2,5,5,16,128]{5,4,3,2,1,0:T(8,128)S(1)}, f32[3,2,5,5,16,128]{5,4,3,2,1,0:T(8,128)S(1)}, u32[]{:S(2)}, u32[]{:S(2)}) collective-permute-start(f32[3,2,5,5,16,128]{5,4,3,2,1,0:T(8,128)S(1)} %get-tuple-element.61), channel_id=1, source_target_pairs={{0,1},{1,0},{2,3},{3,2},{4,5},{5,4},{6,7},{7,6},{8,9},{9,8},{10,11... | collective-permute-start | bytes 3686408 | tf_op jit(solution)/shard_map/matrices_core/ppermute | solution.py:691
  22.7 6.8 %collective-permute-start.16 = (f16[2,2,5,32,128]{4,3,2,1,0:T(8,128)(2,1)S(1)}, f16[2,2,5,32,128]{4,3,2,1,0:T(8,128)(2,1)S(1)}, u32[]{:S(2)}, u32[]{:S(2)}) collective-permute-start(f16[2,2,5,32,128]{4,3,2,1,0:T(8,128)(2,1)S(1)} %convert_element_type.46), channel_id=1, source_target_pairs={{0,24},{8,16},{16,8},{24,0},{1,25},{9,17},{17,9},{25,1},{2,26},{10... | collective-permute-start | bytes 491528 | tf_op jit(solution)/shard_map/chunk0_driving3/ppermute | solution.py:691
  24.4 8.9 %collective-permute-start.15 = (f16[2,2,5,32,128]{4,3,2,1,0:T(8,128)(2,1)S(1)}, f16[2,2,5,32,128]{4,3,2,1,0:T(8,128)(2,1)S(1)}, u32[]{:S(2)}, u32[]{:S(2)}) collective-permute-start(f16[2,2,5,32,128]{4,3,2,1,0:T(8,128)(2,1)S(1)} %convert_element_type.44), channel_id=1, source_target_pairs={{0,16},{8,24},{16,0},{24,8},{1,17},{9,25},{17,1},{25,9},{2,18},{10... | collective-permute-start | bytes 491528 | tf_op jit(solution)/shard_map/chunk0_driving2/ppermute | solution.py:691
  25.4 11.3 %collective-permute-start.14 = (f16[2,2,5,32,128]{4,3,2,1,0:T(8,128)(2,1)S(1)}, f16[2,2,5,32,128]{4,3,2,1,0:T(8,128)(2,1)S(1)}, u32[]{:S(2)}, u32[]{:S(2)}) collective-permute-start(f16[2,2,5,32,128]{4,3,2,1,0:T(8,128)(2,1)S(1)} %convert_element_type.42), channel_id=1, source_target_pairs={{0,8},{8,0},{16,24},{24,16},{1,9},{9,1},{17,25},{25,17},{2,10},{10... | collective-permute-start | bytes 491528 | tf_op jit(solution)/shard_map/chunk0_driving1/ppermute | solution.py:691
  25.6 9.0 %copy-start.2 = (bf16[2,5,5,32,4,128]{5,4,3,2,1,0:T(4,128)(2,1)S(1)}, bf16[2,5,5,32,4,128]{5,4,3,2,1,0:T(4,128)(2,1)}, u32[]{:S(2)}) copy-start(bf16[2,5,5,32,4,128]{5,4,3,2,1,0:T(4,128)(2,1)} %param.7) | copy-start | bytes 4915204
  27.6 12.7 %collective-permute-start.4 = (f16[2,2,5,32,128]{4,3,2,1,0:T(8,128)(2,1)S(1)}, f16[2,2,5,32,128]{4,3,2,1,0:T(8,128)(2,1)S(1)}, u32[]{:S(2)}, u32[]{:S(2)}) collective-permute-start(f16[2,2,5,32,128]{4,3,2,1,0:T(8,128)(2,1)S(1)} %convert_element_type.36), channel_id=1, source_target_pairs={{0,8},{8,0},{16,24},{24,16},{1,9},{9,1},{17,25},{25,17},{2,10},{10... | collective-permute-start | bytes 491528 | tf_op jit(solution)/shard_map/chunk1_driving1/ppermute | solution.py:691
  28.8 11.6 %collective-permute-start.5 = (f16[2,2,5,32,128]{4,3,2,1,0:T(8,128)(2,1)S(1)}, f16[2,2,5,32,128]{4,3,2,1,0:T(8,128)(2,1)S(1)}, u32[]{:S(2)}, u32[]{:S(2)}) collective-permute-start(f16[2,2,5,32,128]{4,3,2,1,0:T(8,128)(2,1)S(1)} %convert_element_type.38), channel_id=1, source_target_pairs={{0,16},{8,24},{16,0},{24,8},{1,17},{9,25},{17,1},{25,9},{2,18},{10... | collective-permute-start | bytes 491528 | tf_op jit(solution)/shard_map/chunk1_driving2/ppermute | solution.py:691
  29.5 10.9 %collective-permute-start.6 = (f16[2,2,5,32,128]{4,3,2,1,0:T(8,128)(2,1)S(1)}, f16[2,2,5,32,128]{4,3,2,1,0:T(8,128)(2,1)S(1)}, u32[]{:S(2)}, u32[]{:S(2)}) collective-permute-start(f16[2,2,5,32,128]{4,3,2,1,0:T(8,128)(2,1)S(1)} %convert_element_type.40), channel_id=1, source_target_pairs={{0,24},{8,16},{16,8},{24,0},{1,25},{9,17},{17,9},{25,1},{2,26},{10... | collective-permute-start | bytes 491528 | tf_op jit(solution)/shard_map/chunk1_driving3/ppermute | solution.py:691
  33.3 10.5 %collective-permute-start.8 = (f32[2,5,5,16,128]{4,3,2,1,0:T(8,128)S(1)}, f32[2,5,5,16,128]{4,3,2,1,0:T(8,128)S(1)}, u32[]{:S(2)}, u32[]{:S(2)}) collective-permute-start(f32[2,5,5,16,128]{4,3,2,1,0:T(8,128)S(1)} %slice_bitcast_fusion), channel_id=1, source_target_pairs={{0,2},{1,3},{2,0},{3,1},{4,6},{5,7},{6,4},{7,5},{8,10},{9,11},{10,... | collective-permute-start | bytes 1228808 | tf_op jit(solution)/shard_map/matrices_outward/ppermute | solution.py:774
  39.5 5.8 %collective-permute-start.17 = (f32[2,2,2,5,16,128]{5,4,3,2,1,0:T(8,128)S(1)}, f32[2,2,2,5,16,128]{5,4,3,2,1,0:T(8,128)S(1)}, u32[]{:S(2)}, u32[]{:S(2)}) collective-permute-start(f32[2,2,2,5,16,128]{5,4,3,2,1,0:T(8,128)S(1)} %get-tuple-element.87), channel_id=1, source_target_pairs={{0,1},{1,0},{2,3},{3,2},{4,5},{5,4},{6,7},{7,6},{8,9},{9,8},{10,11... | collective-permute-start | bytes 983048 | tf_op jit(solution)/shard_map/chunk0_core/ppermute | solution.py:691
  43.2 4.4 %collective-permute-start.7 = (f32[2,2,2,5,16,128]{5,4,3,2,1,0:T(8,128)S(1)}, f32[2,2,2,5,16,128]{5,4,3,2,1,0:T(8,128)S(1)}, u32[]{:S(2)}, u32[]{:S(2)}) collective-permute-start(f32[2,2,2,5,16,128]{5,4,3,2,1,0:T(8,128)S(1)} %get-tuple-element.72), channel_id=1, source_target_pairs={{0,1},{1,0},{2,3},{3,2},{4,5},{5,4},{6,7},{7,6},{8,9},{9,8},{10,11... | collective-permute-start | bytes 983048 | tf_op jit(solution)/shard_map/chunk1_core/ppermute | solution.py:691
  43.8 12.6 %collective-permute-start.9 = (f32[2,5,5,16,128]{4,3,2,1,0:T(8,128)S(1)}, f32[2,5,5,16,128]{4,3,2,1,0:T(8,128)S(1)}, u32[]{:S(2)}, u32[]{:S(2)}) collective-permute-start(f32[2,5,5,16,128]{4,3,2,1,0:T(8,128)S(1)} %upper_half_kernel.1), channel_id=1, source_target_pairs={{0,1},{1,0},{2,4},{4,2},{3,5},{5,3},{6,7},{7,6},{8,9},{9,8},{10,12... | collective-permute-start | bytes 1228808 | tf_op jit(solution)/shard_map/matrices_inward/ppermute | solution.py:810
  45.7 4.6 %collective-permute-start.18 = (f32[2,2,5,16,128]{4,3,2,1,0:T(8,128)S(1)}, f32[2,2,5,16,128]{4,3,2,1,0:T(8,128)S(1)}, u32[]{:S(2)}, u32[]{:S(2)}) collective-permute-start(f32[2,2,5,16,128]{4,3,2,1,0:T(8,128)S(1)} %get-tuple-element.90), channel_id=1, source_target_pairs={{0,2},{1,3},{2,0},{3,1},{4,6},{5,7},{6,4},{7,5},{8,10},{9,11},{10,... | collective-permute-start | bytes 491528 | tf_op jit(solution)/shard_map/chunk0_to_middle/ppermute | solution.py:819
  48.1 6.4 %collective-permute-start.10 = (f32[2,2,5,16,128]{4,3,2,1,0:T(8,128)S(1)}, f32[2,2,5,16,128]{4,3,2,1,0:T(8,128)S(1)}, u32[]{:S(2)}, u32[]{:S(2)}) collective-permute-start(f32[2,2,5,16,128]{4,3,2,1,0:T(8,128)S(1)} %get-tuple-element.76), channel_id=1, source_target_pairs={{0,2},{1,3},{2,0},{3,1},{4,6},{5,7},{6,4},{7,5},{8,10},{9,11},{10,... | collective-permute-start | bytes 491528 | tf_op jit(solution)/shard_map/chunk1_to_middle/ppermute | solution.py:819
  50.3 6.1 %collective-permute-start.19 = (f32[2,2,5,16,128]{4,3,2,1,0:T(8,128)S(1)}, f32[2,2,5,16,128]{4,3,2,1,0:T(8,128)S(1)}, u32[]{:S(2)}, u32[]{:S(2)}) collective-permute-start(f32[2,2,5,16,128]{4,3,2,1,0:T(8,128)S(1)} %halves_kernel.3.mine_ref), channel_id=1, source_target_pairs={{0,1},{1,0},{2,4},{4,2},{3,5},{5,3},{6,7},{7,6},{8,9},{9,8},{10,12... | collective-permute-start | bytes 491528 | tf_op jit(solution)/shard_map/chunk0_middle/ppermute | solution.py:827
  54.5 4.7 %collective-permute-start.11 = (f32[2,2,5,16,128]{4,3,2,1,0:T(8,128)S(1)}, f32[2,2,5,16,128]{4,3,2,1,0:T(8,128)S(1)}, u32[]{:S(2)}, u32[]{:S(2)}) collective-permute-start(f32[2,2,5,16,128]{4,3,2,1,0:T(8,128)S(1)} %halves_kernel.2.mine_ref), channel_id=1, source_target_pairs={{0,1},{1,0},{2,4},{4,2},{3,5},{5,3},{6,7},{7,6},{8,9},{9,8},{10,12... | collective-permute-start | bytes 491528 | tf_op jit(solution)/shard_map/chunk1_middle/ppermute | solution.py:827
  56.5 5.8 %collective-permute-start.20 = (f32[2,2,5,16,128]{4,3,2,1,0:T(8,128)S(1)}, f32[2,2,5,16,128]{4,3,2,1,0:T(8,128)S(1)}, u32[]{:S(2)}, u32[]{:S(2)}) collective-permute-start(f32[2,2,5,16,128]{4,3,2,1,0:T(8,128)S(1)} %get-tuple-element.92), channel_id=1, source_target_pairs={{0,2},{1,3},{2,0},{3,1},{4,6},{5,7},{6,4},{7,5},{8,10},{9,11},{10,... | collective-permute-start | bytes 491528 | tf_op jit(solution)/shard_map/chunk0_to_ends/ppermute | solution.py:835
  59.2 8.7 %collective-permute-start.12 = (f32[2,2,5,16,128]{4,3,2,1,0:T(8,128)S(1)}, f32[2,2,5,16,128]{4,3,2,1,0:T(8,128)S(1)}, u32[]{:S(2)}, u32[]{:S(2)}) collective-permute-start(f32[2,2,5,16,128]{4,3,2,1,0:T(8,128)S(1)} %get-tuple-element.78), channel_id=1, source_target_pairs={{0,2},{1,3},{2,0},{3,1},{4,6},{5,7},{6,4},{7,5},{8,10},{9,11},{10,... | collective-permute-start | bytes 491528 | tf_op jit(solution)/shard_map/chunk1_to_ends/ppermute | solution.py:835
  62.7 7.0 %collective-permute-start.21 = (f32[2,2,2,5,16,128]{5,4,3,2,1,0:T(8,128)S(1)}, f32[2,2,2,5,16,128]{5,4,3,2,1,0:T(8,128)S(1)}, u32[]{:S(2)}, u32[]{:S(2)}) collective-permute-start(f32[2,2,2,5,16,128]{5,4,3,2,1,0:T(8,128)S(1)} %get-tuple-element.94), channel_id=1, source_target_pairs={{0,1},{1,0},{2,3},{3,2},{4,5},{5,4},{6,7},{7,6},{8,9},{9,8},{10,11... | collective-permute-start | bytes 983048 | tf_op jit(solution)/shard_map/chunk0_apart/ppermute | solution.py:691
  68.3 3.4 %collective-permute-start.13 = (f32[2,2,2,5,16,128]{5,4,3,2,1,0:T(8,128)S(1)}, f32[2,2,2,5,16,128]{5,4,3,2,1,0:T(8,128)S(1)}, u32[]{:S(2)}, u32[]{:S(2)}) collective-permute-start(f32[2,2,2,5,16,128]{5,4,3,2,1,0:T(8,128)S(1)} %get-tuple-element.80), channel_id=1, source_target_pairs={{0,1},{1,0},{2,3},{3,2},{4,5},{5,4},{6,7},{7,6},{8,9},{9,8},{10,11... | collective-permute-start | bytes 983048 | tf_op jit(solution)/shard_map/chunk1_apart/ppermute | solution.py:691
